TPU v7x, 512 devices: a whole 4x8x8 slice. The times are simulated.
512 devices in a mesh: pitch: 64 (over x, y, z_hi), radial: 8 (over z_lo, core).
Axes of the slice: x: 4, y: 8, z: 8 (z_hi: 2, z_lo: 4; z = z_hi * 4 + z_lo), core: 2. Of those that a mesh axis runs over, the one named last changes fastest.
Arguments:
- vel: float32 [3, 512, 64, 256], P(None, 'pitch', 'radial'), may hold values from -6 to 6
- rhs_mom: float32 [3, 512, 64, 256], P(None, 'pitch', 'radial'), may hold values from -6 to 6
- mode_inv: float32 [512, 64, 8], P(None, 'radial'), may hold values from -0.4 to 2
- sweep_inv: float32 [3, 3, 512, 64, 256], P(None, None, 'pitch', 'radial'), may hold values from -0.07 to 0.25
Outputs:
- velocity: float32 [3, 512, 64, 256], P(None, 'pitch', 'radial')
- pressure: float32 [512, 64, 256], P('pitch', 'radial')
All inputs are finite; a program needn't handle non-finite values.
Results may differ from a plain program's by a relative error of at most 0.00007.
Values sent between devices are 32-bit elements; how exact they have to be, the bound alone decides.
No kernel may reach another device: no remote copies, remote signals or barrier semaphores. Data moves between devices by JAX's collectives and lax.ppermute only.
A program may use at most 64 MiB of HBM per device.

v0:
```python
import jax
import jax.numpy as jnp
from jax import lax
from jax.sharding import PartitionSpec as P

SWEEPS = 4


coupling = 0.5


def extended(block, sides, width, periodic):
    for axis, dim in sides:
        count = lax.axis_size(axis)
        forward = [(i, i + 1) for i in range(count - 1)]
        if periodic:
            forward.append((count - 1, 0))
        backward = [(target, source) for source, target in forward]
        low = lax.ppermute(
            lax.slice_in_dim(block, block.shape[dim] - width, None, axis=dim), axis, forward
        )
        high = lax.ppermute(lax.slice_in_dim(block, 0, width, axis=dim), axis, backward)
        block = jnp.concatenate([low, block, high], axis=dim)
    return block


def cas_table(count):
    index = jnp.arange(count, dtype=jnp.int32)
    product = index[:, None] * index[None, :] % count
    angle = 2.0 * jnp.pi / count * product.astype(jnp.float32)
    return jnp.cos(angle) + jnp.sin(angle)


def rim_diff(padded, axis):
    length = padded.shape[axis]
    upper = lax.slice_in_dim(padded, 2, length, axis=axis)
    lower = lax.slice_in_dim(padded, 0, length - 2, axis=axis)
    return (upper - lower) * 0.5


def rim_sum(padded, axis):
    length = padded.shape[axis]
    upper = lax.slice_in_dim(padded, 2, length, axis=axis)
    lower = lax.slice_in_dim(padded, 0, length - 2, axis=axis)
    return upper + lower


def axial_pad(field, axis):
    return jnp.pad(field, [(1, 1) if a == axis else (0, 0) for a in range(field.ndim)])


def on_device(vel, rhs_mom, mode_inv, sweep_inv):
    highest = lax.Precision.HIGHEST
    pitch_part = extended(vel[0], (("pitch", 0),), 1, True)
    radial_part = extended(vel[1], (("radial", 1),), 1, False)
    div = rim_diff(pitch_part, 0) + rim_diff(radial_part, 1) + rim_diff(axial_pad(vel[2], 2), 2)
    pencil = lax.all_to_all(div, "pitch", split_axis=2, concat_axis=0, tiled=True)
    lines = pencil.shape[0]
    table = cas_table(lines)
    dhat = jnp.dot(table, pencil.reshape(lines, -1), precision=highest).reshape(pencil.shape)
    modes = jnp.einsum("krs,ksz->krz", mode_inv, dhat, precision=highest)
    press_lines = (
        jnp.dot(table, modes.reshape(lines, -1), precision=highest).reshape(pencil.shape) / lines
    )
    pressure = lax.all_to_all(press_lines, "pitch", split_axis=0, concat_axis=2, tiled=True)
    grad_pitch = rim_diff(extended(pressure, (("pitch", 0),), 1, True), 0)
    grad_radial = rim_diff(extended(pressure, (("radial", 1),), 1, False), 1)
    grad_axial = rim_diff(axial_pad(pressure, 2), 2)
    force = rhs_mom - jnp.stack([grad_pitch, grad_radial, grad_axial])
    state = vel
    for sweep in range(SWEEPS):
        pitch_rim = extended(state, (("pitch", 1),), 1, True)
        radial_rim = extended(state, (("radial", 2),), 1, False)
        beside_all = (
            rim_sum(pitch_rim, 1) + rim_sum(radial_rim, 2) + rim_sum(axial_pad(state, 3), 3)
        )
        res = force - ((1.0 + 6.0 * coupling) * state - coupling * beside_all)
        state = (
            state + sweep_inv[:, 0] * res[0] + sweep_inv[:, 1] * res[1] + sweep_inv[:, 2] * res[2]
        )
    return (state, pressure)


def solution(mesh):
    return jax.shard_map(
        on_device,
        mesh=mesh,
        in_specs=(
            P(None, "pitch", "radial", None),
            P(None, "pitch", "radial", None),
            P(None, "radial", None),
            P(None, None, "pitch", "radial", None),
        ),
        out_specs=(P(None, "pitch", "radial", None), P("pitch", "radial", None)),
        check_vma=False,
    )
```

profile of v0, /device:TPU:1, one launch (start us, length us, event | category | flops | bytes accessed | tf_op | source)
XLA Modules:
  0.0 216.6 jit_solution(17591254839685965373)
XLA Ops:
  0.6 1.0 fusion.85
  1.6 8.8 %collective-permute-start.2 = (f32[8,1,256]{2,0,1:T(8,128)S(1)}, f32[8,1,256]{2,0,1:T(8,128)S(1)}, u32[]{:S(2)}, u32[]{:S(2)}) collective-permute-start(f32[8,1,256]{2,0,1:T(8,128)S(1)} %get-tuple-element.58), channel_id=1, source_target_pairs={{1,0},{2,1},{3,2},{4,3},{5,4},{6,5},{7,6},{9,8},{10,9},{11,10},{12... | collective-permute-start | bytes 24584 | tf_op jit(solution)/shard_map/ppermute | solution.py:22
  10.4 1.9 collective-permute-start.3
  12.4 0.7 slice_bitcast_fusion.15
  13.1 11.4 %collective-permute-start = (f32[1,8,256]{2,1,0:T(8,128)S(1)}, f32[1,8,256]{2,1,0:T(8,128)S(1)}, u32[]{:S(2)}, u32[]{:S(2)}) collective-permute-start(f32[1,8,256]{2,1,0:T(8,128)S(1)} %get-tuple-element.47), channel_id=1, source_target_pairs={{8,0},{16,8},{24,16},{32,24},{40,32},{48,40},{56,48},{64,56},{72,6... | collective-permute-start | bytes 24584 | tf_op jit(solution)/shard_map/ppermute | solution.py:22
  24.5 1.9 collective-permute-start.1
  26.5 10.6 %collective-permute-done.1 = f32[1,8,256]{2,1,0:T(8,128)S(1)} collective-permute-done((f32[1,8,256]{2,1,0:T(8,128)S(1)}, f32[1,8,256]{2,1,0:T(8,128)S(1)}, u32[]{:S(2)}, u32[]{:S(2)}) %collective-permute-start.1) | collective-permute-done | bytes 8224 | tf_op jit(solution)/shard_map/ppermute | solution.py:19
  37.2 0.4 copy.286
  37.6 1.2 reshape.22
  38.8 4.6 %all-to-all-start = ((f32[64,1,256]{2,1,0:T(1,128)}), f32[64,1,256]{2,1,0:T(1,128)S(1)}, u32[]{:S(2)}, u32[]{:S(2)}) async-start(f32[64,1,256]{2,1,0:T(1,128)} %reshape.22), calls=%async_computation | async-start | bytes 131072 | tf_op jit(solution)/shard_map/all_to_all | solution.py:57
  43.4 0.7 copy.290
  44.2 12.4 %all-to-all-done = f32[64,1,256]{2,1,0:T(1,128)S(1)} async-done(((f32[64,1,256]{2,1,0:T(1,128)}), f32[64,1,256]{2,1,0:T(1,128)S(1)}, u32[]{:S(2)}, u32[]{:S(2)}) %all-to-all-start) | async-done | bytes 65568 | tf_op jit(solution)/shard_map/all_to_all | solution.py:57
  56.6 0.5 broadcast.51
  57.1 0.8 reduce
  57.9 0.6 reshape.23
  58.5 1.6 copy.287
  60.1 1.7 reshape.19
  61.9 5.3 %fusion.4 = f32[512,8,4]{0,1,2:T(8,128)S(1)} fusion(f32[8,4,512]{2,1,0:T(4,128)S(1)} %dot_general.20), kind=kOutput, calls=%fused_computation.9 | convolution fusion | flops 104595456 | bytes 131072 | tf_op jit(solution)/shard_map/dot_general | solution.py:60
  67.6 4.5 %convolution_bitcast_fusion = f32[512,8,4]{1,2,0:T(4,128)} fusion(f32[512,8,4]{1,2,0:T(4,128)S(1)} %copy.289, f32[512,8,8]{2,1,0:T(8,128)S(1)} %copy.290), kind=kOutput, calls=%fused_computation.3 | convolution fusion | flops 1572864 | bytes 262144 | tf_op jit(solution)/shard_map/krs,ksz->krz/dot_general | solution.py:61
  72.2 1.5 copy.291
  73.8 5.6 %convolution_multiply_fusion = f32[512,8,4]{0,1,2:T(8,128)S(1)} fusion(f32[8,4,512]{2,1,0:T(4,128)S(1)} %dot_general.25), kind=kOutput, calls=%fused_computation.4 | convolution fusion | flops 104611840 | bytes 131072 | tf_op jit(solution)/shard_map/dot_general | solution.py:63
  79.7 1.8 reshape.24
  81.5 4.6 %all-to-all-start.1 = ((f32[64,1,256]{2,1,0:T(1,128)}), f32[64,1,256]{2,1,0:T(1,128)S(1)}, u32[]{:S(2)}, u32[]{:S(2)}) async-start(f32[64,1,256]{2,1,0:T(1,128)} %reshape.24), calls=%async_computation.1 | async-start | bytes 131072 | tf_op jit(solution)/shard_map/all_to_all | solution.py:65
  86.2 0.6 copy.334
  86.8 3.9 %collective-permute-start.10 = (f32[3,8,1,256]{3,1,2,0:T(8,128)}, f32[3,8,1,256]{3,1,2,0:T(8,128)}, u32[]{:S(2)}, u32[]{:S(2)}) collective-permute-start(f32[3,8,1,256]{3,1,2,0:T(8,128)} %copy.334), channel_id=1, source_target_pairs={{1,0},{2,1},{3,2},{4,3},{5,4},{6,5},{7,6},{9,8},{10,9},{11,10},{12... | collective-permute-start | bytes 73736 | tf_op jit(solution)/shard_map/ppermute | solution.py:22
  90.7 0.6 copy.335
  91.3 2.9 %collective-permute-start.11 = (f32[3,8,1,256]{3,1,2,0:T(8,128)}, f32[3,8,1,256]{3,1,2,0:T(8,128)}, u32[]{:S(2)}, u32[]{:S(2)}) collective-permute-start(f32[3,8,1,256]{3,1,2,0:T(8,128)} %copy.335), channel_id=1, source_target_pairs={{0,1},{1,2},{2,3},{3,4},{4,5},{5,6},{6,7},{8,9},{9,10},{10,11},{11... | collective-permute-start | bytes 73736 | tf_op jit(solution)/shard_map/ppermute | solution.py:19
  94.3 5.0 %all-to-all-done.1 = f32[64,1,256]{2,1,0:T(1,128)S(1)} async-done(((f32[64,1,256]{2,1,0:T(1,128)}), f32[64,1,256]{2,1,0:T(1,128)S(1)}, u32[]{:S(2)}, u32[]{:S(2)}) %all-to-all-start.1) | async-done | bytes 65568 | tf_op jit(solution)/shard_map/all_to_all | solution.py:65
  99.3 0.8 reduce.1
  100.1 1.2 reshape.25
  101.4 0.8 copy.328
  102.3 1.3 fusion.78
  103.6 1.5 copy.302
  105.1 5.1 %collective-permute-start.6 = (f32[8,1,256]{2,0,1:T(8,128)S(1)}, f32[8,1,256]{2,0,1:T(8,128)}, u32[]{:S(2)}, u32[]{:S(2)}) collective-permute-start(f32[8,1,256]{2,0,1:T(8,128)S(1)} %copy.302), channel_id=1, source_target_pairs={{1,0},{2,1},{3,2},{4,3},{5,4},{6,5},{7,6},{9,8},{10,9},{11,10},{12... | collective-permute-start | bytes 24584 | tf_op jit(solution)/shard_map/ppermute | solution.py:22
  110.6 3.0 %collective-permute-start.7 = (f32[8,1,256]{2,0,1:T(8,128)S(1)}, f32[8,1,256]{2,0,1:T(8,128)}, u32[]{:S(2)}, u32[]{:S(2)}) collective-permute-start(f32[8,1,256]{2,0,1:T(8,128)S(1)} %copy.305), channel_id=1, source_target_pairs={{0,1},{1,2},{2,3},{3,4},{4,5},{5,6},{6,7},{8,9},{9,10},{10,11},{11... | collective-permute-start | bytes 24584 | tf_op jit(solution)/shard_map/ppermute | solution.py:19
  113.6 1.4 fusion.77
  114.9 2.9 %copy.296 = f32[1,8,64,4]{1,3,2,0:T(4,128)S(1)} copy(f32[1,8,64,4]{0,2,1,3:T(8,128)} %get-tuple-element.16) | data formatting | bytes 16384 | tf_op jit(solution)/shard_map/slice | solution.py:22
  117.8 4.1 %collective-permute-start.4 = (f32[1,8,256]{1,2,0:T(8,128)S(1)}, f32[1,8,256]{1,2,0:T(8,128)}, u32[]{:S(2)}, u32[]{:S(2)}) collective-permute-start(f32[1,8,256]{1,2,0:T(8,128)S(1)} %bitcast.145), channel_id=1, source_target_pairs={{8,0},{16,8},{24,16},{32,24},{40,32},{48,40},{56,48},{64,56},{72,6... | collective-permute-start | bytes 24584 | tf_op jit(solution)/shard_map/ppermute | solution.py:22
  121.9 1.6 copy.299
  123.6 5.0 %collective-permute-start.5 = (f32[1,8,256]{1,2,0:T(8,128)S(1)}, f32[1,8,256]{1,2,0:T(8,128)S(1)}, u32[]{:S(2)}, u32[]{:S(2)}) collective-permute-start(f32[1,8,256]{1,2,0:T(8,128)S(1)} %bitcast.146), channel_id=1, source_target_pairs={{0,8},{8,16},{16,24},{24,32},{32,40},{40,48},{48,56},{56,64},{64,7... | collective-permute-start | bytes 24584 | tf_op jit(solution)/shard_map/ppermute | solution.py:19
  128.6 0.8 copy.310
  129.4 8.4 %collective-permute-start.8 = (f32[3,1,8,256]{3,2,1,0:T(8,128)S(1)}, f32[3,1,8,256]{3,2,1,0:T(8,128)S(1)}, u32[]{:S(2)}, u32[]{:S(2)}) collective-permute-start(f32[3,1,8,256]{3,2,1,0:T(8,128)S(1)} %get-tuple-element.49), channel_id=1, source_target_pairs={{8,0},{16,8},{24,16},{32,24},{40,32},{48,40},{56,48},{64,56},{72,6... | collective-permute-start | bytes 73736 | tf_op jit(solution)/shard_map/ppermute | solution.py:22
  137.8 0.8 copy.312
  138.9 1.9 collective-permute-start.9
  140.8 0.7 copy.304
  141.5 0.7 copy.306
  142.3 1.0 copy.298
  143.4 8.4 %collective-permute-done.9 = f32[3,1,8,256]{3,2,1,0:T(8,128)S(1)} collective-permute-done((f32[3,1,8,256]{3,2,1,0:T(8,128)S(1)}, f32[3,1,8,256]{3,2,1,0:T(8,128)S(1)}, u32[]{:S(2)}, u32[]{:S(2)}) %collective-permute-start.9) | collective-permute-done | bytes 24608 | tf_op jit(solution)/shard_map/ppermute | solution.py:19
  152.2 3.1 %collective-permute-start.14 = (f32[3,8,1,256]{3,1,2,0:T(8,128)S(1)}, f32[3,8,1,256]{3,1,2,0:T(8,128)S(1)}, u32[]{:S(2)}, u32[]{:S(2)}) collective-permute-start(f32[3,8,1,256]{3,1,2,0:T(8,128)S(1)} %copy.315), channel_id=1, source_target_pairs={{1,0},{2,1},{3,2},{4,3},{5,4},{6,5},{7,6},{9,8},{10,9},{11,10},{12... | collective-permute-start | bytes 73736 | tf_op jit(solution)/shard_map/ppermute | solution.py:22
  155.3 2.8 %collective-permute-start.15 = (f32[3,8,1,256]{3,1,2,0:T(8,128)S(1)}, f32[3,8,1,256]{3,1,2,0:T(8,128)S(1)}, u32[]{:S(2)}, u32[]{:S(2)}) collective-permute-start(f32[3,8,1,256]{3,1,2,0:T(8,128)S(1)} %copy.317), channel_id=1, source_target_pairs={{0,1},{1,2},{2,3},{3,4},{4,5},{5,6},{6,7},{8,9},{9,10},{10,11},{11... | collective-permute-start | bytes 73736 | tf_op jit(solution)/shard_map/ppermute | solution.py:19
  158.1 2.7 %collective-permute-start.12 = (f32[3,1,8,256]{3,2,1,0:T(8,128)S(1)}, f32[3,1,8,256]{3,2,1,0:T(8,128)S(1)}, u32[]{:S(2)}, u32[]{:S(2)}) collective-permute-start(f32[3,1,8,256]{3,2,1,0:T(8,128)S(1)} %get-tuple-element.37), channel_id=1, source_target_pairs={{8,0},{16,8},{24,16},{32,24},{40,32},{48,40},{56,48},{64,56},{72,6... | collective-permute-start | bytes 73736 | tf_op jit(solution)/shard_map/ppermute | solution.py:22
  160.9 6.4 %collective-permute-start.13 = (f32[3,1,8,256]{3,2,1,0:T(8,128)S(1)}, f32[3,1,8,256]{3,2,1,0:T(8,128)S(1)}, u32[]{:S(2)}, u32[]{:S(2)}) collective-permute-start(f32[3,1,8,256]{3,2,1,0:T(8,128)S(1)} %get-tuple-element.38), channel_id=1, source_target_pairs={{0,8},{8,16},{16,24},{24,32},{32,40},{40,48},{48,56},{56,64},{64,7... | collective-permute-start | bytes 73736 | tf_op jit(solution)/shard_map/ppermute | solution.py:19
  167.4 6.7 %collective-permute-done.13 = f32[3,1,8,256]{3,2,1,0:T(8,128)S(1)} collective-permute-done((f32[3,1,8,256]{3,2,1,0:T(8,128)S(1)}, f32[3,1,8,256]{3,2,1,0:T(8,128)S(1)}, u32[]{:S(2)}, u32[]{:S(2)}) %collective-permute-start.13) | collective-permute-done | bytes 24608 | tf_op jit(solution)/shard_map/ppermute | solution.py:19
  174.5 2.6 %collective-permute-start.18 = (f32[3,8,1,256]{3,1,2,0:T(8,128)S(1)}, f32[3,8,1,256]{3,1,2,0:T(8,128)S(1)}, u32[]{:S(2)}, u32[]{:S(2)}) collective-permute-start(f32[3,8,1,256]{3,1,2,0:T(8,128)S(1)} %copy.319), channel_id=1, source_target_pairs={{1,0},{2,1},{3,2},{4,3},{5,4},{6,5},{7,6},{9,8},{10,9},{11,10},{12... | collective-permute-start | bytes 73736 | tf_op jit(solution)/shard_map/ppermute | solution.py:22
  177.1 3.0 %collective-permute-start.19 = (f32[3,8,1,256]{3,1,2,0:T(8,128)S(1)}, f32[3,8,1,256]{3,1,2,0:T(8,128)S(1)}, u32[]{:S(2)}, u32[]{:S(2)}) collective-permute-start(f32[3,8,1,256]{3,1,2,0:T(8,128)S(1)} %copy.321), channel_id=1, source_target_pairs={{0,1},{1,2},{2,3},{3,4},{4,5},{5,6},{6,7},{8,9},{9,10},{10,11},{11... | collective-permute-start | bytes 73736 | tf_op jit(solution)/shard_map/ppermute | solution.py:19
  180.1 1.9 collective-permute-start.16
  182.0 7.3 %collective-permute-start.17 = (f32[3,1,8,256]{3,2,1,0:T(8,128)S(1)}, f32[3,1,8,256]{3,2,1,0:T(8,128)S(1)}, u32[]{:S(2)}, u32[]{:S(2)}) collective-permute-start(f32[3,1,8,256]{3,2,1,0:T(8,128)S(1)} %get-tuple-element.31), channel_id=1, source_target_pairs={{0,8},{8,16},{16,24},{24,32},{32,40},{40,48},{48,56},{56,64},{64,7... | collective-permute-start | bytes 73736 | tf_op jit(solution)/shard_map/ppermute | solution.py:19
  189.4 5.6 %collective-permute-done.17 = f32[3,1,8,256]{3,2,1,0:T(8,128)S(1)} collective-permute-done((f32[3,1,8,256]{3,2,1,0:T(8,128)S(1)}, f32[3,1,8,256]{3,2,1,0:T(8,128)S(1)}, u32[]{:S(2)}, u32[]{:S(2)}) %collective-permute-start.17) | collective-permute-done | bytes 24608 | tf_op jit(solution)/shard_map/ppermute | solution.py:19
  195.4 2.4 %collective-permute-start.22 = (f32[3,8,1,256]{3,1,2,0:T(8,128)S(1)}, f32[3,8,1,256]{3,1,2,0:T(8,128)S(1)}, u32[]{:S(2)}, u32[]{:S(2)}) collective-permute-start(f32[3,8,1,256]{3,1,2,0:T(8,128)S(1)} %copy.323), channel_id=1, source_target_pairs={{1,0},{2,1},{3,2},{4,3},{5,4},{6,5},{7,6},{9,8},{10,9},{11,10},{12... | collective-permute-start | bytes 73736 | tf_op jit(solution)/shard_map/ppermute | solution.py:22
  197.8 3.2 %collective-permute-start.23 = (f32[3,8,1,256]{3,1,2,0:T(8,128)S(1)}, f32[3,8,1,256]{3,1,2,0:T(8,128)S(1)}, u32[]{:S(2)}, u32[]{:S(2)}) collective-permute-start(f32[3,8,1,256]{3,1,2,0:T(8,128)S(1)} %copy.325), channel_id=1, source_target_pairs={{0,1},{1,2},{2,3},{3,4},{4,5},{5,6},{6,7},{8,9},{9,10},{10,11},{11... | collective-permute-start | bytes 73736 | tf_op jit(solution)/shard_map/ppermute | solution.py:19
  201.0 1.9 collective-permute-start.20
  202.9 7.3 %collective-permute-start.21 = (f32[3,1,8,256]{3,2,1,0:T(8,128)S(1)}, f32[3,1,8,256]{3,2,1,0:T(8,128)S(1)}, u32[]{:S(2)}, u32[]{:S(2)}) collective-permute-start(f32[3,1,8,256]{3,2,1,0:T(8,128)S(1)} %get-tuple-element.24), channel_id=1, source_target_pairs={{0,8},{8,16},{16,24},{24,32},{32,40},{40,48},{48,56},{56,64},{64,7... | collective-permute-start | bytes 73736 | tf_op jit(solution)/shard_map/ppermute | solution.py:19
  210.3 5.3 %collective-permute-done.21 = f32[3,1,8,256]{3,2,1,0:T(8,128)S(1)} collective-permute-done((f32[3,1,8,256]{3,2,1,0:T(8,128)S(1)}, f32[3,1,8,256]{3,2,1,0:T(8,128)S(1)}, u32[]{:S(2)}, u32[]{:S(2)}) %collective-permute-start.21) | collective-permute-done | bytes 24608 | tf_op jit(solution)/shard_map/ppermute | solution.py:19
  215.8 0.7 fusion.44
  (74 shorter events, 3.4 us)
Async XLA Ops:
  0.6 42.8 %copy-start.4 = (f32[512,8,8]{0,2,1:T(8,128)S(1)}, f32[512,8,8]{0,2,1:T(8,128)}, u32[]{:S(2)}) copy-start(f32[512,8,8]{0,2,1:T(8,128)} %param.6) | copy-start | bytes 393220
  1.6 24.8 %collective-permute-start.2 = (f32[8,1,256]{2,0,1:T(8,128)S(1)}, f32[8,1,256]{2,0,1:T(8,128)S(1)}, u32[]{:S(2)}, u32[]{:S(2)}) collective-permute-start(f32[8,1,256]{2,0,1:T(8,128)S(1)} %get-tuple-element.58), channel_id=1, source_target_pairs={{1,0},{2,1},{3,2},{4,3},{5,4},{6,5},{7,6},{9,8},{10,9},{11,10},{12... | collective-permute-start | bytes 24584 | tf_op jit(solution)/shard_map/ppermute | solution.py:22
  10.4 16.0 %collective-permute-start.3 = (f32[8,1,256]{2,0,1:T(8,128)S(1)}, f32[8,1,256]{2,0,1:T(8,128)S(1)}, u32[]{:S(2)}, u32[]{:S(2)}) collective-permute-start(f32[8,1,256]{2,0,1:T(8,128)S(1)} %get-tuple-element.59), channel_id=1, source_target_pairs={{0,1},{1,2},{2,3},{3,4},{4,5},{5,6},{6,7},{8,9},{9,10},{10,11},{11... | collective-permute-start | bytes 24584 | tf_op jit(solution)/shard_map/ppermute | solution.py:19
  13.1 13.4 %collective-permute-start = (f32[1,8,256]{2,1,0:T(8,128)S(1)}, f32[1,8,256]{2,1,0:T(8,128)S(1)}, u32[]{:S(2)}, u32[]{:S(2)}) collective-permute-start(f32[1,8,256]{2,1,0:T(8,128)S(1)} %get-tuple-element.47), channel_id=1, source_target_pairs={{8,0},{16,8},{24,16},{32,24},{40,32},{48,40},{56,48},{64,56},{72,6... | collective-permute-start | bytes 24584 | tf_op jit(solution)/shard_map/ppermute | solution.py:22
  24.5 12.6 %collective-permute-start.1 = (f32[1,8,256]{2,1,0:T(8,128)S(1)}, f32[1,8,256]{2,1,0:T(8,128)S(1)}, u32[]{:S(2)}, u32[]{:S(2)}) collective-permute-start(f32[1,8,256]{2,1,0:T(8,128)S(1)} %get-tuple-element.48), channel_id=1, source_target_pairs={{0,8},{8,16},{16,24},{24,32},{32,40},{40,48},{48,56},{56,64},{64,7... | collective-permute-start | bytes 24584 | tf_op jit(solution)/shard_map/ppermute | solution.py:19
  38.8 17.8 %all-to-all-start = ((f32[64,1,256]{2,1,0:T(1,128)}), f32[64,1,256]{2,1,0:T(1,128)S(1)}, u32[]{:S(2)}, u32[]{:S(2)}) async-start(f32[64,1,256]{2,1,0:T(1,128)} %reshape.22), calls=%async_computation | async-start | bytes 131072 | tf_op jit(solution)/shard_map/all_to_all | solution.py:57
  79.3 6.8 %copy-start.1 = (f32[3,8,8,256]{3,2,1,0:T(8,128)S(1)}, f32[3,8,8,256]{3,2,1,0:T(8,128)}, u32[]{:S(2)}) copy-start(f32[3,8,8,256]{3,2,1,0:T(8,128)} %param.4) | copy-start | bytes 589828
  81.5 17.8 %all-to-all-start.1 = ((f32[64,1,256]{2,1,0:T(1,128)}), f32[64,1,256]{2,1,0:T(1,128)S(1)}, u32[]{:S(2)}, u32[]{:S(2)}) async-start(f32[64,1,256]{2,1,0:T(1,128)} %reshape.24), calls=%async_computation.1 | async-start | bytes 131072 | tf_op jit(solution)/shard_map/all_to_all | solution.py:65
  86.8 36.8 %collective-permute-start.10 = (f32[3,8,1,256]{3,1,2,0:T(8,128)}, f32[3,8,1,256]{3,1,2,0:T(8,128)}, u32[]{:S(2)}, u32[]{:S(2)}) collective-permute-start(f32[3,8,1,256]{3,1,2,0:T(8,128)} %copy.334), channel_id=1, source_target_pairs={{1,0},{2,1},{3,2},{4,3},{5,4},{6,5},{7,6},{9,8},{10,9},{11,10},{12... | collective-permute-start | bytes 73736 | tf_op jit(solution)/shard_map/ppermute | solution.py:22
  91.3 38.1 %collective-permute-start.11 = (f32[3,8,1,256]{3,1,2,0:T(8,128)}, f32[3,8,1,256]{3,1,2,0:T(8,128)}, u32[]{:S(2)}, u32[]{:S(2)}) collective-permute-start(f32[3,8,1,256]{3,1,2,0:T(8,128)} %copy.335), channel_id=1, source_target_pairs={{0,1},{1,2},{2,3},{3,4},{4,5},{5,6},{6,7},{8,9},{9,10},{10,11},{11... | collective-permute-start | bytes 73736 | tf_op jit(solution)/shard_map/ppermute | solution.py:19
  105.1 33.8 %collective-permute-start.6 = (f32[8,1,256]{2,0,1:T(8,128)S(1)}, f32[8,1,256]{2,0,1:T(8,128)}, u32[]{:S(2)}, u32[]{:S(2)}) collective-permute-start(f32[8,1,256]{2,0,1:T(8,128)S(1)} %copy.302), channel_id=1, source_target_pairs={{1,0},{2,1},{3,2},{4,3},{5,4},{6,5},{7,6},{9,8},{10,9},{11,10},{12... | collective-permute-start | bytes 24584 | tf_op jit(solution)/shard_map/ppermute | solution.py:22
  110.6 30.9 %collective-permute-start.7 = (f32[8,1,256]{2,0,1:T(8,128)S(1)}, f32[8,1,256]{2,0,1:T(8,128)}, u32[]{:S(2)}, u32[]{:S(2)}) collective-permute-start(f32[8,1,256]{2,0,1:T(8,128)S(1)} %copy.305), channel_id=1, source_target_pairs={{0,1},{1,2},{2,3},{3,4},{4,5},{5,6},{6,7},{8,9},{9,10},{10,11},{11... | collective-permute-start | bytes 24584 | tf_op jit(solution)/shard_map/ppermute | solution.py:19
  114.9 36.9 %copy-start.3 = (f32[3,8,8,256]{3,2,1,0:T(8,128)S(1)}, f32[3,8,8,256]{3,2,1,0:T(8,128)}, u32[]{:S(2)}) copy-start(f32[3,8,8,256]{3,2,1,0:T(8,128)} %param.5) | copy-start | bytes 589828
  117.8 24.5 %collective-permute-start.4 = (f32[1,8,256]{1,2,0:T(8,128)S(1)}, f32[1,8,256]{1,2,0:T(8,128)}, u32[]{:S(2)}, u32[]{:S(2)}) collective-permute-start(f32[1,8,256]{1,2,0:T(8,128)S(1)} %bitcast.145), channel_id=1, source_target_pairs={{8,0},{16,8},{24,16},{32,24},{40,32},{48,40},{56,48},{64,56},{72,6... | collective-permute-start | bytes 24584 | tf_op jit(solution)/shard_map/ppermute | solution.py:22
  121.9 30.1 %copy-start = (f32[3,3,8,8,256]{4,3,2,1,0:T(8,128)S(1)}, f32[3,3,8,8,256]{4,3,2,1,0:T(8,128)}, u32[]{:S(2)}) copy-start(f32[3,3,8,8,256]{4,3,2,1,0:T(8,128)} %param.7) | copy-start | bytes 1769476
  123.6 19.7 %collective-permute-start.5 = (f32[1,8,256]{1,2,0:T(8,128)S(1)}, f32[1,8,256]{1,2,0:T(8,128)S(1)}, u32[]{:S(2)}, u32[]{:S(2)}) collective-permute-start(f32[1,8,256]{1,2,0:T(8,128)S(1)} %bitcast.146), channel_id=1, source_target_pairs={{0,8},{8,16},{16,24},{24,32},{32,40},{40,48},{48,56},{56,64},{64,7... | collective-permute-start | bytes 24584 | tf_op jit(solution)/shard_map/ppermute | solution.py:19
  129.4 14.0 %collective-permute-start.8 = (f32[3,1,8,256]{3,2,1,0:T(8,128)S(1)}, f32[3,1,8,256]{3,2,1,0:T(8,128)S(1)}, u32[]{:S(2)}, u32[]{:S(2)}) collective-permute-start(f32[3,1,8,256]{3,2,1,0:T(8,128)S(1)} %get-tuple-element.49), channel_id=1, source_target_pairs={{8,0},{16,8},{24,16},{32,24},{40,32},{48,40},{56,48},{64,56},{72,6... | collective-permute-start | bytes 73736 | tf_op jit(solution)/shard_map/ppermute | solution.py:22
  138.9 35.4 %copy-start.2 = (f32[8,8,256]{2,1,0:T(8,128)}, f32[8,8,256]{2,1,0:T(8,128)S(1)}, u32[]{:S(2)}) copy-start(f32[8,8,256]{2,1,0:T(8,128)S(1)} %copy.297) | copy-start | bytes 196612
  138.9 12.9 %collective-permute-start.9 = (f32[3,1,8,256]{3,2,1,0:T(8,128)S(1)}, f32[3,1,8,256]{3,2,1,0:T(8,128)S(1)}, u32[]{:S(2)}, u32[]{:S(2)}) collective-permute-start(f32[3,1,8,256]{3,2,1,0:T(8,128)S(1)} %get-tuple-element.50), channel_id=1, source_target_pairs={{0,8},{8,16},{16,24},{24,32},{32,40},{40,48},{48,56},{56,64},{64,7... | collective-permute-start | bytes 73736 | tf_op jit(solution)/shard_map/ppermute | solution.py:19
  152.2 15.1 %collective-permute-start.14 = (f32[3,8,1,256]{3,1,2,0:T(8,128)S(1)}, f32[3,8,1,256]{3,1,2,0:T(8,128)S(1)}, u32[]{:S(2)}, u32[]{:S(2)}) collective-permute-start(f32[3,8,1,256]{3,1,2,0:T(8,128)S(1)} %copy.315), channel_id=1, source_target_pairs={{1,0},{2,1},{3,2},{4,3},{5,4},{6,5},{7,6},{9,8},{10,9},{11,10},{12... | collective-permute-start | bytes 73736 | tf_op jit(solution)/shard_map/ppermute | solution.py:22
  155.3 12.1 %collective-permute-start.15 = (f32[3,8,1,256]{3,1,2,0:T(8,128)S(1)}, f32[3,8,1,256]{3,1,2,0:T(8,128)S(1)}, u32[]{:S(2)}, u32[]{:S(2)}) collective-permute-start(f32[3,8,1,256]{3,1,2,0:T(8,128)S(1)} %copy.317), channel_id=1, source_target_pairs={{0,1},{1,2},{2,3},{3,4},{4,5},{5,6},{6,7},{8,9},{9,10},{10,11},{11... | collective-permute-start | bytes 73736 | tf_op jit(solution)/shard_map/ppermute | solution.py:19
  158.1 9.3 %collective-permute-start.12 = (f32[3,1,8,256]{3,2,1,0:T(8,128)S(1)}, f32[3,1,8,256]{3,2,1,0:T(8,128)S(1)}, u32[]{:S(2)}, u32[]{:S(2)}) collective-permute-start(f32[3,1,8,256]{3,2,1,0:T(8,128)S(1)} %get-tuple-element.37), channel_id=1, source_target_pairs={{8,0},{16,8},{24,16},{32,24},{40,32},{48,40},{56,48},{64,56},{72,6... | collective-permute-start | bytes 73736 | tf_op jit(solution)/shard_map/ppermute | solution.py:22
  160.9 13.2 %collective-permute-start.13 = (f32[3,1,8,256]{3,2,1,0:T(8,128)S(1)}, f32[3,1,8,256]{3,2,1,0:T(8,128)S(1)}, u32[]{:S(2)}, u32[]{:S(2)}) collective-permute-start(f32[3,1,8,256]{3,2,1,0:T(8,128)S(1)} %get-tuple-element.38), channel_id=1, source_target_pairs={{0,8},{8,16},{16,24},{24,32},{32,40},{40,48},{48,56},{56,64},{64,7... | collective-permute-start | bytes 73736 | tf_op jit(solution)/shard_map/ppermute | solution.py:19
  174.5 14.8 %collective-permute-start.18 = (f32[3,8,1,256]{3,1,2,0:T(8,128)S(1)}, f32[3,8,1,256]{3,1,2,0:T(8,128)S(1)}, u32[]{:S(2)}, u32[]{:S(2)}) collective-permute-start(f32[3,8,1,256]{3,1,2,0:T(8,128)S(1)} %copy.319), channel_id=1, source_target_pairs={{1,0},{2,1},{3,2},{4,3},{5,4},{6,5},{7,6},{9,8},{10,9},{11,10},{12... | collective-permute-start | bytes 73736 | tf_op jit(solution)/shard_map/ppermute | solution.py:22
  177.1 12.2 %collective-permute-start.19 = (f32[3,8,1,256]{3,1,2,0:T(8,128)S(1)}, f32[3,8,1,256]{3,1,2,0:T(8,128)S(1)}, u32[]{:S(2)}, u32[]{:S(2)}) collective-permute-start(f32[3,8,1,256]{3,1,2,0:T(8,128)S(1)} %copy.321), channel_id=1, source_target_pairs={{0,1},{1,2},{2,3},{3,4},{4,5},{5,6},{6,7},{8,9},{9,10},{10,11},{11... | collective-permute-start | bytes 73736 | tf_op jit(solution)/shard_map/ppermute | solution.py:19
  180.1 9.3 %collective-permute-start.16 = (f32[3,1,8,256]{3,2,1,0:T(8,128)S(1)}, f32[3,1,8,256]{3,2,1,0:T(8,128)S(1)}, u32[]{:S(2)}, u32[]{:S(2)}) collective-permute-start(f32[3,1,8,256]{3,2,1,0:T(8,128)S(1)} %get-tuple-element.30), channel_id=1, source_target_pairs={{8,0},{16,8},{24,16},{32,24},{40,32},{48,40},{56,48},{64,56},{72,6... | collective-permute-start | bytes 73736 | tf_op jit(solution)/shard_map/ppermute | solution.py:22
  182.0 13.0 %collective-permute-start.17 = (f32[3,1,8,256]{3,2,1,0:T(8,128)S(1)}, f32[3,1,8,256]{3,2,1,0:T(8,128)S(1)}, u32[]{:S(2)}, u32[]{:S(2)}) collective-permute-start(f32[3,1,8,256]{3,2,1,0:T(8,128)S(1)} %get-tuple-element.31), channel_id=1, source_target_pairs={{0,8},{8,16},{16,24},{24,32},{32,40},{40,48},{48,56},{56,64},{64,7... | collective-permute-start | bytes 73736 | tf_op jit(solution)/shard_map/ppermute | solution.py:19
  195.4 14.8 %collective-permute-start.22 = (f32[3,8,1,256]{3,1,2,0:T(8,128)S(1)}, f32[3,8,1,256]{3,1,2,0:T(8,128)S(1)}, u32[]{:S(2)}, u32[]{:S(2)}) collective-permute-start(f32[3,8,1,256]{3,1,2,0:T(8,128)S(1)} %copy.323), channel_id=1, source_target_pairs={{1,0},{2,1},{3,2},{4,3},{5,4},{6,5},{7,6},{9,8},{10,9},{11,10},{12... | collective-permute-start | bytes 73736 | tf_op jit(solution)/shard_map/ppermute | solution.py:22
  197.8 12.4 %collective-permute-start.23 = (f32[3,8,1,256]{3,1,2,0:T(8,128)S(1)}, f32[3,8,1,256]{3,1,2,0:T(8,128)S(1)}, u32[]{:S(2)}, u32[]{:S(2)}) collective-permute-start(f32[3,8,1,256]{3,1,2,0:T(8,128)S(1)} %copy.325), channel_id=1, source_target_pairs={{0,1},{1,2},{2,3},{3,4},{4,5},{5,6},{6,7},{8,9},{9,10},{10,11},{11... | collective-permute-start | bytes 73736 | tf_op jit(solution)/shard_map/ppermute | solution.py:19
  201.0 9.3 %collective-permute-start.20 = (f32[3,1,8,256]{3,2,1,0:T(8,128)S(1)}, f32[3,1,8,256]{3,2,1,0:T(8,128)S(1)}, u32[]{:S(2)}, u32[]{:S(2)}) collective-permute-start(f32[3,1,8,256]{3,2,1,0:T(8,128)S(1)} %get-tuple-element.23), channel_id=1, source_target_pairs={{8,0},{16,8},{24,16},{32,24},{40,32},{48,40},{56,48},{64,56},{72,6... | collective-permute-start | bytes 73736 | tf_op jit(solution)/shard_map/ppermute | solution.py:22
  202.9 12.7 %collective-permute-start.21 = (f32[3,1,8,256]{3,2,1,0:T(8,128)S(1)}, f32[3,1,8,256]{3,2,1,0:T(8,128)S(1)}, u32[]{:S(2)}, u32[]{:S(2)}) collective-permute-start(f32[3,1,8,256]{3,2,1,0:T(8,128)S(1)} %get-tuple-element.24), channel_id=1, source_target_pairs={{0,8},{8,16},{16,24},{24,32},{32,40},{40,48},{48,56},{56,64},{64,7... | collective-permute-start | bytes 73736 | tf_op jit(solution)/shard_map/ppermute | solution.py:19
where the time goes:
time: 218 us; the launch traced here: 217 us
  starting transfers between devices  112 us (51%)
  waiting for transfers between devices  54.2 us (25%)
  local copies, waits for them, and re-layouts  29.8 us (14%)
  matrix products  15.4 us (7%)
  other arithmetic  3.46 us (2%)
    ppermute x12, starting transfers between devices, extended(): lax.ppermute(lax.slice_in_dim(block, 0, width, axis=dim), axis, backward)  56.4 us
    ppermute x12, starting transfers between devices, extended(): lax.ppermute(lax.slice_in_dim(block, block.shape[dim] - width, None, axis...  46.6 us
    ppermute x12, waiting for transfers between devices, extended(): lax.ppermute(lax.slice_in_dim(block, block.shape[dim] - width, None, axis...  36.7 us
    all_to_all x1, waiting for transfers between devices, on_device(): lax.all_to_all(div, 'pitch', split_axis=2, concat_axis=0, tiled=True)  12.4 us
    slice x17, local copies, waits for them, and re-layouts, extended(): lax.slice_in_dim(block, 0, width, axis=dim)  7.98 us
    unnamed x18, local copies, waits for them, and re-layouts  6.75 us
    dot_general x1, matrix products, on_device(): jnp.dot(table, modes.reshape(lines, -1), precision=highest)  5.55 us
    dot_general x1, matrix products, on_device(): jnp.dot(table, pencil.reshape(lines, -1), precision=highest)  5.35 us
  transfers between devices with their start and end apart: 26, of which 7 were waited for; matrix products, arithmetic and copies ran while one was open for 9% of the time, Pallas kernels for 0%

commit v1 on v0

v1 whole, which is shorter than its diff:
```python
import jax
import jax.numpy as jnp
import ml_dtypes
import numpy as np
from jax import lax
from jax.experimental import pallas as pl
from jax.experimental.pallas import tpu as pltpu
from jax.sharding import PartitionSpec as P

SWEEPS = 4
coupling = 0.5
NP, CR, NZ = 512, 8, 256
BLOCKS = 64
LINES = NP // BLOCKS
CHUNK = NZ // BLOCKS
F32 = jnp.float32
BF16 = jnp.bfloat16


def cas_tables():
    index = np.arange(NP)
    angle = 2.0 * np.pi / NP * (index[:, None] * index[None, :] % NP)
    table = np.cos(angle) + np.sin(angle)
    order = (np.arange(BLOCKS)[None, :] * LINES + np.arange(LINES)[:, None]).reshape(-1)
    out = []
    for mat in (table[order, :], table[:, order] / NP):
        high = mat.astype(ml_dtypes.bfloat16)
        low = (mat - high.astype(np.float64)).astype(ml_dtypes.bfloat16)
        out += [high, low]
    return out


def params(mib=24):
    return pltpu.CompilerParams(vmem_limit_bytes=mib * 1024 * 1024)


VMEM = pl.BlockSpec(memory_space=pltpu.VMEM)


def shape(*dims):
    return jax.ShapeDtypeStruct(dims, F32)


def axial(x, step):
    lane = lax.broadcasted_iota(jnp.int32, x.shape, x.ndim - 1)
    moved = pltpu.roll(x, (-step) % NZ, x.ndim - 1)
    return jnp.where(lane == (NZ - 1 if step > 0 else 0), 0.0, moved)


def face_kernel(v1, up, down):
    up[...] = v1[0, :, CR - 1, :]
    down[...] = v1[0, :, 0, :]


def div_kernel(vel, low, high, out):
    row = lax.broadcasted_iota(jnp.int32, (CR, NZ), 0)
    parts = []
    for l in range(LINES):
        v1, v2 = vel[1, l], vel[2, l]
        upper = jnp.where(row == CR - 1, high[l : l + 1, :], pltpu.roll(v1, CR - 1, 0))
        lower = jnp.where(row == 0, low[l : l + 1, :], pltpu.roll(v1, 1, 0))
        parts.append(((upper - lower) + (axial(v2, 1) - axial(v2, -1))) * 0.5)
    for l in range(LINES):
        parts.append(vel[0, l])
    out[...] = jnp.concatenate(parts, axis=0).T


def block_shift(x, step):
    lane = lax.broadcasted_iota(jnp.int32, x.shape, 1) % BLOCKS
    edge = BLOCKS - 1 if step > 0 else 0
    near = pltpu.roll(x, (-step) % 128, 1)
    far = pltpu.roll(x, (BLOCKS - step) % 128, 1)
    return jnp.where(lane == edge, far, near)


def split_dot(x, high, low):
    xh = x.astype(BF16)
    xl = (x - xh.astype(F32)).astype(BF16)
    rows = x.shape[0]
    both = jnp.dot(jnp.concatenate([xh, xl], axis=0), high[...], preferred_element_type=F32)
    return both[:rows] + (both[rows:] + jnp.dot(xh, low[...], preferred_element_type=F32))


def modes_kernel(got, mode, h1, l1, h2, l2, out):
    lane = lax.broadcasted_iota(jnp.int32, (CR, 128), 1)
    sub = lax.broadcasted_iota(jnp.int32, (CR, 128), 0)
    left = lane < BLOCKS
    half = CHUNK // 2
    rows = [[None] * 4 for _ in range(CHUNK)]
    for pair in range(half):
        slabs = [got[pl.ds(2 * pair + e, BLOCKS, stride=CHUNK), :] for e in range(2)]
        a = jnp.concatenate(slabs, axis=0).T
        w = [a[l * CR : (l + 1) * CR] for l in range(LINES)]
        v = [a[NP // 8 + l * CR : NP // 8 + (l + 1) * CR] for l in range(LINES)]
        before = [block_shift(v[-1], -1)] + v[:-1]
        after = v[1:] + [block_shift(v[0], 1)]
        d = [w[l] + (after[l] - before[l]) * 0.5 for l in range(LINES)]
        for t in range(4):
            e, o = d[2 * t], d[2 * t + 1]
            rows[2 * pair][t] = jnp.where(left, e, pltpu.roll(o, BLOCKS, 1))
            rows[2 * pair + 1][t] = jnp.where(left, pltpu.roll(e, BLOCKS, 1), o)
    x = jnp.concatenate([jnp.concatenate(r, axis=1) for r in rows], axis=0)
    dhat = split_dot(x, h1, l1)
    q = []
    for z in range(CHUNK):
        total = None
        for s in range(CR):
            term = mode[:, s, :] * dhat[z * CR + s : z * CR + s + 1, :]
            total = term if total is None else total + term
        q.append(total)
    p = split_dot(jnp.concatenate(q, axis=0), h2, l2)
    for pair in range(half):
        e = []
        for t in range(4):
            a = p[2 * pair * CR : (2 * pair + 1) * CR, t * 128 : (t + 1) * 128]
            b = p[(2 * pair + 1) * CR : (2 * pair + 2) * CR, t * 128 : (t + 1) * 128]
            e.append(jnp.where(left, a, pltpu.roll(b, BLOCKS, 1)))
            e.append(jnp.where(left, pltpu.roll(a, BLOCKS, 1), b))
        wide = [block_shift(x, -1) for x in e[4:]] + e + [block_shift(x, 1) for x in e[:4]]
        low, high = [], []
        for m in range(8):
            a, b = wide[2 * m], wide[2 * m + 1]
            low.append(jnp.where(sub < 4, a, pltpu.roll(b, 4, 0)))
            high.append(jnp.where(sub < 4, pltpu.roll(a, 4, 0), b))
        turned = jnp.concatenate(low + high, axis=0).T
        for z in range(2):
            out[pl.ds(2 * pair + z, BLOCKS, stride=CHUNK), :] = turned[
                z * BLOCKS : (z + 1) * BLOCKS
            ]


def pack_kernel(vel, rhs, inv, fwd, bwd, up, down):
    for c in range(3):
        for d in range(3):
            f = 3 * c + d
            fwd[3 * f : 3 * f + 3] = inv[c, d, 5:8]
            bwd[3 * f : 3 * f + 3] = inv[c, d, 0:3]
            up[f] = inv[c, d, :, 4:8, :]
            down[f] = inv[c, d, :, 0:4, :]
        fwd[27 + 3 * c : 30 + 3 * c] = rhs[c, 5:8]
        bwd[27 + 3 * c : 30 + 3 * c] = rhs[c, 0:3]
        up[9 + c] = rhs[c, :, 4:8, :]
        down[9 + c] = rhs[c, :, 0:4, :]
        fwd[36 + 4 * c : 40 + 4 * c] = vel[c, 4:8]
        bwd[36 + 4 * c : 40 + 4 * c] = vel[c, 0:4]
        up[12 + c] = vel[c, :, 4:8, :]
        down[12 + c] = vel[c, :, 0:4, :]


def corner_kernel(got, before, after, press, up, down):
    turned = got[...].T
    press[...] = turned
    for out, first, part in ((up, 4, 64), (down, 0, 0)):
        two = first + 2 if first else 0
        for m in range(8):
            out[m] = turned[part + 8 * m : part + 8 * m + 8]
        for f in range(12):
            for n, src in enumerate((before[3 * f + 1], before[3 * f + 2], after[3 * f], after[3 * f + 1])):
                out[8 + f, 2 * n : 2 * n + 2, :] = src[two : two + 2]
        for c in range(3):
            g = 36 + 4 * c
            out[20 + 2 * c, 0:4, :] = before[g + 3, first : first + 4, :]
            out[20 + 2 * c, 4:8, :] = after[g, first : first + 4, :]
            for n, src in enumerate((before[g + 1], before[g + 2], after[g + 1], after[g + 2])):
                out[21 + 2 * c, 2 * n : 2 * n + 2, :] = src[two : two + 2]


def sweep_kernel(vel, rhs, inv, press, before, after, rad_low, rad_high, cor_low, cor_high,
                 velocity, pressure, es, ef, eu, ep):
    for l in range(16):
        ep[l, 4:8, :] = press[4 * l : 4 * l + 4]
        ep[l, 8:12, :] = press[64 + 4 * l : 68 + 4 * l]
        ep[l, 0:4, :] = cor_low[l // 2, 4 * (l % 2) : 4 * (l % 2) + 4, :]
        ep[l, 12:16, :] = cor_high[l // 2, 4 * (l % 2) : 4 * (l % 2) + 4, :]
    for l in range(LINES):
        pressure[l] = ep[l + 4, 4:12, :]
    for f in range(12):
        c, d = f // 3, f % 3
        dst = es.at[f] if f < 9 else ef.at[f - 9]
        own = inv.at[c, d] if f < 9 else rhs.at[f - 9]
        dst[3:11, 4:12, :] = own[...]
        dst[3:11, 0:4, :] = rad_low[f]
        dst[3:11, 12:16, :] = rad_high[f]
        dst[0:3, 4:12, :] = before[3 * f : 3 * f + 3]
        dst[11:14, 4:12, :] = after[3 * f : 3 * f + 3]
        for n, line in enumerate((1, 2, 11, 12)):
            dst[line, 2:4, :] = cor_low[8 + f, 2 * n : 2 * n + 2, :]
            dst[line, 12:14, :] = cor_high[8 + f, 2 * n : 2 * n + 2, :]
    for c in range(3):
        dst = eu.at[0, c]
        g = 36 + 4 * c
        dst[4:12, 4:12, :] = vel[c]
        dst[4:12, 0:4, :] = rad_low[12 + c]
        dst[4:12, 12:16, :] = rad_high[12 + c]
        dst[0:4, 4:12, :] = before[g : g + 4]
        dst[12:16, 4:12, :] = after[g : g + 4]
        for n, line in enumerate((3, 12)):
            dst[line, 0:4, :] = cor_low[20 + 2 * c, 4 * n : 4 * n + 4, :]
            dst[line, 12:16, :] = cor_high[20 + 2 * c, 4 * n : 4 * n + 4, :]
        for n, line in enumerate((1, 2, 13, 14)):
            dst[line, 2:4, :] = cor_low[21 + 2 * c, 2 * n : 2 * n + 2, :]
            dst[line, 12:14, :] = cor_high[21 + 2 * c, 2 * n : 2 * n + 2, :]

    def line_step(sweep, j):
        now, later = sweep % 2, 1 - sweep % 2
        if sweep == 0:
            mid = ep[j + 1]
            ef[0, j] = ef[0, j] - (ep[j + 2] - ep[j]) * 0.5
            ef[1, j] = ef[1, j] - (pltpu.roll(mid, 15, 0) - pltpu.roll(mid, 1, 0)) * 0.5
            ef[2, j] = ef[2, j] - (axial(mid, 1) - axial(mid, -1)) * 0.5
        state, res = [], []
        for c in range(3):
            u = eu[now, c, j + 1]
            beside = (eu[now, c, j] + eu[now, c, j + 2]) + (pltpu.roll(u, 15, 0) + pltpu.roll(u, 1, 0))
            beside = beside + (axial(u, 1) + axial(u, -1))
            state.append(u)
            res.append(ef[c, j] - ((1.0 + 6.0 * coupling) * u - coupling * beside))
        for c in range(3):
            new = state[c] + es[3 * c, j] * res[0] + es[3 * c + 1, j] * res[1] + es[3 * c + 2, j] * res[2]
            if sweep == SWEEPS - 1:
                velocity[c, j - 3] = new[4:12]
            else:
                eu[later, c, j + 1] = new

    for sweep in range(SWEEPS):
        @pl.loop(sweep, 14 - sweep)
        def _(j, sweep=sweep):
            line_step(sweep, j)


def both_ways(up, down, axis, periodic):
    count = lax.axis_size(axis)
    forward = [(i, i + 1) for i in range(count - 1)]
    if periodic:
        forward.append((count - 1, 0))
    backward = [(target, source) for source, target in forward]
    return lax.ppermute(up, axis, forward), lax.ppermute(down, axis, backward)


def on_device(vel, rhs_mom, mode_inv, sweep_inv):
    h1, l1, h2, l2 = [jnp.asarray(t) for t in cas_tables()]
    up, down = pl.pallas_call(
        face_kernel,
        grid=(1,),
        in_specs=[pl.BlockSpec((1, LINES, CR, NZ), lambda i: (1, 0, 0, 0))],
        out_specs=[pl.BlockSpec((LINES, NZ), lambda i: (0, 0))] * 2,
        out_shape=[shape(LINES, NZ)] * 2,
        compiler_params=params(),
        name="faces",
    )(vel)
    low, high = both_ways(up, down, "radial", False)
    sent = pl.pallas_call(
        div_kernel,
        in_specs=[VMEM] * 3,
        out_specs=VMEM,
        out_shape=shape(NZ, 128),
        compiler_params=params(),
        name="divergence",
    )(vel, low, high)
    sent = sent.reshape(BLOCKS, CHUNK, 128)
    got = lax.all_to_all(sent, "pitch", split_axis=0, concat_axis=0, tiled=True)

    vel_b, rhs_b, inv_b, _ = lax.optimization_barrier((vel, rhs_mom, sweep_inv, sent))
    fwd, bwd, up, down = pl.pallas_call(
        pack_kernel,
        in_specs=[VMEM] * 3,
        out_specs=[VMEM] * 4,
        out_shape=[shape(48, CR, NZ)] * 2 + [shape(15, LINES, 4, NZ)] * 2,
        compiler_params=params(),
        name="pack",
    )(vel_b, rhs_b, inv_b)
    before, after = both_ways(fwd, bwd, "pitch", True)

    modes = jnp.transpose(mode_inv, (1, 2, 0))
    sent = pl.pallas_call(
        modes_kernel,
        in_specs=[VMEM] * 6,
        out_specs=VMEM,
        out_shape=shape(NZ, 128),
        compiler_params=params(),
        name="modes",
    )(got.reshape(NZ, 128), modes, h1, l1, h2, l2)
    sent = sent.reshape(BLOCKS, CHUNK, 128)
    got = lax.all_to_all(sent, "pitch", split_axis=0, concat_axis=0, tiled=True)
    up, down, _ = lax.optimization_barrier((up, down, sent))
    rad_low, rad_high = both_ways(up, down, "radial", False)

    press, up, down = pl.pallas_call(
        corner_kernel,
        in_specs=[VMEM] * 3,
        out_specs=[VMEM] * 3,
        out_shape=[shape(128, NZ)] + [shape(26, CR, NZ)] * 2,
        compiler_params=params(),
        name="corners",
    )(got.reshape(NZ, 128), before, after)
    cor_low, cor_high = both_ways(up, down, "radial", False)

    return pl.pallas_call(
        sweep_kernel,
        in_specs=[VMEM] * 10,
        out_specs=[VMEM] * 2,
        out_shape=[shape(3, LINES, CR, NZ), shape(LINES, CR, NZ)],
        scratch_shapes=[
            pltpu.VMEM((9, 14, 16, NZ), F32),
            pltpu.VMEM((3, 14, 16, NZ), F32),
            pltpu.VMEM((2, 3, 16, 16, NZ), F32),
            pltpu.VMEM((16, 16, NZ), F32),
        ],
        compiler_params=params(),
        name="sweeps",
    )(vel, rhs_mom, sweep_inv, press, before, after, rad_low, rad_high, cor_low, cor_high)


def solution(mesh):
    return jax.shard_map(
        on_device,
        mesh=mesh,
        in_specs=(
            P(None, "pitch", "radial", None),
            P(None, "pitch", "radial", None),
            P(None, "radial", None),
            P(None, None, "pitch", "radial", None),
        ),
        out_specs=(P(None, "pitch", "radial", None), P("pitch", "radial", None)),
        check_vma=False,
    )
```

time: 218 us -> 105 us (0.48)
  starting transfers between devices: 112 us -> 60.7 us
  waiting for transfers between devices: 54.2 us -> 28.1 us
  local copies, waits for them, and re-layouts: 29.8 us -> 4.98 us
  matrix products: 15.4 us -> 0 us
  Pallas kernels: 0 us -> 9.66 us
  other arithmetic: 3.46 us -> 0 us
    ppermute x24 -> x8, starting transfers between devices: 103 us -> 32.6 us  [both_ways(): return (lax.ppermute(up, axis, forward), lax.ppermute(down, axis, backward))]
    ppermute x24 -> x8, waiting for transfers between devices: 36.7 us -> 16.8 us  [both_ways(): return (lax.ppermute(up, axis, forward), lax.ppermute(down, axis, backward))]
    all_to_all x2, starting transfers between devices: 9.23 us -> 28.1 us  [on_device(): got = lax.all_to_all(sent, 'pitch', split_axis=0, concat_axis=0, tiled=True)]
    dot_general x3 -> x0, matrix products: 15.4 us -> none  [the longest x1 5.55 us: on_device(): jnp.dot(table, modes.reshape(lines, -1), precision=highest)]
    slice x23 -> x0, local copies, waits for them, and re-layouts: 10.9 us -> none  [the longest x17 7.98 us: extended(): lax.slice_in_dim(block, 0, width, axis=dim)]
    pallas_call x0 -> x6, Pallas kernels: none -> 9.66 us  [the longest x1 5.81 us: on_device(): pl.pallas_call(sweep_kernel, in_specs=[VMEM] * 10, out_specs=[VMEM] * 2,...]
    all_to_all x2, waiting for transfers between devices: 17.5 us -> 11.3 us  [on_device(): got = lax.all_to_all(sent, 'pitch', split_axis=0, concat_axis=0, tiled=True)]
    ppermute x12 -> x0, local copies, waits for them, and re-layouts: 4.13 us -> none  [the longest x6 2.51 us: extended(): lax.ppermute(lax.slice_in_dim(block, 0, width, axis=dim), axis, backward)]
  transfers between devices with their start and end apart: 26 -> 10, of which waited for: 7 -> 6; matrix products, arithmetic and copies ran while one was open for 9% -> 0% of each run, Pallas kernels for 0% -> 3%
where the time goes in v1:
time: 105 us; the launch traced here: 104 us
  starting transfers between devices  60.7 us (58%)
  waiting for transfers between devices  28.1 us (27%)
  Pallas kernels  9.66 us (9%)
  local copies, waits for them, and re-layouts  4.98 us (5%)
    ppermute x8, starting transfers between devices, both_ways(): return (lax.ppermute(up, axis, forward), lax.ppermute(down, axis, backward))  32.6 us
    all_to_all x2, starting transfers between devices, on_device(): got = lax.all_to_all(sent, 'pitch', split_axis=0, concat_axis=0, tiled=True)  28.1 us
    ppermute x8, waiting for transfers between devices, both_ways(): return (lax.ppermute(up, axis, forward), lax.ppermute(down, axis, backward))  16.8 us
    all_to_all x2, waiting for transfers between devices, on_device(): got = lax.all_to_all(sent, 'pitch', split_axis=0, concat_axis=0, tiled=True)  11.3 us
    pallas_call x1, Pallas kernels, on_device(): pl.pallas_call(sweep_kernel, in_specs=[VMEM] * 10, out_specs=[VMEM] * 2,...  5.81 us
    unnamed x20, local copies, waits for them, and re-layouts  4.98 us
  transfers between devices with their start and end apart: 10, of which 6 were waited for; matrix products, arithmetic and copies ran while one was open for 0% of the time, Pallas kernels for 3%

profile of v1, /device:TPU:1, one launch (start us, length us, event | category | flops | bytes accessed | tf_op | source)
XLA Modules:
  0.0 104.3 jit_solution(4808915702970403829)
XLA Ops:
  0.6 0.0 copy-start
  0.6 0.9 copy-done
  1.6 0.0 copy-start.2
  1.6 5.5 %collective-permute-start = (f32[8,256]{1,0:T(8,128)S(1)}, f32[8,256]{1,0:T(8,128)S(1)}, u32[]{:S(2)}, u32[]{:S(2)}) collective-permute-start(f32[8,256]{1,0:T(8,128)S(1)} %get-tuple-element.16), channel_id=1, source_target_pairs={{0,1},{1,2},{2,3},{3,4},{4,5},{5,6},{6,7},{8,9},{9,10},{10,11},{11... | collective-permute-start | bytes 24584 | tf_op jit(solution)/shard_map/ppermute | solution.py:237
  7.1 4.7 %collective-permute-start.1 = (f32[8,256]{1,0:T(8,128)S(1)}, f32[8,256]{1,0:T(8,128)S(1)}, u32[]{:S(2)}, u32[]{:S(2)}) collective-permute-start(f32[8,256]{1,0:T(8,128)S(1)} %get-tuple-element.17), channel_id=1, source_target_pairs={{1,0},{2,1},{3,2},{4,3},{5,4},{6,5},{7,6},{9,8},{10,9},{11,10},{12... | collective-permute-start | bytes 24584 | tf_op jit(solution)/shard_map/ppermute | solution.py:237
  11.8 0.0 collective-permute-done.low
  11.8 0.8 collective-permute-done.1.high
  12.6 0.8 divergence.1
  13.4 0.0 copy-start.1
  13.5 17.4 %all-to-all-start = ((f32[64,4,128]{2,1,0:T(4,128)}), f32[64,4,128]{2,1,0:T(4,128)S(1)}, u32[]{:S(2)}, u32[]{:S(2)}) async-start(f32[64,4,128]{2,1,0:T(4,128)} %bitcast), calls=%async_computation | async-start | bytes 262144 | tf_op jit(solution)/shard_map/all_to_all | solution.py:261
  30.9 0.0 copy-done.2
  30.9 0.0 copy-done.1
  30.9 0.0 copy-start.3
  30.9 0.9 copy-done.3
  31.8 0.0 copy-start.5
  31.9 0.0 copy-start.9
  31.9 1.1 %pack.1 = (f32[48,8,256]{2,1,0:T(8,128)}, f32[48,8,256]{2,1,0:T(8,128)}, f32[15,8,4,256]{3,2,1,0:T(4,128)}, f32[15,8,4,256]{3,2,1,0:T(4,128)S(1)}) custom-call(f32[3,8,8,256]{3,2,1,0:T(8,128)S(1)} %copy-done.1, f32[3,8,8,256]{3,2,1,0:T(8,128)S(1)} %copy-done.3, f32[3,3,8,8,256]{4,3,2,1,0:T(8,128)S(1)} %copy-done.2), custom_call_target="tpu_custom_call" | custom-call | tf_op jit(solution)/shard_map/pack/pallas_call | solution.py:264
  33.0 6.8 %collective-permute-start.2 = (f32[48,8,256]{2,1,0:T(8,128)}, f32[48,8,256]{2,1,0:T(8,128)S(1)}, u32[]{:S(2)}, u32[]{:S(2)}) collective-permute-start(f32[48,8,256]{2,1,0:T(8,128)} %get-tuple-element.21), channel_id=1, source_target_pairs={{0,8},{8,16},{16,24},{24,32},{32,40},{40,48},{48,56},{56,64},{64,7... | collective-permute-start | bytes 1179656 | tf_op jit(solution)/shard_map/ppermute | solution.py:237
  39.8 6.6 %collective-permute-start.3 = (f32[48,8,256]{2,1,0:T(8,128)}, f32[48,8,256]{2,1,0:T(8,128)S(1)}, u32[]{:S(2)}, u32[]{:S(2)}) collective-permute-start(f32[48,8,256]{2,1,0:T(8,128)} %get-tuple-element.22), channel_id=1, source_target_pairs={{8,0},{16,8},{24,16},{32,24},{40,32},{48,40},{56,48},{64,56},{72,6... | collective-permute-start | bytes 1179656 | tf_op jit(solution)/shard_map/ppermute | solution.py:237
  46.4 0.0 all-to-all-done
  46.4 0.0 copy-done.5
  46.4 0.0 copy-done.9
  46.4 0.0 copy-start.6
  46.5 1.0 copy-done.6
  47.5 0.0 copy-start.7
  47.5 1.0 copy-done.7
  48.5 0.0 copy-start.8
  48.5 1.0 copy-done.8
  49.6 1.7 %modes.1 = f32[256,128]{1,0:T(8,128)} custom-call(f32[256,128]{1,0:T(8,128)S(1)} %bitcast.5, f32[8,8,512]{2,1,0:T(8,128)S(1)} %bitcast.7, bf16[512,512]{1,0:T(8,128)(2,1)S(1)} %copy-done.8, bf16[512,512]{1,0:T(8,128)(2,1)S(1)} %copy-done.7, bf16[512,512]{1,0:T(8,128)(2,1)S(1)} %copy-done.6, bf16[512,512]{1,0:T(8,128)(2,1)S(1)} %copy-done.5), custom_call_target="tpu_custom_call" | custom-call | tf_op jit(solution)/shard_map/modes/pallas_call | solution.py:275
  51.3 2.8 %collective-permute-start.4 = (f32[15,8,4,256]{3,2,1,0:T(4,128)}, f32[15,8,4,256]{3,2,1,0:T(4,128)S(1)}, u32[]{:S(2)}, u32[]{:S(2)}) collective-permute-start(f32[15,8,4,256]{3,2,1,0:T(4,128)} %get-tuple-element.26), channel_id=1, source_target_pairs={{0,1},{1,2},{2,3},{3,4},{4,5},{5,6},{6,7},{8,9},{9,10},{10,11},{11... | collective-permute-start | bytes 1474568 | tf_op jit(solution)/shard_map/ppermute | solution.py:237
  54.1 1.9 %collective-permute-start.5 = (f32[15,8,4,256]{3,2,1,0:T(4,128)S(1)}, f32[15,8,4,256]{3,2,1,0:T(4,128)S(1)}, u32[]{:S(2)}, u32[]{:S(2)}) collective-permute-start(f32[15,8,4,256]{3,2,1,0:T(4,128)S(1)} %get-tuple-element.27), channel_id=1, source_target_pairs={{1,0},{2,1},{3,2},{4,3},{5,4},{6,5},{7,6},{9,8},{10,9},{11,10},{12... | collective-permute-start | bytes 1474568 | tf_op jit(solution)/shard_map/ppermute | solution.py:237
  56.0 10.6 %all-to-all-start.1 = ((f32[64,4,128]{2,1,0:T(4,128)}), f32[64,4,128]{2,1,0:T(4,128)S(1)}, u32[]{:S(2)}, u32[]{:S(2)}) async-start(f32[64,4,128]{2,1,0:T(4,128)} %bitcast.3), calls=%async_computation.1 | async-start | bytes 262144 | tf_op jit(solution)/shard_map/all_to_all | solution.py:284
  66.7 5.5 %collective-permute-done.2.before = f32[48,8,256]{2,1,0:T(8,128)S(1)} collective-permute-done((f32[48,8,256]{2,1,0:T(8,128)}, f32[48,8,256]{2,1,0:T(8,128)S(1)}, u32[]{:S(2)}, u32[]{:S(2)}) %collective-permute-start.2) | collective-permute-done | bytes 393248 | tf_op jit(solution)/shard_map/ppermute | solution.py:237
  72.1 5.8 %collective-permute-done.3.after = f32[48,8,256]{2,1,0:T(8,128)S(1)} collective-permute-done((f32[48,8,256]{2,1,0:T(8,128)}, f32[48,8,256]{2,1,0:T(8,128)S(1)}, u32[]{:S(2)}, u32[]{:S(2)}) %collective-permute-start.3) | collective-permute-done | bytes 393248 | tf_op jit(solution)/shard_map/ppermute | solution.py:237
  77.9 11.3 %all-to-all-done.1 = f32[64,4,128]{2,1,0:T(4,128)S(1)} async-done(((f32[64,4,128]{2,1,0:T(4,128)}), f32[64,4,128]{2,1,0:T(4,128)S(1)}, u32[]{:S(2)}, u32[]{:S(2)}) %all-to-all-start.1) | async-done | bytes 131104 | tf_op jit(solution)/shard_map/all_to_all | solution.py:284
  89.2 0.0 copy-start.4
  89.2 0.1 corners.1
  89.4 1.9 %collective-permute-start.6 = (f32[26,8,256]{2,1,0:T(8,128)S(1)}, f32[26,8,256]{2,1,0:T(8,128)S(1)}, u32[]{:S(2)}, u32[]{:S(2)}) collective-permute-start(f32[26,8,256]{2,1,0:T(8,128)S(1)} %get-tuple-element.28), channel_id=1, source_target_pairs={{0,1},{1,2},{2,3},{3,4},{4,5},{5,6},{6,7},{8,9},{9,10},{10,11},{11... | collective-permute-start | bytes 638984 | tf_op jit(solution)/shard_map/ppermute | solution.py:237
  91.3 2.4 %collective-permute-start.7 = (f32[26,8,256]{2,1,0:T(8,128)S(1)}, f32[26,8,256]{2,1,0:T(8,128)S(1)}, u32[]{:S(2)}, u32[]{:S(2)}) collective-permute-start(f32[26,8,256]{2,1,0:T(8,128)S(1)} %get-tuple-element.29), channel_id=1, source_target_pairs={{1,0},{2,1},{3,2},{4,3},{5,4},{6,5},{7,6},{9,8},{10,9},{11,10},{12... | collective-permute-start | bytes 638984 | tf_op jit(solution)/shard_map/ppermute | solution.py:237
  93.7 0.3 collective-permute-done.6.cor_low
  94.1 4.4 %collective-permute-done.7.cor_high = f32[26,8,256]{2,1,0:T(8,128)S(1)} collective-permute-done((f32[26,8,256]{2,1,0:T(8,128)S(1)}, f32[26,8,256]{2,1,0:T(8,128)S(1)}, u32[]{:S(2)}, u32[]{:S(2)}) %collective-permute-start.7) | collective-permute-done | bytes 213024 | tf_op jit(solution)/shard_map/ppermute | solution.py:237
  98.5 0.0 collective-permute-done.4.rad_low
  98.5 0.0 collective-permute-done.5.rad_high
  98.5 0.0 copy-done.4
  98.5 5.8 %sweeps.1 = (f32[3,8,8,256]{3,2,1,0:T(8,128)}, f32[8,8,256]{2,1,0:T(8,128)}) custom-call(f32[3,8,8,256]{3,2,1,0:T(8,128)S(1)} %copy-done.1, f32[3,8,8,256]{3,2,1,0:T(8,128)S(1)} %copy-done.4, f32[3,3,8,8,256]{4,3,2,1,0:T(8,128)S(1)} %copy-done.2, f32[128,256]{1,0:T(8,128)S(1)} %get-tuple-element.23.press, f32[48,8,256]{2,1,0:T(8,128)S(1)} %collective-permute-done.2.before, ...), custom_call_target="tpu_custom_call" | custom-call | tf_op jit(solution)/shard_map/sweeps/pallas_call | solution.py:298
  (1 shorter events, 0.0 us)
Async XLA Ops:
  0.6 0.9 copy-start
  1.6 29.3 %copy-start.2 = (f32[3,3,8,8,256]{4,3,2,1,0:T(8,128)S(1)}, f32[3,3,8,8,256]{4,3,2,1,0:T(8,128)}, u32[]{:S(2)}) copy-start(f32[3,3,8,8,256]{4,3,2,1,0:T(8,128)} %inv.2) | copy-start | bytes 1769476
  1.6 10.2 %collective-permute-start = (f32[8,256]{1,0:T(8,128)S(1)}, f32[8,256]{1,0:T(8,128)S(1)}, u32[]{:S(2)}, u32[]{:S(2)}) collective-permute-start(f32[8,256]{1,0:T(8,128)S(1)} %get-tuple-element.16), channel_id=1, source_target_pairs={{0,1},{1,2},{2,3},{3,4},{4,5},{5,6},{6,7},{8,9},{9,10},{10,11},{11... | collective-permute-start | bytes 24584 | tf_op jit(solution)/shard_map/ppermute | solution.py:237
  7.1 5.5 %collective-permute-start.1 = (f32[8,256]{1,0:T(8,128)S(1)}, f32[8,256]{1,0:T(8,128)S(1)}, u32[]{:S(2)}, u32[]{:S(2)}) collective-permute-start(f32[8,256]{1,0:T(8,128)S(1)} %get-tuple-element.17), channel_id=1, source_target_pairs={{1,0},{2,1},{3,2},{4,3},{5,4},{6,5},{7,6},{9,8},{10,9},{11,10},{12... | collective-permute-start | bytes 24584 | tf_op jit(solution)/shard_map/ppermute | solution.py:237
  13.4 17.5 %copy-start.1 = (f32[3,8,8,256]{3,2,1,0:T(8,128)S(1)}, f32[3,8,8,256]{3,2,1,0:T(8,128)}, u32[]{:S(2)}) copy-start(f32[3,8,8,256]{3,2,1,0:T(8,128)} %vel.4) | copy-start | bytes 589828
  13.5 33.0 %all-to-all-start = ((f32[64,4,128]{2,1,0:T(4,128)}), f32[64,4,128]{2,1,0:T(4,128)S(1)}, u32[]{:S(2)}, u32[]{:S(2)}) async-start(f32[64,4,128]{2,1,0:T(4,128)} %bitcast), calls=%async_computation | async-start | bytes 262144 | tf_op jit(solution)/shard_map/all_to_all | solution.py:261
  30.9 0.9 copy-start.3
  31.8 14.6 %copy-start.5 = (bf16[512,512]{1,0:T(8,128)(2,1)S(1)}, bf16[512,512]{1,0:T(8,128)(2,1)}, u32[]{:S(2)}) copy-start(bf16[512,512]{1,0:T(8,128)(2,1)} %constant.11.clone.l2) | copy-start | bytes 1572868
  31.9 14.6 %copy-start.9 = (f32[512,8,8]{0,2,1:T(8,128)S(1)}, f32[512,8,8]{0,2,1:T(8,128)}, u32[]{:S(2)}) copy-start(f32[512,8,8]{0,2,1:T(8,128)} %param.10) | copy-start | bytes 393220
  33.0 39.1 %collective-permute-start.2 = (f32[48,8,256]{2,1,0:T(8,128)}, f32[48,8,256]{2,1,0:T(8,128)S(1)}, u32[]{:S(2)}, u32[]{:S(2)}) collective-permute-start(f32[48,8,256]{2,1,0:T(8,128)} %get-tuple-element.21), channel_id=1, source_target_pairs={{0,8},{8,16},{16,24},{24,32},{32,40},{40,48},{48,56},{56,64},{64,7... | collective-permute-start | bytes 1179656 | tf_op jit(solution)/shard_map/ppermute | solution.py:237
  39.8 38.1 %collective-permute-start.3 = (f32[48,8,256]{2,1,0:T(8,128)}, f32[48,8,256]{2,1,0:T(8,128)S(1)}, u32[]{:S(2)}, u32[]{:S(2)}) collective-permute-start(f32[48,8,256]{2,1,0:T(8,128)} %get-tuple-element.22), channel_id=1, source_target_pairs={{8,0},{16,8},{24,16},{32,24},{40,32},{48,40},{56,48},{64,56},{72,6... | collective-permute-start | bytes 1179656 | tf_op jit(solution)/shard_map/ppermute | solution.py:237
  46.4 1.0 %copy-start.6 = (bf16[512,512]{1,0:T(8,128)(2,1)S(1)}, bf16[512,512]{1,0:T(8,128)(2,1)}, u32[]{:S(2)}) copy-start(bf16[512,512]{1,0:T(8,128)(2,1)} %constant.10.clone.h2) | copy-start | bytes 1572868
  47.5 1.0 copy-start.7
  48.5 1.0 copy-start.8
  51.3 47.2 %collective-permute-start.4 = (f32[15,8,4,256]{3,2,1,0:T(4,128)}, f32[15,8,4,256]{3,2,1,0:T(4,128)S(1)}, u32[]{:S(2)}, u32[]{:S(2)}) collective-permute-start(f32[15,8,4,256]{3,2,1,0:T(4,128)} %get-tuple-element.26), channel_id=1, source_target_pairs={{0,1},{1,2},{2,3},{3,4},{4,5},{5,6},{6,7},{8,9},{9,10},{10,11},{11... | collective-permute-start | bytes 1474568 | tf_op jit(solution)/shard_map/ppermute | solution.py:237
  54.1 44.4 %collective-permute-start.5 = (f32[15,8,4,256]{3,2,1,0:T(4,128)S(1)}, f32[15,8,4,256]{3,2,1,0:T(4,128)S(1)}, u32[]{:S(2)}, u32[]{:S(2)}) collective-permute-start(f32[15,8,4,256]{3,2,1,0:T(4,128)S(1)} %get-tuple-element.27), channel_id=1, source_target_pairs={{1,0},{2,1},{3,2},{4,3},{5,4},{6,5},{7,6},{9,8},{10,9},{11,10},{12... | collective-permute-start | bytes 1474568 | tf_op jit(solution)/shard_map/ppermute | solution.py:237
  56.0 33.2 %all-to-all-start.1 = ((f32[64,4,128]{2,1,0:T(4,128)}), f32[64,4,128]{2,1,0:T(4,128)S(1)}, u32[]{:S(2)}, u32[]{:S(2)}) async-start(f32[64,4,128]{2,1,0:T(4,128)} %bitcast.3), calls=%async_computation.1 | async-start | bytes 262144 | tf_op jit(solution)/shard_map/all_to_all | solution.py:284
  89.2 9.2 %copy-start.4 = (f32[3,8,8,256]{3,2,1,0:T(8,128)S(1)}, f32[3,8,8,256]{3,2,1,0:T(8,128)}, u32[]{:S(2)}) copy-start(f32[3,8,8,256]{3,2,1,0:T(8,128)} %rhs.2) | copy-start | bytes 589828
  89.4 4.7 %collective-permute-start.6 = (f32[26,8,256]{2,1,0:T(8,128)S(1)}, f32[26,8,256]{2,1,0:T(8,128)S(1)}, u32[]{:S(2)}, u32[]{:S(2)}) collective-permute-start(f32[26,8,256]{2,1,0:T(8,128)S(1)} %get-tuple-element.28), channel_id=1, source_target_pairs={{0,1},{1,2},{2,3},{3,4},{4,5},{5,6},{6,7},{8,9},{9,10},{10,11},{11... | collective-permute-start | bytes 638984 | tf_op jit(solution)/shard_map/ppermute | solution.py:237
  91.3 7.2 %collective-permute-start.7 = (f32[26,8,256]{2,1,0:T(8,128)S(1)}, f32[26,8,256]{2,1,0:T(8,128)S(1)}, u32[]{:S(2)}, u32[]{:S(2)}) collective-permute-start(f32[26,8,256]{2,1,0:T(8,128)S(1)} %get-tuple-element.29), channel_id=1, source_target_pairs={{1,0},{2,1},{3,2},{4,3},{5,4},{6,5},{7,6},{9,8},{10,9},{11,10},{12... | collective-permute-start | bytes 638984 | tf_op jit(solution)/shard_map/ppermute | solution.py:237

commit v2 on v1

v2 whole, which is shorter than its diff:
```python
import functools

import jax
import jax.numpy as jnp
import ml_dtypes
import numpy as np
from jax import lax
from jax.experimental import pallas as pl
from jax.experimental.pallas import tpu as pltpu
from jax.sharding import PartitionSpec as P

SWEEPS = 4
FIRST = (13,)
BULK = tuple(range(13)) + (14,)
coupling = 0.5
NP, CR, NZ = 512, 8, 256
BLOCKS = 64
LINES = NP // BLOCKS
CHUNK = NZ // BLOCKS
F32 = jnp.float32
BF16 = jnp.bfloat16


def cas_tables():
    index = np.arange(NP)
    angle = 2.0 * np.pi / NP * (index[:, None] * index[None, :] % NP)
    table = np.cos(angle) + np.sin(angle)
    order = (np.arange(BLOCKS)[None, :] * LINES + np.arange(LINES)[:, None]).reshape(-1)
    mat = table[order, :]
    high = mat.astype(ml_dtypes.bfloat16)
    low = (mat - high.astype(np.float64)).astype(ml_dtypes.bfloat16)
    return np.concatenate([high, low])


def params(mib=24):
    return pltpu.CompilerParams(vmem_limit_bytes=mib * 1024 * 1024)


VMEM = pl.BlockSpec(memory_space=pltpu.VMEM)


def shape(*dims):
    return jax.ShapeDtypeStruct(dims, F32)


def axial(x, step):
    lane = lax.broadcasted_iota(jnp.int32, x.shape, x.ndim - 1)
    moved = pltpu.roll(x, (-step) % NZ, x.ndim - 1)
    return jnp.where(lane == (NZ - 1 if step > 0 else 0), 0.0, moved)


def rows_of(vel, rhs, inv, f):
    return inv.at[f // 3, f % 3] if f < 9 else rhs.at[f - 9] if f < 12 else vel.at[f - 12]


def pack_rows(fields, vel, rhs, inv, up, down):
    for n, f in enumerate(fields):
        src = rows_of(vel, rhs, inv, f)
        up[n] = src[:, 4:8, :]
        down[n] = src[:, 0:4, :]


def div_kernel(vel, low, high, out):
    row = lax.broadcasted_iota(jnp.int32, (CR, NZ), 0)
    parts = []
    for l in range(LINES):
        v1, v2 = vel[1, l], vel[2, l]
        upper = jnp.where(row == CR - 1, high[0, l, 0:1, :], pltpu.roll(v1, CR - 1, 0))
        lower = jnp.where(row == 0, low[0, l, 3:4, :], pltpu.roll(v1, 1, 0))
        parts.append(((upper - lower) + (axial(v2, 1) - axial(v2, -1))) * 0.5)
    for l in range(LINES):
        parts.append(vel[0, l])
    out[...] = jnp.concatenate(parts, axis=0).T


def block_shift(x, step):
    lane = lax.broadcasted_iota(jnp.int32, x.shape, 1) % BLOCKS
    edge = BLOCKS - 1 if step > 0 else 0
    near = pltpu.roll(x, (-step) % 128, 1)
    far = pltpu.roll(x, (BLOCKS - step) % 128, 1)
    return jnp.where(lane == edge, far, near)


def split_dot(x, table, dim):
    dims = (((1,), (dim,)), ((), ()))
    xh = x.astype(BF16)
    xl = (x - xh.astype(F32)).astype(BF16)
    rows = x.shape[0]
    both = jnp.concatenate([xh, xl], axis=0)
    both = lax.dot_general(both, table[0:NP], dims, preferred_element_type=F32)
    cross = lax.dot_general(xh, table[NP : 2 * NP], dims, preferred_element_type=F32)
    return both[:rows] + (both[rows:] + cross)


def modes_kernel(got, mode, table, out):
    lane = lax.broadcasted_iota(jnp.int32, (CR, 128), 1)
    sub = lax.broadcasted_iota(jnp.int32, (CR, 128), 0)
    left = lane < BLOCKS
    half = CHUNK // 2
    rows = [[None] * 4 for _ in range(CHUNK)]
    for pair in range(half):
        slabs = [got[pl.ds(2 * pair + e, BLOCKS, stride=CHUNK), :] for e in range(2)]
        a = jnp.concatenate(slabs, axis=0).T
        w = [a[l * CR : (l + 1) * CR] for l in range(LINES)]
        v = [a[NP // 8 + l * CR : NP // 8 + (l + 1) * CR] for l in range(LINES)]
        before = [block_shift(v[-1], -1)] + v[:-1]
        after = v[1:] + [block_shift(v[0], 1)]
        d = [w[l] + (after[l] - before[l]) * 0.5 for l in range(LINES)]
        for t in range(4):
            e, o = d[2 * t], d[2 * t + 1]
            rows[2 * pair][t] = jnp.where(left, e, pltpu.roll(o, BLOCKS, 1))
            rows[2 * pair + 1][t] = jnp.where(left, pltpu.roll(e, BLOCKS, 1), o)
    x = jnp.concatenate([jnp.concatenate(r, axis=1) for r in rows], axis=0)
    dhat = split_dot(x, table, 0)
    q = []
    for z in range(CHUNK):
        total = None
        for s in range(CR):
            term = mode[:, s, :] * dhat[z * CR + s : z * CR + s + 1, :]
            total = term if total is None else total + term
        q.append(total)
    p = split_dot(jnp.concatenate(q, axis=0), table, 1) * (1.0 / NP)
    for pair in range(half):
        e = []
        for t in range(4):
            a = p[2 * pair * CR : (2 * pair + 1) * CR, t * 128 : (t + 1) * 128]
            b = p[(2 * pair + 1) * CR : (2 * pair + 2) * CR, t * 128 : (t + 1) * 128]
            e.append(jnp.where(left, a, pltpu.roll(b, BLOCKS, 1)))
            e.append(jnp.where(left, pltpu.roll(a, BLOCKS, 1), b))
        wide = [block_shift(x, -1) for x in e[4:]] + e + [block_shift(x, 1) for x in e[:4]]
        low, high = [], []
        for m in range(8):
            a, b = wide[2 * m], wide[2 * m + 1]
            low.append(jnp.where(sub < 4, a, pltpu.roll(b, 4, 0)))
            high.append(jnp.where(sub < 4, pltpu.roll(a, 4, 0), b))
        turned = jnp.concatenate(low + high, axis=0).T
        for z in range(2):
            out[pl.ds(2 * pair + z, BLOCKS, stride=CHUNK), :] = turned[
                z * BLOCKS : (z + 1) * BLOCKS
            ]


def pack_forward(vel, rhs, inv, fwd):
    for f in range(9):
        fwd[3 * f : 3 * f + 3] = inv[f // 3, f % 3, 1:4]
    for c in range(3):
        fwd[27 + 3 * c : 30 + 3 * c] = rhs[c, 1:4]
        fwd[36 + 4 * c : 40 + 4 * c] = vel[c]


def pack_rest(vel, rhs, inv, bwd, up, down):
    for f in range(9):
        bwd[3 * f : 3 * f + 3] = inv[f // 3, f % 3, 0:3]
    for c in range(3):
        bwd[27 + 3 * c : 30 + 3 * c] = rhs[c, 0:3]
        bwd[36 + 4 * c : 40 + 4 * c] = vel[c, 0:4]
    pack_rows(BULK, vel, rhs, inv, up, down)


def corner_kernel(side, halo, up, down):
    for out, first in ((up, 4), (down, 0)):
        two = first + 2 if first else 0
        for f in range(12):
            for n in range(2):
                src = halo[3 * f + n + 1 - side]
                out[f // 2, 4 * (f % 2) + 2 * n : 4 * (f % 2) + 2 * n + 2, :] = src[two : two + 2]
        for c in range(3):
            g = 36 + 4 * c
            out[6 + c, 0:4, :] = halo[g + 3 - 3 * side, first : first + 4, :]
            for n in range(2):
                src = halo[g + 1 + n]
                out[6 + c, 4 + 2 * n : 6 + 2 * n, :] = src[two : two + 2]


def turn_kernel(got, bef_up, bef_down, aft_up, aft_down, press, up, down):
    turned = got[...].T
    press[...] = turned
    for m in range(8):
        up[m] = turned[64 + 8 * m : 72 + 8 * m]
        down[m] = turned[8 * m : 8 * m + 8]
    up[8:17] = bef_up[...]
    down[8:17] = bef_down[...]
    up[17:26] = aft_up[...]
    down[17:26] = aft_down[...]


def beyond(f, first, bulk):
    return first[FIRST.index(f)] if f in FIRST else bulk[BULK.index(f)]


def sweep_kernel(vel, rhs, inv, press, before, after, low, high, rad_low, rad_high, cor_low, cor_high,
                 velocity, pressure, es, ef, eu, ep):
    for l in range(16):
        ep[l, 4:8, :] = press[4 * l : 4 * l + 4]
        ep[l, 8:12, :] = press[64 + 4 * l : 68 + 4 * l]
        ep[l, 0:4, :] = cor_low[l // 2, 4 * (l % 2) : 4 * (l % 2) + 4, :]
        ep[l, 12:16, :] = cor_high[l // 2, 4 * (l % 2) : 4 * (l % 2) + 4, :]
    for l in range(LINES):
        pressure[l] = ep[l + 4, 4:12, :]
    for f in range(12):
        c, d = f // 3, f % 3
        dst = es.at[f] if f < 9 else ef.at[f - 9]
        own = inv.at[c, d] if f < 9 else rhs.at[f - 9]
        dst[3:11, 4:12, :] = own[...]
        dst[3:11, 0:4, :] = beyond(f, low, rad_low)
        dst[3:11, 12:16, :] = beyond(f, high, rad_high)
        dst[0:3, 4:12, :] = before[3 * f : 3 * f + 3]
        dst[11:14, 4:12, :] = after[3 * f : 3 * f + 3]
        for n, line in enumerate((1, 2, 11, 12)):
            t, r = 8 + 9 * (n // 2) + f // 2, 4 * (f % 2) + 2 * (n % 2)
            dst[line, 2:4, :] = cor_low[t, r : r + 2, :]
            dst[line, 12:14, :] = cor_high[t, r : r + 2, :]
    for c in range(3):
        dst = eu.at[0, c]
        g = 36 + 4 * c
        dst[4:12, 4:12, :] = vel[c]
        dst[4:12, 0:4, :] = beyond(12 + c, low, rad_low)
        dst[4:12, 12:16, :] = beyond(12 + c, high, rad_high)
        dst[0:4, 4:12, :] = before[g : g + 4]
        dst[12:16, 4:12, :] = after[g : g + 4]
        for n, line in enumerate((3, 12)):
            t = 14 + 9 * n + c
            dst[line, 0:4, :] = cor_low[t, 0:4, :]
            dst[line, 12:16, :] = cor_high[t, 0:4, :]
        for n, line in enumerate((1, 2, 13, 14)):
            t, r = 14 + 9 * (n // 2) + c, 4 + 2 * (n % 2)
            dst[line, 2:4, :] = cor_low[t, r : r + 2, :]
            dst[line, 12:14, :] = cor_high[t, r : r + 2, :]

    def line_step(sweep, j):
        now, later = sweep % 2, 1 - sweep % 2
        if sweep == 0:
            mid = ep[j + 1]
            ef[0, j] = ef[0, j] - (ep[j + 2] - ep[j]) * 0.5
            ef[1, j] = ef[1, j] - (pltpu.roll(mid, 15, 0) - pltpu.roll(mid, 1, 0)) * 0.5
            ef[2, j] = ef[2, j] - (axial(mid, 1) - axial(mid, -1)) * 0.5
        state, res = [], []
        for c in range(3):
            u = eu[now, c, j + 1]
            beside = (eu[now, c, j] + eu[now, c, j + 2]) + (pltpu.roll(u, 15, 0) + pltpu.roll(u, 1, 0))
            beside = beside + (axial(u, 1) + axial(u, -1))
            state.append(u)
            res.append(ef[c, j] - ((1.0 + 6.0 * coupling) * u - coupling * beside))
        for c in range(3):
            new = state[c] + es[3 * c, j] * res[0] + es[3 * c + 1, j] * res[1] + es[3 * c + 2, j] * res[2]
            if sweep == SWEEPS - 1:
                velocity[c, j - 3] = new[4:12]
            else:
                eu[later, c, j + 1] = new

    for sweep in range(SWEEPS):
        @pl.loop(sweep, 14 - sweep)
        def _(j, sweep=sweep):
            line_step(sweep, j)


def both_ways(up, down, axis, periodic):
    count = lax.axis_size(axis)
    forward = [(i, i + 1) for i in range(count - 1)]
    if periodic:
        forward.append((count - 1, 0))
    backward = [(target, source) for source, target in forward]
    return lax.ppermute(up, axis, forward), lax.ppermute(down, axis, backward)


def corners(side, halo):
    return pl.pallas_call(
        functools.partial(corner_kernel, side),
        in_specs=[VMEM],
        out_specs=[VMEM] * 2,
        out_shape=[shape(9, CR, NZ)] * 2,
        compiler_params=params(8),
        name="corners",
    )(halo)


def on_device(vel, rhs_mom, mode_inv, sweep_inv):
    table = jnp.asarray(cas_tables())
    up, down = pl.pallas_call(
        functools.partial(pack_rows, FIRST),
        in_specs=[VMEM] * 3,
        out_specs=[VMEM] * 2,
        out_shape=[shape(len(FIRST), LINES, 4, NZ)] * 2,
        compiler_params=params(60),
        name="pack_first",
    )(vel, rhs_mom, sweep_inv)
    low, high = both_ways(up, down, "radial", False)
    fwd = pl.pallas_call(
        pack_forward,
        grid=(1,),
        in_specs=[pl.BlockSpec((3, 4, CR, NZ), lambda i: (0, 1, 0, 0))] * 2
        + [pl.BlockSpec((3, 3, 4, CR, NZ), lambda i: (0, 0, 1, 0, 0))],
        out_specs=pl.BlockSpec((48, CR, NZ), lambda i: (0, 0, 0)),
        out_shape=shape(48, CR, NZ),
        compiler_params=params(60),
        name="pack_forward",
    )(vel, rhs_mom, sweep_inv)
    fwd, low, high = lax.optimization_barrier((fwd, low, high))
    before = lax.ppermute(fwd, "pitch", [(i, (i + 1) % BLOCKS) for i in range(BLOCKS)])
    sent = pl.pallas_call(
        div_kernel,
        grid=(1,),
        in_specs=[pl.BlockSpec((3, LINES, CR, NZ), lambda i: (0, 0, 0, 0))]
        + [pl.BlockSpec((1, LINES, 4, NZ), lambda i: (FIRST.index(13), 0, 0, 0))] * 2,
        out_specs=pl.BlockSpec((NZ, 128), lambda i: (0, 0)),
        out_shape=shape(NZ, 128),
        compiler_params=params(60),
        name="divergence",
    )(vel, low, high)
    sent = sent.reshape(BLOCKS, CHUNK, 128)
    vel_b, rhs_b, inv_b, sent = lax.optimization_barrier((vel, rhs_mom, sweep_inv, sent))
    got = lax.all_to_all(sent, "pitch", split_axis=0, concat_axis=0, tiled=True)
    bwd, up, down = pl.pallas_call(
        pack_rest,
        in_specs=[VMEM] * 3,
        out_specs=[VMEM] * 3,
        out_shape=[shape(48, CR, NZ)] + [shape(len(BULK), LINES, 4, NZ)] * 2,
        compiler_params=params(60),
        name="pack_rest",
    )(vel_b, rhs_b, inv_b)
    after = lax.ppermute(bwd, "pitch", [((i + 1) % BLOCKS, i) for i in range(BLOCKS)])

    bef = corners(0, before)
    got, bef = lax.optimization_barrier((got, bef))
    modes = jnp.transpose(mode_inv, (1, 2, 0))
    sent = pl.pallas_call(
        modes_kernel,
        in_specs=[VMEM] * 3,
        out_specs=VMEM,
        out_shape=shape(NZ, 128),
        compiler_params=params(8),
        name="modes",
    )(got.reshape(NZ, 128), modes, table)
    sent = sent.reshape(BLOCKS, CHUNK, 128)
    got = lax.all_to_all(sent, "pitch", split_axis=0, concat_axis=0, tiled=True)
    up, down, _ = lax.optimization_barrier((up, down, sent))
    after, _ = lax.optimization_barrier((after, sent))
    rad_low, rad_high = both_ways(up, down, "radial", False)
    aft = corners(1, after)
    press, up, down = pl.pallas_call(
        turn_kernel,
        in_specs=[VMEM] * 5,
        out_specs=[VMEM] * 3,
        out_shape=[shape(128, NZ)] + [shape(26, CR, NZ)] * 2,
        compiler_params=params(8),
        name="turn",
    )(got.reshape(NZ, 128), *bef, *aft)
    cor_low, cor_high = both_ways(up, down, "radial", False)

    return pl.pallas_call(
        sweep_kernel,
        in_specs=[VMEM] * 12,
        out_specs=[VMEM] * 2,
        out_shape=[shape(3, LINES, CR, NZ), shape(LINES, CR, NZ)],
        scratch_shapes=[
            pltpu.VMEM((9, 14, 16, NZ), F32),
            pltpu.VMEM((3, 14, 16, NZ), F32),
            pltpu.VMEM((2, 3, 16, 16, NZ), F32),
            pltpu.VMEM((16, 16, NZ), F32),
        ],
        compiler_params=params(16),
        name="sweeps",
    )(vel, rhs_mom, sweep_inv, press, before, after, low, high, rad_low, rad_high, cor_low, cor_high)


def solution(mesh):
    return jax.shard_map(
        on_device,
        mesh=mesh,
        in_specs=(
            P(None, "pitch", "radial", None),
            P(None, "pitch", "radial", None),
            P(None, "radial", None),
            P(None, None, "pitch", "radial", None),
        ),
        out_specs=(P(None, "pitch", "radial", None), P("pitch", "radial", None)),
        check_vma=False,
    )
```

time: 105 us -> 95.6 us (0.910)
  waiting for transfers between devices: 28.1 us -> 9.4 us
  starting transfers between devices: 60.7 us -> 69 us
  Pallas kernels: 9.66 us -> 15.7 us
  local copies, waits for them, and re-layouts: 4.98 us -> 0.04 us
    ppermute x0 -> x2, starting transfers between devices: none -> 20 us  [the longest x1 11.5 us: on_device(): lax.ppermute(bwd, 'pitch', [((i + 1) % BLOCKS, i) for i in range(BLOCKS)])]
    ppermute x8 -> x6, waiting for transfers between devices: 16.8 us -> 5.23 us  [both_ways(): return (lax.ppermute(up, axis, forward), lax.ppermute(down, axis, backward))]
    all_to_all x2, starting transfers between devices: 28.1 us -> 18.8 us  [on_device(): got = lax.all_to_all(sent, 'pitch', split_axis=0, concat_axis=0, tiled=True)]
    all_to_all x2, waiting for transfers between devices: 11.3 us -> 4.17 us  [on_device(): got = lax.all_to_all(sent, 'pitch', split_axis=0, concat_axis=0, tiled=True)]
    pallas_call x6 -> x9, Pallas kernels: 9.66 us -> 15.7 us  [the longest x1 5.81 us: on_device(): pl.pallas_call(sweep_kernel, in_specs=[VMEM] * 12, out_specs=[VMEM] * 2,...]
    unnamed x20, local copies, waits for them, and re-layouts: 4.98 us -> 0.04 us
    ppermute x8 -> x6, starting transfers between devices: 32.6 us -> 30.2 us  [both_ways(): return (lax.ppermute(up, axis, forward), lax.ppermute(down, axis, backward))]
  transfers between devices with their start and end apart: 10 -> 10, of which waited for: 6 -> 3; matrix products, arithmetic and copies ran while one was open for 0% -> 0% of each run, Pallas kernels for 3% -> 8%
where the time goes in v2:
time: 95.6 us; the launch traced here: 95.1 us
  starting transfers between devices  69 us (72%)
  Pallas kernels  15.7 us (16%)
  waiting for transfers between devices  9.4 us (10%)
    ppermute x6, starting transfers between devices, both_ways(): return (lax.ppermute(up, axis, forward), lax.ppermute(down, axis, backward))  30.2 us
    all_to_all x2, starting transfers between devices, on_device(): got = lax.all_to_all(sent, 'pitch', split_axis=0, concat_axis=0, tiled=True)  18.8 us
    ppermute x1, starting transfers between devices, on_device(): lax.ppermute(bwd, 'pitch', [((i + 1) % BLOCKS, i) for i in range(BLOCKS)])  11.5 us
    ppermute x1, starting transfers between devices, on_device(): lax.ppermute(fwd, 'pitch', [(i, (i + 1) % BLOCKS) for i in range(BLOCKS)])  8.56 us
    pallas_call x1, Pallas kernels, on_device(): pl.pallas_call(sweep_kernel, in_specs=[VMEM] * 12, out_specs=[VMEM] * 2,...  5.81 us
    ppermute x6, waiting for transfers between devices, both_ways(): return (lax.ppermute(up, axis, forward), lax.ppermute(down, axis, backward))  5.23 us
    all_to_all x2, waiting for transfers between devices, on_device(): got = lax.all_to_all(sent, 'pitch', split_axis=0, concat_axis=0, tiled=True)  4.17 us
    pallas_call x1, Pallas kernels, on_device(): pl.pallas_call(pack_rest, in_specs=[VMEM] * 3, out_specs=[VMEM] * 3, out_...  2.35 us
  transfers between devices with their start and end apart: 10, of which 3 were waited for; matrix products, arithmetic and copies ran while one was open for 0% of the time, Pallas kernels for 8%

profile of v2, /device:TPU:1, one launch (start us, length us, event | category | flops | bytes accessed | tf_op | source)
XLA Modules:
  0.0 95.1 jit_solution(8093444979351353176)
XLA Ops:
  0.6 1.9 %pack_first.1 = (f32[1,8,4,256]{3,2,1,0:T(4,128)}, f32[1,8,4,256]{3,2,1,0:T(4,128)}) custom-call(f32[3,8,8,256]{3,2,1,0:T(8,128)} %vel.8, f32[3,8,8,256]{3,2,1,0:T(8,128)} %rhs.6, f32[3,3,8,8,256]{4,3,2,1,0:T(8,128)} %inv.6), custom_call_target="tpu_custom_call" | custom-call | tf_op jit(solution)/shard_map/pack_first/pallas_call | solution.py:279
  2.5 5.4 %collective-permute-start = (f32[1,8,4,256]{3,2,1,0:T(4,128)}, f32[1,8,4,256]{3,2,1,0:T(4,128)S(1)}, u32[]{:S(2)}, u32[]{:S(2)}) collective-permute-start(f32[1,8,4,256]{3,2,1,0:T(4,128)} %get-tuple-element.27), channel_id=1, source_target_pairs={{0,1},{1,2},{2,3},{3,4},{4,5},{5,6},{6,7},{8,9},{9,10},{10,11},{11... | collective-permute-start | bytes 98312 | tf_op jit(solution)/shard_map/ppermute | solution.py:263
  7.9 4.7 %collective-permute-start.1 = (f32[1,8,4,256]{3,2,1,0:T(4,128)}, f32[1,8,4,256]{3,2,1,0:T(4,128)S(1)}, u32[]{:S(2)}, u32[]{:S(2)}) collective-permute-start(f32[1,8,4,256]{3,2,1,0:T(4,128)} %get-tuple-element.28), channel_id=1, source_target_pairs={{1,0},{2,1},{3,2},{4,3},{5,4},{6,5},{7,6},{9,8},{10,9},{11,10},{12... | collective-permute-start | bytes 98312 | tf_op jit(solution)/shard_map/ppermute | solution.py:263
  12.6 1.9 %pack_forward.1 = f32[48,8,256]{2,1,0:T(8,128)} custom-call(f32[3,8,8,256]{3,2,1,0:T(8,128)} %vel.8, f32[3,8,8,256]{3,2,1,0:T(8,128)} %rhs.6, f32[3,3,8,8,256]{4,3,2,1,0:T(8,128)} %inv.6), custom_call_target="tpu_custom_call" | custom-call | tf_op jit(solution)/shard_map/pack_forward/pallas_call | solution.py:288
  14.5 0.0 copy-start.3
  14.5 0.0 collective-permute-done.low
  14.5 0.0 copy-start.4
  14.5 0.0 collective-permute-done.1.high
  14.5 0.0 copy-start.6
  14.5 8.6 %collective-permute-start.2 = (f32[48,8,256]{2,1,0:T(8,128)}, f32[48,8,256]{2,1,0:T(8,128)S(1)}, u32[]{:S(2)}, u32[]{:S(2)}) collective-permute-start(f32[48,8,256]{2,1,0:T(8,128)} %pack_forward.1), channel_id=1, source_target_pairs={{0,8},{8,16},{16,24},{24,32},{32,40},{40,48},{48,56},{56,64},{64,7... | collective-permute-start | bytes 1179656 | tf_op jit(solution)/shard_map/ppermute | solution.py:299
  23.1 0.0 copy-done.4
  23.1 0.0 copy-done.6
  23.1 1.8 %divergence.1 = f32[256,128]{1,0:T(8,128)} custom-call(f32[3,8,8,256]{3,2,1,0:T(8,128)} %vel.8, f32[1,8,4,256]{3,2,1,0:T(4,128)} %copy-done.4, f32[1,8,4,256]{3,2,1,0:T(4,128)} %copy-done.6), custom_call_target="tpu_custom_call" | custom-call | tf_op jit(solution)/shard_map/divergence/pallas_call | solution.py:300
  24.9 10.3 %all-to-all-start = ((f32[64,4,128]{2,1,0:T(4,128)}), f32[64,4,128]{2,1,0:T(4,128)S(1)}, u32[]{:S(2)}, u32[]{:S(2)}) async-start(f32[64,4,128]{2,1,0:T(4,128)} %bitcast.8), calls=%async_computation | async-start | bytes 262144 | tf_op jit(solution)/shard_map/all_to_all | solution.py:312
  35.2 2.4 %pack_rest.1 = (f32[48,8,256]{2,1,0:T(8,128)}, f32[14,8,4,256]{3,2,1,0:T(4,128)}, f32[14,8,4,256]{3,2,1,0:T(4,128)}) custom-call(f32[3,8,8,256]{3,2,1,0:T(8,128)} %vel.8, f32[3,8,8,256]{3,2,1,0:T(8,128)} %rhs.6, f32[3,3,8,8,256]{4,3,2,1,0:T(8,128)} %inv.6), custom_call_target="tpu_custom_call" | custom-call | tf_op jit(solution)/shard_map/pack_rest/pallas_call | solution.py:313
  37.6 0.0 copy-start.8
  37.6 11.5 %collective-permute-start.3 = (f32[48,8,256]{2,1,0:T(8,128)}, f32[48,8,256]{2,1,0:T(8,128)S(1)}, u32[]{:S(2)}, u32[]{:S(2)}) collective-permute-start(f32[48,8,256]{2,1,0:T(8,128)} %get-tuple-element.41), channel_id=1, source_target_pairs={{8,0},{16,8},{24,16},{32,24},{40,32},{48,40},{56,48},{64,56},{72,6... | collective-permute-start | bytes 1179656 | tf_op jit(solution)/shard_map/ppermute | solution.py:321
  49.0 0.0 collective-permute-done.2.halo.before
  49.1 0.0 all-to-all-done
  49.1 0.0 copy-done.3
  49.1 0.0 copy-done.8
  49.1 0.0 copy-start.9
  49.1 1.8 %modes.1 = f32[256,128]{1,0:T(8,128)} custom-call(f32[256,128]{1,0:T(8,128)S(1)} %bitcast.6, f32[8,8,512]{2,1,0:T(8,128)S(1)} %bitcast.7, bf16[1024,512]{1,0:T(8,128)(2,1)S(1)} %copy-done.3), custom_call_target="tpu_custom_call" | custom-call | tf_op jit(solution)/shard_map/modes/pallas_call | solution.py:326
  51.0 0.0 copy-start
  51.0 8.5 %all-to-all-start.1 = ((f32[64,4,128]{2,1,0:T(4,128)}), f32[64,4,128]{2,1,0:T(4,128)S(1)}, u32[]{:S(2)}, u32[]{:S(2)}) async-start(f32[64,4,128]{2,1,0:T(4,128)} %bitcast.3), calls=%async_computation.1 | async-start | bytes 262144 | tf_op jit(solution)/shard_map/all_to_all | solution.py:335
  59.4 7.6 %collective-permute-start.4 = (f32[14,8,4,256]{3,2,1,0:T(4,128)}, f32[14,8,4,256]{3,2,1,0:T(4,128)S(1)}, u32[]{:S(2)}, u32[]{:S(2)}) collective-permute-start(f32[14,8,4,256]{3,2,1,0:T(4,128)} %get-tuple-element.48), channel_id=1, source_target_pairs={{0,1},{1,2},{2,3},{3,4},{4,5},{5,6},{6,7},{8,9},{9,10},{10,11},{11... | collective-permute-start | bytes 1376264 | tf_op jit(solution)/shard_map/ppermute | solution.py:263
  67.1 0.0 copy-done.9
  67.1 1.9 %collective-permute-start.5 = (f32[14,8,4,256]{3,2,1,0:T(4,128)S(1)}, f32[14,8,4,256]{3,2,1,0:T(4,128)S(1)}, u32[]{:S(2)}, u32[]{:S(2)}) collective-permute-start(f32[14,8,4,256]{3,2,1,0:T(4,128)S(1)} %copy-done.9), channel_id=1, source_target_pairs={{1,0},{2,1},{3,2},{4,3},{5,4},{6,5},{7,6},{9,8},{10,9},{11,10},{12... | collective-permute-start | bytes 1376264 | tf_op jit(solution)/shard_map/ppermute | solution.py:263
  69.0 0.0 collective-permute-done.3.halo.after
  69.0 0.0 copy-start.7
  69.1 4.2 %all-to-all-done.1 = f32[64,4,128]{2,1,0:T(4,128)S(1)} async-done(((f32[64,4,128]{2,1,0:T(4,128)}), f32[64,4,128]{2,1,0:T(4,128)S(1)}, u32[]{:S(2)}, u32[]{:S(2)}) %all-to-all-start.1) | async-done | bytes 131104 | tf_op jit(solution)/shard_map/all_to_all | solution.py:335
  73.2 0.0 copy-start.1
  73.2 0.0 copy-start.2
  73.2 0.0 copy-start.5
  73.2 0.1 turn.1
  73.3 8.7 %collective-permute-start.6 = (f32[26,8,256]{2,1,0:T(8,128)S(1)}, f32[26,8,256]{2,1,0:T(8,128)S(1)}, u32[]{:S(2)}, u32[]{:S(2)}) collective-permute-start(f32[26,8,256]{2,1,0:T(8,128)S(1)} %get-tuple-element.50), channel_id=1, source_target_pairs={{0,1},{1,2},{2,3},{3,4},{4,5},{5,6},{6,7},{8,9},{9,10},{10,11},{11... | collective-permute-start | bytes 638984 | tf_op jit(solution)/shard_map/ppermute | solution.py:263
  82.1 1.9 %collective-permute-start.7 = (f32[26,8,256]{2,1,0:T(8,128)S(1)}, f32[26,8,256]{2,1,0:T(8,128)S(1)}, u32[]{:S(2)}, u32[]{:S(2)}) collective-permute-start(f32[26,8,256]{2,1,0:T(8,128)S(1)} %get-tuple-element.51), channel_id=1, source_target_pairs={{1,0},{2,1},{3,2},{4,3},{5,4},{6,5},{7,6},{9,8},{10,9},{11,10},{12... | collective-permute-start | bytes 638984 | tf_op jit(solution)/shard_map/ppermute | solution.py:263
  84.0 0.0 collective-permute-done.4.rad_low
  84.0 0.0 collective-permute-done.5.rad_high
  84.0 0.8 collective-permute-done.6.cor_low
  84.8 4.4 %collective-permute-done.7.cor_high = f32[26,8,256]{2,1,0:T(8,128)S(1)} collective-permute-done((f32[26,8,256]{2,1,0:T(8,128)S(1)}, f32[26,8,256]{2,1,0:T(8,128)S(1)}, u32[]{:S(2)}, u32[]{:S(2)}) %collective-permute-start.7) | collective-permute-done | bytes 213024 | tf_op jit(solution)/shard_map/ppermute | solution.py:263
  89.2 0.0 copy-done
  89.2 0.0 copy-done.7
  89.2 0.0 copy-done.1
  89.2 0.0 copy-done.2
  89.3 0.0 copy-done.5
  89.3 5.8 %sweeps.1 = (f32[3,8,8,256]{3,2,1,0:T(8,128)}, f32[8,8,256]{2,1,0:T(8,128)}) custom-call(f32[3,8,8,256]{3,2,1,0:T(8,128)S(1)} %copy-done.1, f32[3,8,8,256]{3,2,1,0:T(8,128)S(1)} %copy-done.2, f32[3,3,8,8,256]{4,3,2,1,0:T(8,128)S(1)} %copy-done, f32[128,256]{1,0:T(8,128)S(1)} %get-tuple-element.45.press, ...), custom_call_target="tpu_custom_call" | custom-call | tf_op jit(solution)/shard_map/sweeps/pallas_call | solution.py:350
  (2 shorter events, 0.1 us)
Async XLA Ops:
  2.5 12.0 %collective-permute-start = (f32[1,8,4,256]{3,2,1,0:T(4,128)}, f32[1,8,4,256]{3,2,1,0:T(4,128)S(1)}, u32[]{:S(2)}, u32[]{:S(2)}) collective-permute-start(f32[1,8,4,256]{3,2,1,0:T(4,128)} %get-tuple-element.27), channel_id=1, source_target_pairs={{0,1},{1,2},{2,3},{3,4},{4,5},{5,6},{6,7},{8,9},{9,10},{10,11},{11... | collective-permute-start | bytes 98312 | tf_op jit(solution)/shard_map/ppermute | solution.py:263
  7.9 6.6 %collective-permute-start.1 = (f32[1,8,4,256]{3,2,1,0:T(4,128)}, f32[1,8,4,256]{3,2,1,0:T(4,128)S(1)}, u32[]{:S(2)}, u32[]{:S(2)}) collective-permute-start(f32[1,8,4,256]{3,2,1,0:T(4,128)} %get-tuple-element.28), channel_id=1, source_target_pairs={{1,0},{2,1},{3,2},{4,3},{5,4},{6,5},{7,6},{9,8},{10,9},{11,10},{12... | collective-permute-start | bytes 98312 | tf_op jit(solution)/shard_map/ppermute | solution.py:263
  14.5 34.6 %copy-start.3 = (bf16[1024,512]{1,0:T(8,128)(2,1)S(1)}, bf16[1024,512]{1,0:T(8,128)(2,1)}, u32[]{:S(2)}) copy-start(bf16[1024,512]{1,0:T(8,128)(2,1)} %constant.2.clone.table) | copy-start | bytes 3145732
  14.5 8.6 %copy-start.4 = (f32[1,8,4,256]{3,2,1,0:T(4,128)}, f32[1,8,4,256]{3,2,1,0:T(4,128)S(1)}, u32[]{:S(2)}) copy-start(f32[1,8,4,256]{3,2,1,0:T(4,128)S(1)} %collective-permute-done.low) | copy-start | bytes 98308
  14.5 8.6 %copy-start.6 = (f32[1,8,4,256]{3,2,1,0:T(4,128)}, f32[1,8,4,256]{3,2,1,0:T(4,128)S(1)}, u32[]{:S(2)}) copy-start(f32[1,8,4,256]{3,2,1,0:T(4,128)S(1)} %collective-permute-done.1.high) | copy-start | bytes 98308
  14.5 34.5 %collective-permute-start.2 = (f32[48,8,256]{2,1,0:T(8,128)}, f32[48,8,256]{2,1,0:T(8,128)S(1)}, u32[]{:S(2)}, u32[]{:S(2)}) collective-permute-start(f32[48,8,256]{2,1,0:T(8,128)} %pack_forward.1), channel_id=1, source_target_pairs={{0,8},{8,16},{16,24},{24,32},{32,40},{40,48},{48,56},{56,64},{64,7... | collective-permute-start | bytes 1179656 | tf_op jit(solution)/shard_map/ppermute | solution.py:299
  24.9 24.2 %all-to-all-start = ((f32[64,4,128]{2,1,0:T(4,128)}), f32[64,4,128]{2,1,0:T(4,128)S(1)}, u32[]{:S(2)}, u32[]{:S(2)}) async-start(f32[64,4,128]{2,1,0:T(4,128)} %bitcast.8), calls=%async_computation | async-start | bytes 262144 | tf_op jit(solution)/shard_map/all_to_all | solution.py:312
  37.6 11.6 %copy-start.8 = (f32[512,8,8]{0,2,1:T(8,128)S(1)}, f32[512,8,8]{0,2,1:T(8,128)}, u32[]{:S(2)}) copy-start(f32[512,8,8]{0,2,1:T(8,128)} %param.7) | copy-start | bytes 393220
  37.6 31.4 %collective-permute-start.3 = (f32[48,8,256]{2,1,0:T(8,128)}, f32[48,8,256]{2,1,0:T(8,128)S(1)}, u32[]{:S(2)}, u32[]{:S(2)}) collective-permute-start(f32[48,8,256]{2,1,0:T(8,128)} %get-tuple-element.41), channel_id=1, source_target_pairs={{8,0},{16,8},{24,16},{32,24},{40,32},{48,40},{56,48},{64,56},{72,6... | collective-permute-start | bytes 1179656 | tf_op jit(solution)/shard_map/ppermute | solution.py:321
  49.1 17.9 %copy-start.9 = (f32[14,8,4,256]{3,2,1,0:T(4,128)S(1)}, f32[14,8,4,256]{3,2,1,0:T(4,128)}, u32[]{:S(2)}) copy-start(f32[14,8,4,256]{3,2,1,0:T(4,128)} %get-tuple-element.49) | copy-start | bytes 1376260
  51.0 38.3 %copy-start = (f32[3,3,8,8,256]{4,3,2,1,0:T(8,128)S(1)}, f32[3,3,8,8,256]{4,3,2,1,0:T(8,128)}, u32[]{:S(2)}) copy-start(f32[3,3,8,8,256]{4,3,2,1,0:T(8,128)} %inv.6) | copy-start | bytes 1769476
  51.0 22.3 %all-to-all-start.1 = ((f32[64,4,128]{2,1,0:T(4,128)}), f32[64,4,128]{2,1,0:T(4,128)S(1)}, u32[]{:S(2)}, u32[]{:S(2)}) async-start(f32[64,4,128]{2,1,0:T(4,128)} %bitcast.3), calls=%async_computation.1 | async-start | bytes 262144 | tf_op jit(solution)/shard_map/all_to_all | solution.py:335
  59.4 24.6 %collective-permute-start.4 = (f32[14,8,4,256]{3,2,1,0:T(4,128)}, f32[14,8,4,256]{3,2,1,0:T(4,128)S(1)}, u32[]{:S(2)}, u32[]{:S(2)}) collective-permute-start(f32[14,8,4,256]{3,2,1,0:T(4,128)} %get-tuple-element.48), channel_id=1, source_target_pairs={{0,1},{1,2},{2,3},{3,4},{4,5},{5,6},{6,7},{8,9},{9,10},{10,11},{11... | collective-permute-start | bytes 1376264 | tf_op jit(solution)/shard_map/ppermute | solution.py:263
  67.1 16.9 %collective-permute-start.5 = (f32[14,8,4,256]{3,2,1,0:T(4,128)S(1)}, f32[14,8,4,256]{3,2,1,0:T(4,128)S(1)}, u32[]{:S(2)}, u32[]{:S(2)}) collective-permute-start(f32[14,8,4,256]{3,2,1,0:T(4,128)S(1)} %copy-done.9), channel_id=1, source_target_pairs={{1,0},{2,1},{3,2},{4,3},{5,4},{6,5},{7,6},{9,8},{10,9},{11,10},{12... | collective-permute-start | bytes 1376264 | tf_op jit(solution)/shard_map/ppermute | solution.py:263
  69.0 20.2 %copy-start.7 = (f32[1,8,4,256]{3,2,1,0:T(4,128)S(1)}, f32[1,8,4,256]{3,2,1,0:T(4,128)}, u32[]{:S(2)}) copy-start(f32[1,8,4,256]{3,2,1,0:T(4,128)} %copy-done.6) | copy-start | bytes 98308
  73.2 16.0 %copy-start.1 = (f32[3,8,8,256]{3,2,1,0:T(8,128)S(1)}, f32[3,8,8,256]{3,2,1,0:T(8,128)}, u32[]{:S(2)}) copy-start(f32[3,8,8,256]{3,2,1,0:T(8,128)} %vel.8) | copy-start | bytes 589828
  73.2 16.0 %copy-start.2 = (f32[3,8,8,256]{3,2,1,0:T(8,128)S(1)}, f32[3,8,8,256]{3,2,1,0:T(8,128)}, u32[]{:S(2)}) copy-start(f32[3,8,8,256]{3,2,1,0:T(8,128)} %rhs.6) | copy-start | bytes 589828
  73.2 16.0 %copy-start.5 = (f32[1,8,4,256]{3,2,1,0:T(4,128)S(1)}, f32[1,8,4,256]{3,2,1,0:T(4,128)}, u32[]{:S(2)}) copy-start(f32[1,8,4,256]{3,2,1,0:T(4,128)} %copy-done.4) | copy-start | bytes 98308
  73.3 11.5 %collective-permute-start.6 = (f32[26,8,256]{2,1,0:T(8,128)S(1)}, f32[26,8,256]{2,1,0:T(8,128)S(1)}, u32[]{:S(2)}, u32[]{:S(2)}) collective-permute-start(f32[26,8,256]{2,1,0:T(8,128)S(1)} %get-tuple-element.50), channel_id=1, source_target_pairs={{0,1},{1,2},{2,3},{3,4},{4,5},{5,6},{6,7},{8,9},{9,10},{10,11},{11... | collective-permute-start | bytes 638984 | tf_op jit(solution)/shard_map/ppermute | solution.py:263
  82.1 7.2 %collective-permute-start.7 = (f32[26,8,256]{2,1,0:T(8,128)S(1)}, f32[26,8,256]{2,1,0:T(8,128)S(1)}, u32[]{:S(2)}, u32[]{:S(2)}) collective-permute-start(f32[26,8,256]{2,1,0:T(8,128)S(1)} %get-tuple-element.51), channel_id=1, source_target_pairs={{1,0},{2,1},{3,2},{4,3},{5,4},{6,5},{7,6},{9,8},{10,9},{11,10},{12... | collective-permute-start | bytes 638984 | tf_op jit(solution)/shard_map/ppermute | solution.py:263

commit v3 on v2

--- a/solution.py
+++ b/solution.py
@@ -10,7 +10,6 @@
 from jax.sharding import PartitionSpec as P
 
 SWEEPS = 4
-FIRST = (13,)
 BULK = tuple(range(13)) + (14,)
 coupling = 0.5
 NP, CR, NZ = 512, 8, 256
@@ -49,13 +48,14 @@
     return jnp.where(lane == (NZ - 1 if step > 0 else 0), 0.0, moved)
 
 
-def rows_of(vel, rhs, inv, f):
-    return inv.at[f // 3, f % 3] if f < 9 else rhs.at[f - 9] if f < 12 else vel.at[f - 12]
-
-
-def pack_rows(fields, vel, rhs, inv, up, down):
-    for n, f in enumerate(fields):
-        src = rows_of(vel, rhs, inv, f)
+def pack_first(v1, up, down):
+    up[0] = v1[0, :, 4:8, :]
+    down[0] = v1[0, :, 0:4, :]
+
+
+def pack_rows(vel, rhs, inv, up, down):
+    for n, f in enumerate(BULK):
+        src = inv.at[f // 3, f % 3] if f < 9 else rhs.at[f - 9] if f < 12 else vel.at[f - 12]
         up[n] = src[:, 4:8, :]
         down[n] = src[:, 0:4, :]
 
@@ -154,7 +154,7 @@
     for c in range(3):
         bwd[27 + 3 * c : 30 + 3 * c] = rhs[c, 0:3]
         bwd[36 + 4 * c : 40 + 4 * c] = vel[c, 0:4]
-    pack_rows(BULK, vel, rhs, inv, up, down)
+    pack_rows(vel, rhs, inv, up, down)
 
 
 def corner_kernel(side, halo, up, down):
@@ -185,7 +185,7 @@
 
 
 def beyond(f, first, bulk):
-    return first[FIRST.index(f)] if f in FIRST else bulk[BULK.index(f)]
+    return bulk[BULK.index(f)] if f in BULK else first[0]
 
 
 def sweep_kernel(vel, rhs, inv, press, before, after, low, high, rad_low, rad_high, cor_low, cor_high,
@@ -249,8 +249,7 @@
                 eu[later, c, j + 1] = new
 
     for sweep in range(SWEEPS):
-        @pl.loop(sweep, 14 - sweep)
-        def _(j, sweep=sweep):
+        for j in range(sweep, 14 - sweep):
             line_step(sweep, j)
 
 
@@ -277,13 +276,14 @@
 def on_device(vel, rhs_mom, mode_inv, sweep_inv):
     table = jnp.asarray(cas_tables())
     up, down = pl.pallas_call(
-        functools.partial(pack_rows, FIRST),
-        in_specs=[VMEM] * 3,
-        out_specs=[VMEM] * 2,
-        out_shape=[shape(len(FIRST), LINES, 4, NZ)] * 2,
+        pack_first,
+        grid=(1,),
+        in_specs=[pl.BlockSpec((1, LINES, CR, NZ), lambda i: (1, 0, 0, 0))],
+        out_specs=[pl.BlockSpec((1, LINES, 4, NZ), lambda i: (0, 0, 0, 0))] * 2,
+        out_shape=[shape(1, LINES, 4, NZ)] * 2,
         compiler_params=params(60),
         name="pack_first",
-    )(vel, rhs_mom, sweep_inv)
+    )(vel)
     low, high = both_ways(up, down, "radial", False)
     fwd = pl.pallas_call(
         pack_forward,
@@ -301,7 +301,7 @@
         div_kernel,
         grid=(1,),
         in_specs=[pl.BlockSpec((3, LINES, CR, NZ), lambda i: (0, 0, 0, 0))]
-        + [pl.BlockSpec((1, LINES, 4, NZ), lambda i: (FIRST.index(13), 0, 0, 0))] * 2,
+        + [pl.BlockSpec((1, LINES, 4, NZ), lambda i: (0, 0, 0, 0))] * 2,
         out_specs=pl.BlockSpec((NZ, 128), lambda i: (0, 0)),
         out_shape=shape(NZ, 128),
         compiler_params=params(60),

time: 95.6 us -> 92.3 us (0.965)
  Pallas kernels: 15.7 us -> 12.4 us
    pallas_call x1, Pallas kernels: 5.81 us -> 2.87 us  [on_device(): pl.pallas_call(sweep_kernel, in_specs=[VMEM] * 12, out_specs=[VMEM] * 2,...]
  transfers between devices with their start and end apart: 10 -> 10, of which waited for: 3 -> 3; matrix products, arithmetic and copies ran while one was open for 0% -> 0% of each run, Pallas kernels for 8% -> 9%
where the time goes in v3:
time: 92.3 us; the launch traced here: 91.7 us
  starting transfers between devices  69 us (75%)
  Pallas kernels  12.4 us (13%)
  waiting for transfers between devices  9.4 us (10%)
    ppermute x6, starting transfers between devices, both_ways(): return (lax.ppermute(up, axis, forward), lax.ppermute(down, axis, backward))  30.2 us
    all_to_all x2, starting transfers between devices, on_device(): got = lax.all_to_all(sent, 'pitch', split_axis=0, concat_axis=0, tiled=True)  18.8 us
    ppermute x1, starting transfers between devices, on_device(): lax.ppermute(bwd, 'pitch', [((i + 1) % BLOCKS, i) for i in range(BLOCKS)])  11.5 us
    ppermute x1, starting transfers between devices, on_device(): lax.ppermute(fwd, 'pitch', [(i, (i + 1) % BLOCKS) for i in range(BLOCKS)])  8.56 us
    ppermute x6, waiting for transfers between devices, both_ways(): return (lax.ppermute(up, axis, forward), lax.ppermute(down, axis, backward))  5.23 us
    all_to_all x2, waiting for transfers between devices, on_device(): got = lax.all_to_all(sent, 'pitch', split_axis=0, concat_axis=0, tiled=True)  4.17 us
    pallas_call x1, Pallas kernels, on_device(): pl.pallas_call(sweep_kernel, in_specs=[VMEM] * 12, out_specs=[VMEM] * 2,...  2.87 us
    pallas_call x1, Pallas kernels, on_device(): pl.pallas_call(pack_rest, in_specs=[VMEM] * 3, out_specs=[VMEM] * 3, out_...  2.35 us
  transfers between devices with their start and end apart: 10, of which 3 were waited for; matrix products, arithmetic and copies ran while one was open for 0% of the time, Pallas kernels for 9%

profile of v3, /device:TPU:1, one launch (start us, length us, event | category | flops | bytes accessed | tf_op | source)
XLA Modules:
  0.0 91.7 jit_solution(18166713708737562318)
XLA Ops:
  0.6 1.5 %pack_first.1 = (f32[1,8,4,256]{3,2,1,0:T(4,128)}, f32[1,8,4,256]{3,2,1,0:T(4,128)}) custom-call(f32[3,8,8,256]{3,2,1,0:T(8,128)} %vel.6), custom_call_target="tpu_custom_call" | custom-call | tf_op jit(solution)/shard_map/pack_first/pallas_call | solution.py:278
  2.1 5.4 %collective-permute-start = (f32[1,8,4,256]{3,2,1,0:T(4,128)}, f32[1,8,4,256]{3,2,1,0:T(4,128)S(1)}, u32[]{:S(2)}, u32[]{:S(2)}) collective-permute-start(f32[1,8,4,256]{3,2,1,0:T(4,128)} %get-tuple-element.27), channel_id=1, source_target_pairs={{0,1},{1,2},{2,3},{3,4},{4,5},{5,6},{6,7},{8,9},{9,10},{10,11},{11... | collective-permute-start | bytes 98312 | tf_op jit(solution)/shard_map/ppermute | solution.py:262
  7.5 4.7 %collective-permute-start.1 = (f32[1,8,4,256]{3,2,1,0:T(4,128)}, f32[1,8,4,256]{3,2,1,0:T(4,128)S(1)}, u32[]{:S(2)}, u32[]{:S(2)}) collective-permute-start(f32[1,8,4,256]{3,2,1,0:T(4,128)} %get-tuple-element.28), channel_id=1, source_target_pairs={{1,0},{2,1},{3,2},{4,3},{5,4},{6,5},{7,6},{9,8},{10,9},{11,10},{12... | collective-permute-start | bytes 98312 | tf_op jit(solution)/shard_map/ppermute | solution.py:262
  12.2 1.9 %pack_forward.1 = f32[48,8,256]{2,1,0:T(8,128)} custom-call(f32[3,8,8,256]{3,2,1,0:T(8,128)} %vel.6, f32[3,8,8,256]{3,2,1,0:T(8,128)} %rhs.4, f32[3,3,8,8,256]{4,3,2,1,0:T(8,128)} %inv.4), custom_call_target="tpu_custom_call" | custom-call | tf_op jit(solution)/shard_map/pack_forward/pallas_call | solution.py:288
  14.1 0.0 copy-start.3
  14.1 0.0 collective-permute-done.low
  14.1 0.0 copy-start.4
  14.1 0.0 collective-permute-done.1.high
  14.1 0.0 copy-start.6
  14.1 8.6 %collective-permute-start.2 = (f32[48,8,256]{2,1,0:T(8,128)}, f32[48,8,256]{2,1,0:T(8,128)S(1)}, u32[]{:S(2)}, u32[]{:S(2)}) collective-permute-start(f32[48,8,256]{2,1,0:T(8,128)} %pack_forward.1), channel_id=1, source_target_pairs={{0,8},{8,16},{16,24},{24,32},{32,40},{40,48},{48,56},{56,64},{64,7... | collective-permute-start | bytes 1179656 | tf_op jit(solution)/shard_map/ppermute | solution.py:299
  22.7 0.0 copy-done.4
  22.7 0.0 copy-done.6
  22.7 1.8 %divergence.1 = f32[256,128]{1,0:T(8,128)} custom-call(f32[3,8,8,256]{3,2,1,0:T(8,128)} %vel.6, f32[1,8,4,256]{3,2,1,0:T(4,128)} %copy-done.4, f32[1,8,4,256]{3,2,1,0:T(4,128)} %copy-done.6), custom_call_target="tpu_custom_call" | custom-call | tf_op jit(solution)/shard_map/divergence/pallas_call | solution.py:300
  24.5 10.3 %all-to-all-start = ((f32[64,4,128]{2,1,0:T(4,128)}), f32[64,4,128]{2,1,0:T(4,128)S(1)}, u32[]{:S(2)}, u32[]{:S(2)}) async-start(f32[64,4,128]{2,1,0:T(4,128)} %bitcast.8), calls=%async_computation | async-start | bytes 262144 | tf_op jit(solution)/shard_map/all_to_all | solution.py:312
  34.8 2.4 %pack_rest.1 = (f32[48,8,256]{2,1,0:T(8,128)}, f32[14,8,4,256]{3,2,1,0:T(4,128)}, f32[14,8,4,256]{3,2,1,0:T(4,128)}) custom-call(f32[3,8,8,256]{3,2,1,0:T(8,128)} %vel.6, f32[3,8,8,256]{3,2,1,0:T(8,128)} %rhs.4, f32[3,3,8,8,256]{4,3,2,1,0:T(8,128)} %inv.4), custom_call_target="tpu_custom_call" | custom-call | tf_op jit(solution)/shard_map/pack_rest/pallas_call | solution.py:313
  37.1 0.0 copy-start.8
  37.1 11.5 %collective-permute-start.3 = (f32[48,8,256]{2,1,0:T(8,128)}, f32[48,8,256]{2,1,0:T(8,128)S(1)}, u32[]{:S(2)}, u32[]{:S(2)}) collective-permute-start(f32[48,8,256]{2,1,0:T(8,128)} %get-tuple-element.41), channel_id=1, source_target_pairs={{8,0},{16,8},{24,16},{32,24},{40,32},{48,40},{56,48},{64,56},{72,6... | collective-permute-start | bytes 1179656 | tf_op jit(solution)/shard_map/ppermute | solution.py:321
  48.6 0.0 collective-permute-done.2.halo.before
  48.7 0.0 all-to-all-done
  48.7 0.0 copy-done.3
  48.7 0.0 copy-done.8
  48.7 0.0 copy-start.9
  48.7 1.8 %modes.1 = f32[256,128]{1,0:T(8,128)} custom-call(f32[256,128]{1,0:T(8,128)S(1)} %bitcast.6, f32[8,8,512]{2,1,0:T(8,128)S(1)} %bitcast.7, bf16[1024,512]{1,0:T(8,128)(2,1)S(1)} %copy-done.3), custom_call_target="tpu_custom_call" | custom-call | tf_op jit(solution)/shard_map/modes/pallas_call | solution.py:326
  50.5 0.0 copy-start
  50.5 8.5 %all-to-all-start.1 = ((f32[64,4,128]{2,1,0:T(4,128)}), f32[64,4,128]{2,1,0:T(4,128)S(1)}, u32[]{:S(2)}, u32[]{:S(2)}) async-start(f32[64,4,128]{2,1,0:T(4,128)} %bitcast.3), calls=%async_computation.1 | async-start | bytes 262144 | tf_op jit(solution)/shard_map/all_to_all | solution.py:335
  59.0 7.6 %collective-permute-start.4 = (f32[14,8,4,256]{3,2,1,0:T(4,128)}, f32[14,8,4,256]{3,2,1,0:T(4,128)S(1)}, u32[]{:S(2)}, u32[]{:S(2)}) collective-permute-start(f32[14,8,4,256]{3,2,1,0:T(4,128)} %get-tuple-element.48), channel_id=1, source_target_pairs={{0,1},{1,2},{2,3},{3,4},{4,5},{5,6},{6,7},{8,9},{9,10},{10,11},{11... | collective-permute-start | bytes 1376264 | tf_op jit(solution)/shard_map/ppermute | solution.py:262
  66.6 0.0 copy-done.9
  66.6 1.9 %collective-permute-start.5 = (f32[14,8,4,256]{3,2,1,0:T(4,128)S(1)}, f32[14,8,4,256]{3,2,1,0:T(4,128)S(1)}, u32[]{:S(2)}, u32[]{:S(2)}) collective-permute-start(f32[14,8,4,256]{3,2,1,0:T(4,128)S(1)} %copy-done.9), channel_id=1, source_target_pairs={{1,0},{2,1},{3,2},{4,3},{5,4},{6,5},{7,6},{9,8},{10,9},{11,10},{12... | collective-permute-start | bytes 1376264 | tf_op jit(solution)/shard_map/ppermute | solution.py:262
  68.6 0.0 collective-permute-done.3.halo.after
  68.6 0.0 copy-start.7
  68.6 4.2 %all-to-all-done.1 = f32[64,4,128]{2,1,0:T(4,128)S(1)} async-done(((f32[64,4,128]{2,1,0:T(4,128)}), f32[64,4,128]{2,1,0:T(4,128)S(1)}, u32[]{:S(2)}, u32[]{:S(2)}) %all-to-all-start.1) | async-done | bytes 131104 | tf_op jit(solution)/shard_map/all_to_all | solution.py:335
  72.8 0.0 copy-start.1
  72.8 0.0 copy-start.2
  72.8 0.0 copy-start.5
  72.8 0.1 turn.1
  72.9 8.7 %collective-permute-start.6 = (f32[26,8,256]{2,1,0:T(8,128)S(1)}, f32[26,8,256]{2,1,0:T(8,128)S(1)}, u32[]{:S(2)}, u32[]{:S(2)}) collective-permute-start(f32[26,8,256]{2,1,0:T(8,128)S(1)} %get-tuple-element.50), channel_id=1, source_target_pairs={{0,1},{1,2},{2,3},{3,4},{4,5},{5,6},{6,7},{8,9},{9,10},{10,11},{11... | collective-permute-start | bytes 638984 | tf_op jit(solution)/shard_map/ppermute | solution.py:262
  81.6 1.9 %collective-permute-start.7 = (f32[26,8,256]{2,1,0:T(8,128)S(1)}, f32[26,8,256]{2,1,0:T(8,128)S(1)}, u32[]{:S(2)}, u32[]{:S(2)}) collective-permute-start(f32[26,8,256]{2,1,0:T(8,128)S(1)} %get-tuple-element.51), channel_id=1, source_target_pairs={{1,0},{2,1},{3,2},{4,3},{5,4},{6,5},{7,6},{9,8},{10,9},{11,10},{12... | collective-permute-start | bytes 638984 | tf_op jit(solution)/shard_map/ppermute | solution.py:262
  83.6 0.0 collective-permute-done.4.rad_low
  83.6 0.0 collective-permute-done.5.rad_high
  83.6 0.8 collective-permute-done.6.cor_low
  84.4 4.4 %collective-permute-done.7.cor_high = f32[26,8,256]{2,1,0:T(8,128)S(1)} collective-permute-done((f32[26,8,256]{2,1,0:T(8,128)S(1)}, f32[26,8,256]{2,1,0:T(8,128)S(1)}, u32[]{:S(2)}, u32[]{:S(2)}) %collective-permute-start.7) | collective-permute-done | bytes 213024 | tf_op jit(solution)/shard_map/ppermute | solution.py:262
  88.8 0.0 copy-done
  88.8 0.0 copy-done.7
  88.8 0.0 copy-done.1
  88.8 0.0 copy-done.2
  88.8 0.0 copy-done.5
  88.8 2.9 %sweeps.1 = (f32[3,8,8,256]{3,2,1,0:T(8,128)}, f32[8,8,256]{2,1,0:T(8,128)}) custom-call(f32[3,8,8,256]{3,2,1,0:T(8,128)S(1)} %copy-done.1, f32[3,8,8,256]{3,2,1,0:T(8,128)S(1)} %copy-done.2, f32[3,3,8,8,256]{4,3,2,1,0:T(8,128)S(1)} %copy-done, f32[128,256]{1,0:T(8,128)S(1)} %get-tuple-element.45.press, ...), custom_call_target="tpu_custom_call" | custom-call | tf_op jit(solution)/shard_map/sweeps/pallas_call | solution.py:350
  (2 shorter events, 0.1 us)
Async XLA Ops:
  2.1 12.0 %collective-permute-start = (f32[1,8,4,256]{3,2,1,0:T(4,128)}, f32[1,8,4,256]{3,2,1,0:T(4,128)S(1)}, u32[]{:S(2)}, u32[]{:S(2)}) collective-permute-start(f32[1,8,4,256]{3,2,1,0:T(4,128)} %get-tuple-element.27), channel_id=1, source_target_pairs={{0,1},{1,2},{2,3},{3,4},{4,5},{5,6},{6,7},{8,9},{9,10},{10,11},{11... | collective-permute-start | bytes 98312 | tf_op jit(solution)/shard_map/ppermute | solution.py:262
  7.5 6.6 %collective-permute-start.1 = (f32[1,8,4,256]{3,2,1,0:T(4,128)}, f32[1,8,4,256]{3,2,1,0:T(4,128)S(1)}, u32[]{:S(2)}, u32[]{:S(2)}) collective-permute-start(f32[1,8,4,256]{3,2,1,0:T(4,128)} %get-tuple-element.28), channel_id=1, source_target_pairs={{1,0},{2,1},{3,2},{4,3},{5,4},{6,5},{7,6},{9,8},{10,9},{11,10},{12... | collective-permute-start | bytes 98312 | tf_op jit(solution)/shard_map/ppermute | solution.py:262
  14.1 34.6 %copy-start.3 = (bf16[1024,512]{1,0:T(8,128)(2,1)S(1)}, bf16[1024,512]{1,0:T(8,128)(2,1)}, u32[]{:S(2)}) copy-start(bf16[1024,512]{1,0:T(8,128)(2,1)} %constant.2.clone.table) | copy-start | bytes 3145732
  14.1 8.6 %copy-start.4 = (f32[1,8,4,256]{3,2,1,0:T(4,128)}, f32[1,8,4,256]{3,2,1,0:T(4,128)S(1)}, u32[]{:S(2)}) copy-start(f32[1,8,4,256]{3,2,1,0:T(4,128)S(1)} %collective-permute-done.low) | copy-start | bytes 98308
  14.1 8.6 %copy-start.6 = (f32[1,8,4,256]{3,2,1,0:T(4,128)}, f32[1,8,4,256]{3,2,1,0:T(4,128)S(1)}, u32[]{:S(2)}) copy-start(f32[1,8,4,256]{3,2,1,0:T(4,128)S(1)} %collective-permute-done.1.high) | copy-start | bytes 98308
  14.1 34.5 %collective-permute-start.2 = (f32[48,8,256]{2,1,0:T(8,128)}, f32[48,8,256]{2,1,0:T(8,128)S(1)}, u32[]{:S(2)}, u32[]{:S(2)}) collective-permute-start(f32[48,8,256]{2,1,0:T(8,128)} %pack_forward.1), channel_id=1, source_target_pairs={{0,8},{8,16},{16,24},{24,32},{32,40},{40,48},{48,56},{56,64},{64,7... | collective-permute-start | bytes 1179656 | tf_op jit(solution)/shard_map/ppermute | solution.py:299
  24.5 24.2 %all-to-all-start = ((f32[64,4,128]{2,1,0:T(4,128)}), f32[64,4,128]{2,1,0:T(4,128)S(1)}, u32[]{:S(2)}, u32[]{:S(2)}) async-start(f32[64,4,128]{2,1,0:T(4,128)} %bitcast.8), calls=%async_computation | async-start | bytes 262144 | tf_op jit(solution)/shard_map/all_to_all | solution.py:312
  37.1 11.6 %copy-start.8 = (f32[512,8,8]{0,2,1:T(8,128)S(1)}, f32[512,8,8]{0,2,1:T(8,128)}, u32[]{:S(2)}) copy-start(f32[512,8,8]{0,2,1:T(8,128)} %param.7) | copy-start | bytes 393220
  37.1 31.4 %collective-permute-start.3 = (f32[48,8,256]{2,1,0:T(8,128)}, f32[48,8,256]{2,1,0:T(8,128)S(1)}, u32[]{:S(2)}, u32[]{:S(2)}) collective-permute-start(f32[48,8,256]{2,1,0:T(8,128)} %get-tuple-element.41), channel_id=1, source_target_pairs={{8,0},{16,8},{24,16},{32,24},{40,32},{48,40},{56,48},{64,56},{72,6... | collective-permute-start | bytes 1179656 | tf_op jit(solution)/shard_map/ppermute | solution.py:321
  48.7 17.9 %copy-start.9 = (f32[14,8,4,256]{3,2,1,0:T(4,128)S(1)}, f32[14,8,4,256]{3,2,1,0:T(4,128)}, u32[]{:S(2)}) copy-start(f32[14,8,4,256]{3,2,1,0:T(4,128)} %get-tuple-element.49) | copy-start | bytes 1376260
  50.5 38.3 %copy-start = (f32[3,3,8,8,256]{4,3,2,1,0:T(8,128)S(1)}, f32[3,3,8,8,256]{4,3,2,1,0:T(8,128)}, u32[]{:S(2)}) copy-start(f32[3,3,8,8,256]{4,3,2,1,0:T(8,128)} %inv.4) | copy-start | bytes 1769476
  50.5 22.3 %all-to-all-start.1 = ((f32[64,4,128]{2,1,0:T(4,128)}), f32[64,4,128]{2,1,0:T(4,128)S(1)}, u32[]{:S(2)}, u32[]{:S(2)}) async-start(f32[64,4,128]{2,1,0:T(4,128)} %bitcast.3), calls=%async_computation.1 | async-start | bytes 262144 | tf_op jit(solution)/shard_map/all_to_all | solution.py:335
  59.0 24.6 %collective-permute-start.4 = (f32[14,8,4,256]{3,2,1,0:T(4,128)}, f32[14,8,4,256]{3,2,1,0:T(4,128)S(1)}, u32[]{:S(2)}, u32[]{:S(2)}) collective-permute-start(f32[14,8,4,256]{3,2,1,0:T(4,128)} %get-tuple-element.48), channel_id=1, source_target_pairs={{0,1},{1,2},{2,3},{3,4},{4,5},{5,6},{6,7},{8,9},{9,10},{10,11},{11... | collective-permute-start | bytes 1376264 | tf_op jit(solution)/shard_map/ppermute | solution.py:262
  66.6 16.9 %collective-permute-start.5 = (f32[14,8,4,256]{3,2,1,0:T(4,128)S(1)}, f32[14,8,4,256]{3,2,1,0:T(4,128)S(1)}, u32[]{:S(2)}, u32[]{:S(2)}) collective-permute-start(f32[14,8,4,256]{3,2,1,0:T(4,128)S(1)} %copy-done.9), channel_id=1, source_target_pairs={{1,0},{2,1},{3,2},{4,3},{5,4},{6,5},{7,6},{9,8},{10,9},{11,10},{12... | collective-permute-start | bytes 1376264 | tf_op jit(solution)/shard_map/ppermute | solution.py:262
  68.6 20.2 %copy-start.7 = (f32[1,8,4,256]{3,2,1,0:T(4,128)S(1)}, f32[1,8,4,256]{3,2,1,0:T(4,128)}, u32[]{:S(2)}) copy-start(f32[1,8,4,256]{3,2,1,0:T(4,128)} %copy-done.6) | copy-start | bytes 98308
  72.8 16.0 %copy-start.1 = (f32[3,8,8,256]{3,2,1,0:T(8,128)S(1)}, f32[3,8,8,256]{3,2,1,0:T(8,128)}, u32[]{:S(2)}) copy-start(f32[3,8,8,256]{3,2,1,0:T(8,128)} %vel.6) | copy-start | bytes 589828
  72.8 16.0 %copy-start.2 = (f32[3,8,8,256]{3,2,1,0:T(8,128)S(1)}, f32[3,8,8,256]{3,2,1,0:T(8,128)}, u32[]{:S(2)}) copy-start(f32[3,8,8,256]{3,2,1,0:T(8,128)} %rhs.4) | copy-start | bytes 589828
  72.8 16.0 %copy-start.5 = (f32[1,8,4,256]{3,2,1,0:T(4,128)S(1)}, f32[1,8,4,256]{3,2,1,0:T(4,128)}, u32[]{:S(2)}) copy-start(f32[1,8,4,256]{3,2,1,0:T(4,128)} %copy-done.4) | copy-start | bytes 98308
  72.9 11.5 %collective-permute-start.6 = (f32[26,8,256]{2,1,0:T(8,128)S(1)}, f32[26,8,256]{2,1,0:T(8,128)S(1)}, u32[]{:S(2)}, u32[]{:S(2)}) collective-permute-start(f32[26,8,256]{2,1,0:T(8,128)S(1)} %get-tuple-element.50), channel_id=1, source_target_pairs={{0,1},{1,2},{2,3},{3,4},{4,5},{5,6},{6,7},{8,9},{9,10},{10,11},{11... | collective-permute-start | bytes 638984 | tf_op jit(solution)/shard_map/ppermute | solution.py:262
  81.6 7.2 %collective-permute-start.7 = (f32[26,8,256]{2,1,0:T(8,128)S(1)}, f32[26,8,256]{2,1,0:T(8,128)S(1)}, u32[]{:S(2)}, u32[]{:S(2)}) collective-permute-start(f32[26,8,256]{2,1,0:T(8,128)S(1)} %get-tuple-element.51), channel_id=1, source_target_pairs={{1,0},{2,1},{3,2},{4,3},{5,4},{6,5},{7,6},{9,8},{10,9},{11,10},{12... | collective-permute-start | bytes 638984 | tf_op jit(solution)/shard_map/ppermute | solution.py:262

commit v4 on v3

--- a/solution.py
+++ b/solution.py
@@ -144,16 +144,18 @@
     for f in range(9):
         fwd[3 * f : 3 * f + 3] = inv[f // 3, f % 3, 1:4]
     for c in range(3):
-        fwd[27 + 3 * c : 30 + 3 * c] = rhs[c, 1:4]
-        fwd[36 + 4 * c : 40 + 4 * c] = vel[c]
+        fwd[27 + 3 * c] = rhs[c, 1] + coupling * vel[c, 0]
+        fwd[28 + 3 * c : 30 + 3 * c] = rhs[c, 2:4]
+        fwd[36 + 3 * c : 39 + 3 * c] = vel[c, 1:4]
 
 
 def pack_rest(vel, rhs, inv, bwd, up, down):
     for f in range(9):
         bwd[3 * f : 3 * f + 3] = inv[f // 3, f % 3, 0:3]
     for c in range(3):
-        bwd[27 + 3 * c : 30 + 3 * c] = rhs[c, 0:3]
-        bwd[36 + 4 * c : 40 + 4 * c] = vel[c, 0:4]
+        bwd[27 + 3 * c : 29 + 3 * c] = rhs[c, 0:2]
+        bwd[29 + 3 * c] = rhs[c, 2] + coupling * vel[c, 3]
+        bwd[36 + 3 * c : 39 + 3 * c] = vel[c, 0:3]
     pack_rows(vel, rhs, inv, up, down)
 
 
@@ -165,10 +167,10 @@
                 src = halo[3 * f + n + 1 - side]
                 out[f // 2, 4 * (f % 2) + 2 * n : 4 * (f % 2) + 2 * n + 2, :] = src[two : two + 2]
         for c in range(3):
-            g = 36 + 4 * c
-            out[6 + c, 0:4, :] = halo[g + 3 - 3 * side, first : first + 4, :]
+            g = 36 + 3 * c
+            out[6 + c, 0:4, :] = halo[g + 2 - 2 * side, first : first + 4, :]
             for n in range(2):
-                src = halo[g + 1 + n]
+                src = halo[g + n + side]
                 out[6 + c, 4 + 2 * n : 6 + 2 * n, :] = src[two : two + 2]
 
 
@@ -212,12 +214,13 @@
             dst[line, 12:14, :] = cor_high[t, r : r + 2, :]
     for c in range(3):
         dst = eu.at[0, c]
-        g = 36 + 4 * c
+        g = 36 + 3 * c
         dst[4:12, 4:12, :] = vel[c]
         dst[4:12, 0:4, :] = beyond(12 + c, low, rad_low)
         dst[4:12, 12:16, :] = beyond(12 + c, high, rad_high)
-        dst[0:4, 4:12, :] = before[g : g + 4]
-        dst[12:16, 4:12, :] = after[g : g + 4]
+        dst[1:4, 4:12, :] = before[g : g + 3]
+        dst[12:15, 4:12, :] = after[g : g + 3]
+        dst[0, 4:12, :] = dst[15, 4:12, :] = jnp.zeros((CR, NZ), F32)
         for n, line in enumerate((3, 12)):
             t = 14 + 9 * n + c
             dst[line, 0:4, :] = cor_low[t, 0:4, :]
@@ -290,8 +293,8 @@
         grid=(1,),
         in_specs=[pl.BlockSpec((3, 4, CR, NZ), lambda i: (0, 1, 0, 0))] * 2
         + [pl.BlockSpec((3, 3, 4, CR, NZ), lambda i: (0, 0, 1, 0, 0))],
-        out_specs=pl.BlockSpec((48, CR, NZ), lambda i: (0, 0, 0)),
-        out_shape=shape(48, CR, NZ),
+        out_specs=pl.BlockSpec((45, CR, NZ), lambda i: (0, 0, 0)),
+        out_shape=shape(45, CR, NZ),
         compiler_params=params(60),
         name="pack_forward",
     )(vel, rhs_mom, sweep_inv)
@@ -314,7 +317,7 @@
         pack_rest,
         in_specs=[VMEM] * 3,
         out_specs=[VMEM] * 3,
-        out_shape=[shape(48, CR, NZ)] + [shape(len(BULK), LINES, 4, NZ)] * 2,
+        out_shape=[shape(45, CR, NZ)] + [shape(len(BULK), LINES, 4, NZ)] * 2,
         compiler_params=params(60),
         name="pack_rest",
     )(vel_b, rhs_b, inv_b)

time: 92.3 us -> 91.2 us (0.988)
    all_to_all x2, starting transfers between devices: 18.8 us -> 17 us  [on_device(): got = lax.all_to_all(sent, 'pitch', split_axis=0, concat_axis=0, tiled=True)]
    ppermute x6, starting transfers between devices: 30.2 us -> 31.7 us  [both_ways(): return (lax.ppermute(up, axis, forward), lax.ppermute(down, axis, backward))]
where the time goes in v4:
time: 91.2 us; the launch traced here: 90.6 us
  starting transfers between devices  68.8 us (75%)
  Pallas kernels  12.4 us (14%)
  waiting for transfers between devices  8.52 us (9%)
    ppermute x6, starting transfers between devices, both_ways(): return (lax.ppermute(up, axis, forward), lax.ppermute(down, axis, backward))  31.7 us
    all_to_all x2, starting transfers between devices, on_device(): got = lax.all_to_all(sent, 'pitch', split_axis=0, concat_axis=0, tiled=True)  17 us
    ppermute x1, starting transfers between devices, on_device(): lax.ppermute(bwd, 'pitch', [((i + 1) % BLOCKS, i) for i in range(BLOCKS)])  11.5 us
    ppermute x1, starting transfers between devices, on_device(): lax.ppermute(fwd, 'pitch', [(i, (i + 1) % BLOCKS) for i in range(BLOCKS)])  8.59 us
    ppermute x6, waiting for transfers between devices, both_ways(): return (lax.ppermute(up, axis, forward), lax.ppermute(down, axis, backward))  5.23 us
    all_to_all x2, waiting for transfers between devices, on_device(): got = lax.all_to_all(sent, 'pitch', split_axis=0, concat_axis=0, tiled=True)  3.29 us
    pallas_call x1, Pallas kernels, on_device(): pl.pallas_call(sweep_kernel, in_specs=[VMEM] * 12, out_specs=[VMEM] * 2,...  2.87 us
    pallas_call x1, Pallas kernels, on_device(): pl.pallas_call(pack_rest, in_specs=[VMEM] * 3, out_specs=[VMEM] * 3, out_...  2.4 us
  transfers between devices with their start and end apart: 10, of which 3 were waited for; matrix products, arithmetic and copies ran while one was open for 0% of the time, Pallas kernels for 9%

profile of v4, /device:TPU:1, one launch (start us, length us, event | category | flops | bytes accessed | tf_op | source)
XLA Modules:
  0.0 90.6 jit_solution(17063877501476352297)
XLA Ops:
  0.6 1.5 %pack_first.1 = (f32[1,8,4,256]{3,2,1,0:T(4,128)}, f32[1,8,4,256]{3,2,1,0:T(4,128)}) custom-call(f32[3,8,8,256]{3,2,1,0:T(8,128)} %vel.6), custom_call_target="tpu_custom_call" | custom-call | tf_op jit(solution)/shard_map/pack_first/pallas_call | solution.py:281
  2.1 5.4 %collective-permute-start = (f32[1,8,4,256]{3,2,1,0:T(4,128)}, f32[1,8,4,256]{3,2,1,0:T(4,128)S(1)}, u32[]{:S(2)}, u32[]{:S(2)}) collective-permute-start(f32[1,8,4,256]{3,2,1,0:T(4,128)} %get-tuple-element.27), channel_id=1, source_target_pairs={{0,1},{1,2},{2,3},{3,4},{4,5},{5,6},{6,7},{8,9},{9,10},{10,11},{11... | collective-permute-start | bytes 98312 | tf_op jit(solution)/shard_map/ppermute | solution.py:265
  7.5 4.7 %collective-permute-start.1 = (f32[1,8,4,256]{3,2,1,0:T(4,128)}, f32[1,8,4,256]{3,2,1,0:T(4,128)S(1)}, u32[]{:S(2)}, u32[]{:S(2)}) collective-permute-start(f32[1,8,4,256]{3,2,1,0:T(4,128)} %get-tuple-element.28), channel_id=1, source_target_pairs={{1,0},{2,1},{3,2},{4,3},{5,4},{6,5},{7,6},{9,8},{10,9},{11,10},{12... | collective-permute-start | bytes 98312 | tf_op jit(solution)/shard_map/ppermute | solution.py:265
  12.2 1.9 %pack_forward.1 = f32[45,8,256]{2,1,0:T(8,128)} custom-call(f32[3,8,8,256]{3,2,1,0:T(8,128)} %vel.6, f32[3,8,8,256]{3,2,1,0:T(8,128)} %rhs.4, f32[3,3,8,8,256]{4,3,2,1,0:T(8,128)} %inv.4), custom_call_target="tpu_custom_call" | custom-call | tf_op jit(solution)/shard_map/pack_forward/pallas_call | solution.py:291
  14.0 0.0 copy-start.3
  14.0 0.0 collective-permute-done.low
  14.0 0.0 copy-start.4
  14.0 0.0 collective-permute-done.1.high
  14.1 0.0 copy-start.6
  14.1 8.6 %collective-permute-start.2 = (f32[45,8,256]{2,1,0:T(8,128)}, f32[45,8,256]{2,1,0:T(8,128)S(1)}, u32[]{:S(2)}, u32[]{:S(2)}) collective-permute-start(f32[45,8,256]{2,1,0:T(8,128)} %pack_forward.1), channel_id=1, source_target_pairs={{0,8},{8,16},{16,24},{24,32},{32,40},{40,48},{48,56},{56,64},{64,7... | collective-permute-start | bytes 1105928 | tf_op jit(solution)/shard_map/ppermute | solution.py:302
  22.7 0.0 copy-done.4
  22.7 0.0 copy-done.6
  22.7 1.8 %divergence.1 = f32[256,128]{1,0:T(8,128)} custom-call(f32[3,8,8,256]{3,2,1,0:T(8,128)} %vel.6, f32[1,8,4,256]{3,2,1,0:T(4,128)} %copy-done.4, f32[1,8,4,256]{3,2,1,0:T(4,128)} %copy-done.6), custom_call_target="tpu_custom_call" | custom-call | tf_op jit(solution)/shard_map/divergence/pallas_call | solution.py:303
  24.5 10.3 %all-to-all-start = ((f32[64,4,128]{2,1,0:T(4,128)}), f32[64,4,128]{2,1,0:T(4,128)S(1)}, u32[]{:S(2)}, u32[]{:S(2)}) async-start(f32[64,4,128]{2,1,0:T(4,128)} %bitcast.8), calls=%async_computation | async-start | bytes 262144 | tf_op jit(solution)/shard_map/all_to_all | solution.py:315
  34.8 2.4 %pack_rest.1 = (f32[45,8,256]{2,1,0:T(8,128)}, f32[14,8,4,256]{3,2,1,0:T(4,128)}, f32[14,8,4,256]{3,2,1,0:T(4,128)}) custom-call(f32[3,8,8,256]{3,2,1,0:T(8,128)} %vel.6, f32[3,8,8,256]{3,2,1,0:T(8,128)} %rhs.4, f32[3,3,8,8,256]{4,3,2,1,0:T(8,128)} %inv.4), custom_call_target="tpu_custom_call" | custom-call | tf_op jit(solution)/shard_map/pack_rest/pallas_call | solution.py:316
  37.2 0.0 copy-start.8
  37.2 11.5 %collective-permute-start.3 = (f32[45,8,256]{2,1,0:T(8,128)}, f32[45,8,256]{2,1,0:T(8,128)S(1)}, u32[]{:S(2)}, u32[]{:S(2)}) collective-permute-start(f32[45,8,256]{2,1,0:T(8,128)} %get-tuple-element.41), channel_id=1, source_target_pairs={{8,0},{16,8},{24,16},{32,24},{40,32},{48,40},{56,48},{64,56},{72,6... | collective-permute-start | bytes 1105928 | tf_op jit(solution)/shard_map/ppermute | solution.py:324
  48.7 0.0 collective-permute-done.2.halo.before
  48.7 0.0 all-to-all-done
  48.7 0.0 copy-done.3
  48.7 0.0 copy-done.8
  48.8 0.0 copy-start.9
  48.8 1.8 %modes.1 = f32[256,128]{1,0:T(8,128)} custom-call(f32[256,128]{1,0:T(8,128)S(1)} %bitcast.6, f32[8,8,512]{2,1,0:T(8,128)S(1)} %bitcast.7, bf16[1024,512]{1,0:T(8,128)(2,1)S(1)} %copy-done.3), custom_call_target="tpu_custom_call" | custom-call | tf_op jit(solution)/shard_map/modes/pallas_call | solution.py:329
  50.6 0.0 copy-start
  50.6 6.7 %all-to-all-start.1 = ((f32[64,4,128]{2,1,0:T(4,128)}), f32[64,4,128]{2,1,0:T(4,128)S(1)}, u32[]{:S(2)}, u32[]{:S(2)}) async-start(f32[64,4,128]{2,1,0:T(4,128)} %bitcast.3), calls=%async_computation.1 | async-start | bytes 262144 | tf_op jit(solution)/shard_map/all_to_all | solution.py:338
  57.3 8.2 %collective-permute-start.4 = (f32[14,8,4,256]{3,2,1,0:T(4,128)}, f32[14,8,4,256]{3,2,1,0:T(4,128)S(1)}, u32[]{:S(2)}, u32[]{:S(2)}) collective-permute-start(f32[14,8,4,256]{3,2,1,0:T(4,128)} %get-tuple-element.48), channel_id=1, source_target_pairs={{0,1},{1,2},{2,3},{3,4},{4,5},{5,6},{6,7},{8,9},{9,10},{10,11},{11... | collective-permute-start | bytes 1376264 | tf_op jit(solution)/shard_map/ppermute | solution.py:265
  65.5 0.0 copy-done.9
  65.5 1.9 %collective-permute-start.5 = (f32[14,8,4,256]{3,2,1,0:T(4,128)S(1)}, f32[14,8,4,256]{3,2,1,0:T(4,128)S(1)}, u32[]{:S(2)}, u32[]{:S(2)}) collective-permute-start(f32[14,8,4,256]{3,2,1,0:T(4,128)S(1)} %copy-done.9), channel_id=1, source_target_pairs={{1,0},{2,1},{3,2},{4,3},{5,4},{6,5},{7,6},{9,8},{10,9},{11,10},{12... | collective-permute-start | bytes 1376264 | tf_op jit(solution)/shard_map/ppermute | solution.py:265
  67.5 0.0 collective-permute-done.3.halo.after
  67.5 0.0 copy-start.7
  67.5 3.3 %all-to-all-done.1 = f32[64,4,128]{2,1,0:T(4,128)S(1)} async-done(((f32[64,4,128]{2,1,0:T(4,128)}), f32[64,4,128]{2,1,0:T(4,128)S(1)}, u32[]{:S(2)}, u32[]{:S(2)}) %all-to-all-start.1) | async-done | bytes 131104 | tf_op jit(solution)/shard_map/all_to_all | solution.py:338
  70.8 0.0 copy-start.1
  70.8 0.0 copy-start.2
  70.8 0.0 copy-start.5
  70.8 0.1 turn.1
  70.9 9.6 %collective-permute-start.6 = (f32[26,8,256]{2,1,0:T(8,128)S(1)}, f32[26,8,256]{2,1,0:T(8,128)S(1)}, u32[]{:S(2)}, u32[]{:S(2)}) collective-permute-start(f32[26,8,256]{2,1,0:T(8,128)S(1)} %get-tuple-element.50), channel_id=1, source_target_pairs={{0,1},{1,2},{2,3},{3,4},{4,5},{5,6},{6,7},{8,9},{9,10},{10,11},{11... | collective-permute-start | bytes 638984 | tf_op jit(solution)/shard_map/ppermute | solution.py:265
  80.5 1.9 %collective-permute-start.7 = (f32[26,8,256]{2,1,0:T(8,128)S(1)}, f32[26,8,256]{2,1,0:T(8,128)S(1)}, u32[]{:S(2)}, u32[]{:S(2)}) collective-permute-start(f32[26,8,256]{2,1,0:T(8,128)S(1)} %get-tuple-element.51), channel_id=1, source_target_pairs={{1,0},{2,1},{3,2},{4,3},{5,4},{6,5},{7,6},{9,8},{10,9},{11,10},{12... | collective-permute-start | bytes 638984 | tf_op jit(solution)/shard_map/ppermute | solution.py:265
  82.5 0.0 collective-permute-done.4.rad_low
  82.5 0.0 collective-permute-done.5.rad_high
  82.5 0.8 collective-permute-done.6.cor_low
  83.3 4.4 %collective-permute-done.7.cor_high = f32[26,8,256]{2,1,0:T(8,128)S(1)} collective-permute-done((f32[26,8,256]{2,1,0:T(8,128)S(1)}, f32[26,8,256]{2,1,0:T(8,128)S(1)}, u32[]{:S(2)}, u32[]{:S(2)}) %collective-permute-start.7) | collective-permute-done | bytes 213024 | tf_op jit(solution)/shard_map/ppermute | solution.py:265
  87.7 0.0 copy-done
  87.7 0.0 copy-done.7
  87.7 0.0 copy-done.1
  87.7 0.0 copy-done.2
  87.7 0.0 copy-done.5
  87.7 2.9 %sweeps.1 = (f32[3,8,8,256]{3,2,1,0:T(8,128)}, f32[8,8,256]{2,1,0:T(8,128)}) custom-call(f32[3,8,8,256]{3,2,1,0:T(8,128)S(1)} %copy-done.1, f32[3,8,8,256]{3,2,1,0:T(8,128)S(1)} %copy-done.2, f32[3,3,8,8,256]{4,3,2,1,0:T(8,128)S(1)} %copy-done, f32[128,256]{1,0:T(8,128)S(1)} %get-tuple-element.45.press, ...), custom_call_target="tpu_custom_call" | custom-call | tf_op jit(solution)/shard_map/sweeps/pallas_call | solution.py:353
  (2 shorter events, 0.1 us)
Async XLA Ops:
  2.1 11.9 %collective-permute-start = (f32[1,8,4,256]{3,2,1,0:T(4,128)}, f32[1,8,4,256]{3,2,1,0:T(4,128)S(1)}, u32[]{:S(2)}, u32[]{:S(2)}) collective-permute-start(f32[1,8,4,256]{3,2,1,0:T(4,128)} %get-tuple-element.27), channel_id=1, source_target_pairs={{0,1},{1,2},{2,3},{3,4},{4,5},{5,6},{6,7},{8,9},{9,10},{10,11},{11... | collective-permute-start | bytes 98312 | tf_op jit(solution)/shard_map/ppermute | solution.py:265
  7.5 6.6 %collective-permute-start.1 = (f32[1,8,4,256]{3,2,1,0:T(4,128)}, f32[1,8,4,256]{3,2,1,0:T(4,128)S(1)}, u32[]{:S(2)}, u32[]{:S(2)}) collective-permute-start(f32[1,8,4,256]{3,2,1,0:T(4,128)} %get-tuple-element.28), channel_id=1, source_target_pairs={{1,0},{2,1},{3,2},{4,3},{5,4},{6,5},{7,6},{9,8},{10,9},{11,10},{12... | collective-permute-start | bytes 98312 | tf_op jit(solution)/shard_map/ppermute | solution.py:265
  14.0 34.7 %copy-start.3 = (bf16[1024,512]{1,0:T(8,128)(2,1)S(1)}, bf16[1024,512]{1,0:T(8,128)(2,1)}, u32[]{:S(2)}) copy-start(bf16[1024,512]{1,0:T(8,128)(2,1)} %constant.2.clone.table) | copy-start | bytes 3145732
  14.0 8.6 %copy-start.4 = (f32[1,8,4,256]{3,2,1,0:T(4,128)}, f32[1,8,4,256]{3,2,1,0:T(4,128)S(1)}, u32[]{:S(2)}) copy-start(f32[1,8,4,256]{3,2,1,0:T(4,128)S(1)} %collective-permute-done.low) | copy-start | bytes 98308
  14.1 8.6 %copy-start.6 = (f32[1,8,4,256]{3,2,1,0:T(4,128)}, f32[1,8,4,256]{3,2,1,0:T(4,128)S(1)}, u32[]{:S(2)}) copy-start(f32[1,8,4,256]{3,2,1,0:T(4,128)S(1)} %collective-permute-done.1.high) | copy-start | bytes 98308
  14.1 34.6 %collective-permute-start.2 = (f32[45,8,256]{2,1,0:T(8,128)}, f32[45,8,256]{2,1,0:T(8,128)S(1)}, u32[]{:S(2)}, u32[]{:S(2)}) collective-permute-start(f32[45,8,256]{2,1,0:T(8,128)} %pack_forward.1), channel_id=1, source_target_pairs={{0,8},{8,16},{16,24},{24,32},{32,40},{40,48},{48,56},{56,64},{64,7... | collective-permute-start | bytes 1105928 | tf_op jit(solution)/shard_map/ppermute | solution.py:302
  24.5 24.2 %all-to-all-start = ((f32[64,4,128]{2,1,0:T(4,128)}), f32[64,4,128]{2,1,0:T(4,128)S(1)}, u32[]{:S(2)}, u32[]{:S(2)}) async-start(f32[64,4,128]{2,1,0:T(4,128)} %bitcast.8), calls=%async_computation | async-start | bytes 262144 | tf_op jit(solution)/shard_map/all_to_all | solution.py:315
  37.2 11.6 %copy-start.8 = (f32[512,8,8]{0,2,1:T(8,128)S(1)}, f32[512,8,8]{0,2,1:T(8,128)}, u32[]{:S(2)}) copy-start(f32[512,8,8]{0,2,1:T(8,128)} %param.7) | copy-start | bytes 393220
  37.2 30.3 %collective-permute-start.3 = (f32[45,8,256]{2,1,0:T(8,128)}, f32[45,8,256]{2,1,0:T(8,128)S(1)}, u32[]{:S(2)}, u32[]{:S(2)}) collective-permute-start(f32[45,8,256]{2,1,0:T(8,128)} %get-tuple-element.41), channel_id=1, source_target_pairs={{8,0},{16,8},{24,16},{32,24},{40,32},{48,40},{56,48},{64,56},{72,6... | collective-permute-start | bytes 1105928 | tf_op jit(solution)/shard_map/ppermute | solution.py:324
  48.8 16.8 %copy-start.9 = (f32[14,8,4,256]{3,2,1,0:T(4,128)S(1)}, f32[14,8,4,256]{3,2,1,0:T(4,128)}, u32[]{:S(2)}) copy-start(f32[14,8,4,256]{3,2,1,0:T(4,128)} %get-tuple-element.49) | copy-start | bytes 1376260
  50.6 37.1 %copy-start = (f32[3,3,8,8,256]{4,3,2,1,0:T(8,128)S(1)}, f32[3,3,8,8,256]{4,3,2,1,0:T(8,128)}, u32[]{:S(2)}) copy-start(f32[3,3,8,8,256]{4,3,2,1,0:T(8,128)} %inv.4) | copy-start | bytes 1769476
  50.6 20.2 %all-to-all-start.1 = ((f32[64,4,128]{2,1,0:T(4,128)}), f32[64,4,128]{2,1,0:T(4,128)S(1)}, u32[]{:S(2)}, u32[]{:S(2)}) async-start(f32[64,4,128]{2,1,0:T(4,128)} %bitcast.3), calls=%async_computation.1 | async-start | bytes 262144 | tf_op jit(solution)/shard_map/all_to_all | solution.py:338
  57.3 25.2 %collective-permute-start.4 = (f32[14,8,4,256]{3,2,1,0:T(4,128)}, f32[14,8,4,256]{3,2,1,0:T(4,128)S(1)}, u32[]{:S(2)}, u32[]{:S(2)}) collective-permute-start(f32[14,8,4,256]{3,2,1,0:T(4,128)} %get-tuple-element.48), channel_id=1, source_target_pairs={{0,1},{1,2},{2,3},{3,4},{4,5},{5,6},{6,7},{8,9},{9,10},{10,11},{11... | collective-permute-start | bytes 1376264 | tf_op jit(solution)/shard_map/ppermute | solution.py:265
  65.5 17.0 %collective-permute-start.5 = (f32[14,8,4,256]{3,2,1,0:T(4,128)S(1)}, f32[14,8,4,256]{3,2,1,0:T(4,128)S(1)}, u32[]{:S(2)}, u32[]{:S(2)}) collective-permute-start(f32[14,8,4,256]{3,2,1,0:T(4,128)S(1)} %copy-done.9), channel_id=1, source_target_pairs={{1,0},{2,1},{3,2},{4,3},{5,4},{6,5},{7,6},{9,8},{10,9},{11,10},{12... | collective-permute-start | bytes 1376264 | tf_op jit(solution)/shard_map/ppermute | solution.py:265
  67.5 20.2 %copy-start.7 = (f32[1,8,4,256]{3,2,1,0:T(4,128)S(1)}, f32[1,8,4,256]{3,2,1,0:T(4,128)}, u32[]{:S(2)}) copy-start(f32[1,8,4,256]{3,2,1,0:T(4,128)} %copy-done.6) | copy-start | bytes 98308
  70.8 16.9 %copy-start.1 = (f32[3,8,8,256]{3,2,1,0:T(8,128)S(1)}, f32[3,8,8,256]{3,2,1,0:T(8,128)}, u32[]{:S(2)}) copy-start(f32[3,8,8,256]{3,2,1,0:T(8,128)} %vel.6) | copy-start | bytes 589828
  70.8 16.9 %copy-start.2 = (f32[3,8,8,256]{3,2,1,0:T(8,128)S(1)}, f32[3,8,8,256]{3,2,1,0:T(8,128)}, u32[]{:S(2)}) copy-start(f32[3,8,8,256]{3,2,1,0:T(8,128)} %rhs.4) | copy-start | bytes 589828
  70.8 16.9 %copy-start.5 = (f32[1,8,4,256]{3,2,1,0:T(4,128)S(1)}, f32[1,8,4,256]{3,2,1,0:T(4,128)}, u32[]{:S(2)}) copy-start(f32[1,8,4,256]{3,2,1,0:T(4,128)} %copy-done.4) | copy-start | bytes 98308
  70.9 12.4 %collective-permute-start.6 = (f32[26,8,256]{2,1,0:T(8,128)S(1)}, f32[26,8,256]{2,1,0:T(8,128)S(1)}, u32[]{:S(2)}, u32[]{:S(2)}) collective-permute-start(f32[26,8,256]{2,1,0:T(8,128)S(1)} %get-tuple-element.50), channel_id=1, source_target_pairs={{0,1},{1,2},{2,3},{3,4},{4,5},{5,6},{6,7},{8,9},{9,10},{10,11},{11... | collective-permute-start | bytes 638984 | tf_op jit(solution)/shard_map/ppermute | solution.py:265
  80.5 7.2 %collective-permute-start.7 = (f32[26,8,256]{2,1,0:T(8,128)S(1)}, f32[26,8,256]{2,1,0:T(8,128)S(1)}, u32[]{:S(2)}, u32[]{:S(2)}) collective-permute-start(f32[26,8,256]{2,1,0:T(8,128)S(1)} %get-tuple-element.51), channel_id=1, source_target_pairs={{1,0},{2,1},{3,2},{4,3},{5,4},{6,5},{7,6},{9,8},{10,9},{11,10},{12... | collective-permute-start | bytes 638984 | tf_op jit(solution)/shard_map/ppermute | solution.py:265

commit v5 on v4

--- a/solution.py
+++ b/solution.py
@@ -284,7 +284,7 @@
         in_specs=[pl.BlockSpec((1, LINES, CR, NZ), lambda i: (1, 0, 0, 0))],
         out_specs=[pl.BlockSpec((1, LINES, 4, NZ), lambda i: (0, 0, 0, 0))] * 2,
         out_shape=[shape(1, LINES, 4, NZ)] * 2,
-        compiler_params=params(60),
+        compiler_params=params(24),
         name="pack_first",
     )(vel)
     low, high = both_ways(up, down, "radial", False)
@@ -307,7 +307,7 @@
         + [pl.BlockSpec((1, LINES, 4, NZ), lambda i: (0, 0, 0, 0))] * 2,
         out_specs=pl.BlockSpec((NZ, 128), lambda i: (0, 0)),
         out_shape=shape(NZ, 128),
-        compiler_params=params(60),
+        compiler_params=params(24),
         name="divergence",
     )(vel, low, high)
     sent = sent.reshape(BLOCKS, CHUNK, 128)

time: 91.2 us -> 90.7 us (level)
  Pallas kernels: 12.4 us -> 9.93 us
    all_to_all x2, starting transfers between devices: 17 us -> 18.5 us  [on_device(): got = lax.all_to_all(sent, 'pitch', split_axis=0, concat_axis=0, tiled=True)]
    pallas_call x1, Pallas kernels: 1.47 us -> 0.01 us  [on_device(): pl.pallas_call(pack_first, grid=(1,), in_specs=[pl.BlockSpec((1, LINES, C...]
    pallas_call x1, Pallas kernels: 1.79 us -> 0.84 us  [on_device(): pl.pallas_call(div_kernel, grid=(1,), in_specs=[pl.BlockSpec((3, LINES, C...]
    unnamed x20 -> x16, local copies, waits for them, and re-layouts: 0.04 us -> 0.95 us
  transfers between devices with their start and end apart: 10 -> 10, of which waited for: 3 -> 3; matrix products, arithmetic and copies ran while one was open for 0% -> 0% of each run, Pallas kernels for 9% -> 8%
where the time goes in v5:
time: 90.7 us; the launch traced here: 90.2 us
  starting transfers between devices  69.5 us (77%)
  Pallas kernels  9.93 us (11%)
  waiting for transfers between devices  9 us (10%)
  local copies, waits for them, and re-layouts  0.95 us (1%)
    ppermute x6, starting transfers between devices, both_ways(): return (lax.ppermute(up, axis, forward), lax.ppermute(down, axis, backward))  31.1 us
    all_to_all x2, starting transfers between devices, on_device(): got = lax.all_to_all(sent, 'pitch', split_axis=0, concat_axis=0, tiled=True)  18.5 us
    ppermute x1, starting transfers between devices, on_device(): lax.ppermute(bwd, 'pitch', [((i + 1) % BLOCKS, i) for i in range(BLOCKS)])  11.5 us
    ppermute x1, starting transfers between devices, on_device(): lax.ppermute(fwd, 'pitch', [(i, (i + 1) % BLOCKS) for i in range(BLOCKS)])  8.41 us
    ppermute x6, waiting for transfers between devices, both_ways(): return (lax.ppermute(up, axis, forward), lax.ppermute(down, axis, backward))  5.23 us
    all_to_all x2, waiting for transfers between devices, on_device(): got = lax.all_to_all(sent, 'pitch', split_axis=0, concat_axis=0, tiled=True)  3.77 us
    pallas_call x1, Pallas kernels, on_device(): pl.pallas_call(sweep_kernel, in_specs=[VMEM] * 12, out_specs=[VMEM] * 2,...  2.87 us
    pallas_call x1, Pallas kernels, on_device(): pl.pallas_call(pack_rest, in_specs=[VMEM] * 3, out_specs=[VMEM] * 3, out_...  2.36 us
  transfers between devices with their start and end apart: 10, of which 3 were waited for; matrix products, arithmetic and copies ran while one was open for 0% of the time, Pallas kernels for 8%

profile of v5, /device:TPU:1, one launch (start us, length us, event | category | flops | bytes accessed | tf_op | source)
XLA Modules:
  0.0 90.2 jit_solution(8191455667003390632)
XLA Ops:
  0.6 0.0 copy-start.1
  0.6 0.9 %copy-done.1 = f32[3,8,8,256]{3,2,1,0:T(8,128)S(1)} copy-done((f32[3,8,8,256]{3,2,1,0:T(8,128)S(1)}, f32[3,8,8,256]{3,2,1,0:T(8,128)}, u32[]{:S(2)}) %copy-start.1) | copy-done | bytes 196632
  1.6 5.4 %collective-permute-start = (f32[1,8,4,256]{3,2,1,0:T(4,128)S(1)}, f32[1,8,4,256]{3,2,1,0:T(4,128)S(1)}, u32[]{:S(2)}, u32[]{:S(2)}) collective-permute-start(f32[1,8,4,256]{3,2,1,0:T(4,128)S(1)} %get-tuple-element.27), channel_id=1, source_target_pairs={{0,1},{1,2},{2,3},{3,4},{4,5},{5,6},{6,7},{8,9},{9,10},{10,11},{11... | collective-permute-start | bytes 98312 | tf_op jit(solution)/shard_map/ppermute | solution.py:265
  7.0 0.0 copy-start.2
  7.0 4.8 %collective-permute-start.1 = (f32[1,8,4,256]{3,2,1,0:T(4,128)S(1)}, f32[1,8,4,256]{3,2,1,0:T(4,128)S(1)}, u32[]{:S(2)}, u32[]{:S(2)}) collective-permute-start(f32[1,8,4,256]{3,2,1,0:T(4,128)S(1)} %get-tuple-element.28), channel_id=1, source_target_pairs={{1,0},{2,1},{3,2},{4,3},{5,4},{6,5},{7,6},{9,8},{10,9},{11,10},{12... | collective-permute-start | bytes 98312 | tf_op jit(solution)/shard_map/ppermute | solution.py:265
  11.8 1.8 %pack_forward.1 = f32[45,8,256]{2,1,0:T(8,128)} custom-call(f32[3,8,8,256]{3,2,1,0:T(8,128)} %vel.6, f32[3,8,8,256]{3,2,1,0:T(8,128)} %rhs.4, f32[3,3,8,8,256]{4,3,2,1,0:T(8,128)} %inv.4), custom_call_target="tpu_custom_call" | custom-call | tf_op jit(solution)/shard_map/pack_forward/pallas_call | solution.py:291
  13.6 0.0 copy-start.5
  13.6 0.0 collective-permute-done.low
  13.6 0.0 collective-permute-done.1.high
  13.6 8.4 %collective-permute-start.2 = (f32[45,8,256]{2,1,0:T(8,128)}, f32[45,8,256]{2,1,0:T(8,128)S(1)}, u32[]{:S(2)}, u32[]{:S(2)}) collective-permute-start(f32[45,8,256]{2,1,0:T(8,128)} %pack_forward.1), channel_id=1, source_target_pairs={{0,8},{8,16},{16,24},{24,32},{32,40},{40,48},{48,56},{56,64},{64,7... | collective-permute-start | bytes 1105928 | tf_op jit(solution)/shard_map/ppermute | solution.py:302
  22.1 0.0 copy-done.2
  22.1 0.8 divergence.1
  22.9 10.3 %all-to-all-start = ((f32[64,4,128]{2,1,0:T(4,128)}), f32[64,4,128]{2,1,0:T(4,128)S(1)}, u32[]{:S(2)}, u32[]{:S(2)}) async-start(f32[64,4,128]{2,1,0:T(4,128)} %bitcast), calls=%async_computation | async-start | bytes 262144 | tf_op jit(solution)/shard_map/all_to_all | solution.py:315
  33.2 2.4 %pack_rest.1 = (f32[45,8,256]{2,1,0:T(8,128)}, f32[14,8,4,256]{3,2,1,0:T(4,128)}, f32[14,8,4,256]{3,2,1,0:T(4,128)}) custom-call(f32[3,8,8,256]{3,2,1,0:T(8,128)} %vel.6, f32[3,8,8,256]{3,2,1,0:T(8,128)} %rhs.4, f32[3,3,8,8,256]{4,3,2,1,0:T(8,128)} %inv.4), custom_call_target="tpu_custom_call" | custom-call | tf_op jit(solution)/shard_map/pack_rest/pallas_call | solution.py:316
  35.6 0.0 copy-start.6
  35.6 11.5 %collective-permute-start.3 = (f32[45,8,256]{2,1,0:T(8,128)}, f32[45,8,256]{2,1,0:T(8,128)S(1)}, u32[]{:S(2)}, u32[]{:S(2)}) collective-permute-start(f32[45,8,256]{2,1,0:T(8,128)} %get-tuple-element.41), channel_id=1, source_target_pairs={{8,0},{16,8},{24,16},{32,24},{40,32},{48,40},{56,48},{64,56},{72,6... | collective-permute-start | bytes 1105928 | tf_op jit(solution)/shard_map/ppermute | solution.py:324
  47.1 0.0 collective-permute-done.2.halo.before
  47.1 0.0 all-to-all-done
  47.1 0.0 copy-done.5
  47.1 0.0 copy-done.6
  47.2 0.0 copy-start.7
  47.2 1.8 %modes.1 = f32[256,128]{1,0:T(8,128)} custom-call(f32[256,128]{1,0:T(8,128)S(1)} %bitcast.6, f32[8,8,512]{2,1,0:T(8,128)S(1)} %bitcast.7, bf16[1024,512]{1,0:T(8,128)(2,1)S(1)} %copy-done.5), custom_call_target="tpu_custom_call" | custom-call | tf_op jit(solution)/shard_map/modes/pallas_call | solution.py:329
  49.0 0.0 copy-start
  49.0 8.2 %all-to-all-start.1 = ((f32[64,4,128]{2,1,0:T(4,128)}), f32[64,4,128]{2,1,0:T(4,128)S(1)}, u32[]{:S(2)}, u32[]{:S(2)}) async-start(f32[64,4,128]{2,1,0:T(4,128)} %bitcast.3), calls=%async_computation.1 | async-start | bytes 262144 | tf_op jit(solution)/shard_map/all_to_all | solution.py:338
  57.2 8.1 %collective-permute-start.4 = (f32[14,8,4,256]{3,2,1,0:T(4,128)}, f32[14,8,4,256]{3,2,1,0:T(4,128)S(1)}, u32[]{:S(2)}, u32[]{:S(2)}) collective-permute-start(f32[14,8,4,256]{3,2,1,0:T(4,128)} %get-tuple-element.48), channel_id=1, source_target_pairs={{0,1},{1,2},{2,3},{3,4},{4,5},{5,6},{6,7},{8,9},{9,10},{10,11},{11... | collective-permute-start | bytes 1376264 | tf_op jit(solution)/shard_map/ppermute | solution.py:265
  65.3 0.0 copy-done.7
  65.3 1.9 %collective-permute-start.5 = (f32[14,8,4,256]{3,2,1,0:T(4,128)S(1)}, f32[14,8,4,256]{3,2,1,0:T(4,128)S(1)}, u32[]{:S(2)}, u32[]{:S(2)}) collective-permute-start(f32[14,8,4,256]{3,2,1,0:T(4,128)S(1)} %copy-done.7), channel_id=1, source_target_pairs={{1,0},{2,1},{3,2},{4,3},{5,4},{6,5},{7,6},{9,8},{10,9},{11,10},{12... | collective-permute-start | bytes 1376264 | tf_op jit(solution)/shard_map/ppermute | solution.py:265
  67.2 0.0 collective-permute-done.3.halo.after
  67.3 3.8 %all-to-all-done.1 = f32[64,4,128]{2,1,0:T(4,128)S(1)} async-done(((f32[64,4,128]{2,1,0:T(4,128)}), f32[64,4,128]{2,1,0:T(4,128)S(1)}, u32[]{:S(2)}, u32[]{:S(2)}) %all-to-all-start.1) | async-done | bytes 131104 | tf_op jit(solution)/shard_map/all_to_all | solution.py:338
  71.0 0.0 copy-start.3
  71.0 0.0 copy-start.4
  71.0 0.1 turn.1
  71.1 9.0 %collective-permute-start.6 = (f32[26,8,256]{2,1,0:T(8,128)S(1)}, f32[26,8,256]{2,1,0:T(8,128)S(1)}, u32[]{:S(2)}, u32[]{:S(2)}) collective-permute-start(f32[26,8,256]{2,1,0:T(8,128)S(1)} %get-tuple-element.50), channel_id=1, source_target_pairs={{0,1},{1,2},{2,3},{3,4},{4,5},{5,6},{6,7},{8,9},{9,10},{10,11},{11... | collective-permute-start | bytes 638984 | tf_op jit(solution)/shard_map/ppermute | solution.py:265
  80.1 1.9 %collective-permute-start.7 = (f32[26,8,256]{2,1,0:T(8,128)S(1)}, f32[26,8,256]{2,1,0:T(8,128)S(1)}, u32[]{:S(2)}, u32[]{:S(2)}) collective-permute-start(f32[26,8,256]{2,1,0:T(8,128)S(1)} %get-tuple-element.51), channel_id=1, source_target_pairs={{1,0},{2,1},{3,2},{4,3},{5,4},{6,5},{7,6},{9,8},{10,9},{11,10},{12... | collective-permute-start | bytes 638984 | tf_op jit(solution)/shard_map/ppermute | solution.py:265
  82.1 0.0 collective-permute-done.4.rad_low
  82.1 0.0 collective-permute-done.5.rad_high
  82.1 0.8 collective-permute-done.6.cor_low
  82.9 4.4 %collective-permute-done.7.cor_high = f32[26,8,256]{2,1,0:T(8,128)S(1)} collective-permute-done((f32[26,8,256]{2,1,0:T(8,128)S(1)}, f32[26,8,256]{2,1,0:T(8,128)S(1)}, u32[]{:S(2)}, u32[]{:S(2)}) %collective-permute-start.7) | collective-permute-done | bytes 213024 | tf_op jit(solution)/shard_map/ppermute | solution.py:265
  87.3 0.0 copy-done
  87.3 0.0 copy-done.3
  87.3 0.0 copy-done.4
  87.3 2.9 %sweeps.1 = (f32[3,8,8,256]{3,2,1,0:T(8,128)}, f32[8,8,256]{2,1,0:T(8,128)}) custom-call(f32[3,8,8,256]{3,2,1,0:T(8,128)S(1)} %copy-done.3, f32[3,8,8,256]{3,2,1,0:T(8,128)S(1)} %copy-done.4, f32[3,3,8,8,256]{4,3,2,1,0:T(8,128)S(1)} %copy-done, f32[128,256]{1,0:T(8,128)S(1)} %get-tuple-element.45.press, ...), custom_call_target="tpu_custom_call" | custom-call | tf_op jit(solution)/shard_map/sweeps/pallas_call | solution.py:353
  (3 shorter events, 0.1 us)
Async XLA Ops:
  0.6 0.9 %copy-start.1 = (f32[3,8,8,256]{3,2,1,0:T(8,128)S(1)}, f32[3,8,8,256]{3,2,1,0:T(8,128)}, u32[]{:S(2)}) copy-start(f32[3,8,8,256]{3,2,1,0:T(8,128)} %vel.6) | copy-start | bytes 589828
  1.6 12.1 %collective-permute-start = (f32[1,8,4,256]{3,2,1,0:T(4,128)S(1)}, f32[1,8,4,256]{3,2,1,0:T(4,128)S(1)}, u32[]{:S(2)}, u32[]{:S(2)}) collective-permute-start(f32[1,8,4,256]{3,2,1,0:T(4,128)S(1)} %get-tuple-element.27), channel_id=1, source_target_pairs={{0,1},{1,2},{2,3},{3,4},{4,5},{5,6},{6,7},{8,9},{9,10},{10,11},{11... | collective-permute-start | bytes 98312 | tf_op jit(solution)/shard_map/ppermute | solution.py:265
  7.0 15.1 %copy-start.2 = (f32[3,8,8,256]{3,2,1,0:T(8,128)S(1)}, f32[3,8,8,256]{3,2,1,0:T(8,128)}, u32[]{:S(2)}) copy-start(f32[3,8,8,256]{3,2,1,0:T(8,128)} %vel.6) | copy-start | bytes 589828
  7.0 6.7 %collective-permute-start.1 = (f32[1,8,4,256]{3,2,1,0:T(4,128)S(1)}, f32[1,8,4,256]{3,2,1,0:T(4,128)S(1)}, u32[]{:S(2)}, u32[]{:S(2)}) collective-permute-start(f32[1,8,4,256]{3,2,1,0:T(4,128)S(1)} %get-tuple-element.28), channel_id=1, source_target_pairs={{1,0},{2,1},{3,2},{4,3},{5,4},{6,5},{7,6},{9,8},{10,9},{11,10},{12... | collective-permute-start | bytes 98312 | tf_op jit(solution)/shard_map/ppermute | solution.py:265
  13.6 33.5 %copy-start.5 = (bf16[1024,512]{1,0:T(8,128)(2,1)S(1)}, bf16[1024,512]{1,0:T(8,128)(2,1)}, u32[]{:S(2)}) copy-start(bf16[1024,512]{1,0:T(8,128)(2,1)} %constant.2.clone.table) | copy-start | bytes 3145732
  13.6 33.4 %collective-permute-start.2 = (f32[45,8,256]{2,1,0:T(8,128)}, f32[45,8,256]{2,1,0:T(8,128)S(1)}, u32[]{:S(2)}, u32[]{:S(2)}) collective-permute-start(f32[45,8,256]{2,1,0:T(8,128)} %pack_forward.1), channel_id=1, source_target_pairs={{0,8},{8,16},{16,24},{24,32},{32,40},{40,48},{48,56},{56,64},{64,7... | collective-permute-start | bytes 1105928 | tf_op jit(solution)/shard_map/ppermute | solution.py:302
  22.9 24.2 %all-to-all-start = ((f32[64,4,128]{2,1,0:T(4,128)}), f32[64,4,128]{2,1,0:T(4,128)S(1)}, u32[]{:S(2)}, u32[]{:S(2)}) async-start(f32[64,4,128]{2,1,0:T(4,128)} %bitcast), calls=%async_computation | async-start | bytes 262144 | tf_op jit(solution)/shard_map/all_to_all | solution.py:315
  35.6 11.6 %copy-start.6 = (f32[512,8,8]{0,2,1:T(8,128)S(1)}, f32[512,8,8]{0,2,1:T(8,128)}, u32[]{:S(2)}) copy-start(f32[512,8,8]{0,2,1:T(8,128)} %param.7) | copy-start | bytes 393220
  35.6 31.6 %collective-permute-start.3 = (f32[45,8,256]{2,1,0:T(8,128)}, f32[45,8,256]{2,1,0:T(8,128)S(1)}, u32[]{:S(2)}, u32[]{:S(2)}) collective-permute-start(f32[45,8,256]{2,1,0:T(8,128)} %get-tuple-element.41), channel_id=1, source_target_pairs={{8,0},{16,8},{24,16},{32,24},{40,32},{48,40},{56,48},{64,56},{72,6... | collective-permute-start | bytes 1105928 | tf_op jit(solution)/shard_map/ppermute | solution.py:324
  47.2 18.1 %copy-start.7 = (f32[14,8,4,256]{3,2,1,0:T(4,128)S(1)}, f32[14,8,4,256]{3,2,1,0:T(4,128)}, u32[]{:S(2)}) copy-start(f32[14,8,4,256]{3,2,1,0:T(4,128)} %get-tuple-element.49) | copy-start | bytes 1376260
  49.0 38.3 %copy-start = (f32[3,3,8,8,256]{4,3,2,1,0:T(8,128)S(1)}, f32[3,3,8,8,256]{4,3,2,1,0:T(8,128)}, u32[]{:S(2)}) copy-start(f32[3,3,8,8,256]{4,3,2,1,0:T(8,128)} %inv.4) | copy-start | bytes 1769476
  49.0 22.0 %all-to-all-start.1 = ((f32[64,4,128]{2,1,0:T(4,128)}), f32[64,4,128]{2,1,0:T(4,128)S(1)}, u32[]{:S(2)}, u32[]{:S(2)}) async-start(f32[64,4,128]{2,1,0:T(4,128)} %bitcast.3), calls=%async_computation.1 | async-start | bytes 262144 | tf_op jit(solution)/shard_map/all_to_all | solution.py:338
  57.2 24.9 %collective-permute-start.4 = (f32[14,8,4,256]{3,2,1,0:T(4,128)}, f32[14,8,4,256]{3,2,1,0:T(4,128)S(1)}, u32[]{:S(2)}, u32[]{:S(2)}) collective-permute-start(f32[14,8,4,256]{3,2,1,0:T(4,128)} %get-tuple-element.48), channel_id=1, source_target_pairs={{0,1},{1,2},{2,3},{3,4},{4,5},{5,6},{6,7},{8,9},{9,10},{10,11},{11... | collective-permute-start | bytes 1376264 | tf_op jit(solution)/shard_map/ppermute | solution.py:265
  65.3 16.8 %collective-permute-start.5 = (f32[14,8,4,256]{3,2,1,0:T(4,128)S(1)}, f32[14,8,4,256]{3,2,1,0:T(4,128)S(1)}, u32[]{:S(2)}, u32[]{:S(2)}) collective-permute-start(f32[14,8,4,256]{3,2,1,0:T(4,128)S(1)} %copy-done.7), channel_id=1, source_target_pairs={{1,0},{2,1},{3,2},{4,3},{5,4},{6,5},{7,6},{9,8},{10,9},{11,10},{12... | collective-permute-start | bytes 1376264 | tf_op jit(solution)/shard_map/ppermute | solution.py:265
  71.0 16.3 %copy-start.3 = (f32[3,8,8,256]{3,2,1,0:T(8,128)S(1)}, f32[3,8,8,256]{3,2,1,0:T(8,128)}, u32[]{:S(2)}) copy-start(f32[3,8,8,256]{3,2,1,0:T(8,128)} %vel.6) | copy-start | bytes 589828
  71.0 16.3 %copy-start.4 = (f32[3,8,8,256]{3,2,1,0:T(8,128)S(1)}, f32[3,8,8,256]{3,2,1,0:T(8,128)}, u32[]{:S(2)}) copy-start(f32[3,8,8,256]{3,2,1,0:T(8,128)} %rhs.4) | copy-start | bytes 589828
  71.1 11.8 %collective-permute-start.6 = (f32[26,8,256]{2,1,0:T(8,128)S(1)}, f32[26,8,256]{2,1,0:T(8,128)S(1)}, u32[]{:S(2)}, u32[]{:S(2)}) collective-permute-start(f32[26,8,256]{2,1,0:T(8,128)S(1)} %get-tuple-element.50), channel_id=1, source_target_pairs={{0,1},{1,2},{2,3},{3,4},{4,5},{5,6},{6,7},{8,9},{9,10},{10,11},{11... | collective-permute-start | bytes 638984 | tf_op jit(solution)/shard_map/ppermute | solution.py:265
  80.1 7.2 %collective-permute-start.7 = (f32[26,8,256]{2,1,0:T(8,128)S(1)}, f32[26,8,256]{2,1,0:T(8,128)S(1)}, u32[]{:S(2)}, u32[]{:S(2)}) collective-permute-start(f32[26,8,256]{2,1,0:T(8,128)S(1)} %get-tuple-element.51), channel_id=1, source_target_pairs={{1,0},{2,1},{3,2},{4,3},{5,4},{6,5},{7,6},{9,8},{10,9},{11,10},{12... | collective-permute-start | bytes 638984 | tf_op jit(solution)/shard_map/ppermute | solution.py:265

commit v6 on v5

--- a/solution.py
+++ b/solution.py
@@ -295,7 +295,7 @@
         + [pl.BlockSpec((3, 3, 4, CR, NZ), lambda i: (0, 0, 1, 0, 0))],
         out_specs=pl.BlockSpec((45, CR, NZ), lambda i: (0, 0, 0)),
         out_shape=shape(45, CR, NZ),
-        compiler_params=params(60),
+        compiler_params=params(24),
         name="pack_forward",
     )(vel, rhs_mom, sweep_inv)
     fwd, low, high = lax.optimization_barrier((fwd, low, high))

time: 90.7 us -> 89.8 us (0.990)
  Pallas kernels: 9.93 us -> 8.11 us
  local copies, waits for them, and re-layouts: 0.95 us -> 2.01 us
    pallas_call x1, Pallas kernels: 1.84 us -> 0.03 us  [on_device(): pl.pallas_call(pack_forward, grid=(1,), in_specs=[pl.BlockSpec((3, 4, CR,...]
    ppermute x6, starting transfers between devices: 31.1 us -> 29.9 us  [both_ways(): return (lax.ppermute(up, axis, forward), lax.ppermute(down, axis, backward))]
    unnamed x16 -> x18, local copies, waits for them, and re-layouts: 0.95 us -> 2.01 us
  transfers between devices with their start and end apart: 10 -> 10, of which waited for: 3 -> 3; matrix products, arithmetic and copies ran while one was open for 0% -> 0% of each run, Pallas kernels for 8% -> 6%
where the time goes in v6:
time: 89.8 us; the launch traced here: 89.3 us
  starting transfers between devices  68.6 us (76%)
  waiting for transfers between devices  9.72 us (11%)
  Pallas kernels  8.11 us (9%)
  local copies, waits for them, and re-layouts  2.01 us (2%)
    ppermute x6, starting transfers between devices, both_ways(): return (lax.ppermute(up, axis, forward), lax.ppermute(down, axis, backward))  29.9 us
    all_to_all x2, starting transfers between devices, on_device(): got = lax.all_to_all(sent, 'pitch', split_axis=0, concat_axis=0, tiled=True)  18.1 us
    ppermute x1, starting transfers between devices, on_device(): lax.ppermute(bwd, 'pitch', [((i + 1) % BLOCKS, i) for i in range(BLOCKS)])  11.5 us
    ppermute x1, starting transfers between devices, on_device(): lax.ppermute(fwd, 'pitch', [(i, (i + 1) % BLOCKS) for i in range(BLOCKS)])  9.12 us
    ppermute x6, waiting for transfers between devices, both_ways(): return (lax.ppermute(up, axis, forward), lax.ppermute(down, axis, backward))  5.23 us
    all_to_all x2, waiting for transfers between devices, on_device(): got = lax.all_to_all(sent, 'pitch', split_axis=0, concat_axis=0, tiled=True)  4.49 us
    pallas_call x1, Pallas kernels, on_device(): pl.pallas_call(sweep_kernel, in_specs=[VMEM] * 12, out_specs=[VMEM] * 2,...  2.87 us
    pallas_call x1, Pallas kernels, on_device(): pl.pallas_call(pack_rest, in_specs=[VMEM] * 3, out_specs=[VMEM] * 3, out_...  2.36 us
  transfers between devices with their start and end apart: 10, of which 3 were waited for; matrix products, arithmetic and copies ran while one was open for 0% of the time, Pallas kernels for 6%

profile of v6, /device:TPU:1, one launch (start us, length us, event | category | flops | bytes accessed | tf_op | source)
XLA Modules:
  0.0 89.3 jit_solution(12086769365532375284)
XLA Ops:
  0.6 0.0 copy-start.2
  0.6 0.9 %copy-done.2 = f32[3,8,8,256]{3,2,1,0:T(8,128)S(1)} copy-done((f32[3,8,8,256]{3,2,1,0:T(8,128)S(1)}, f32[3,8,8,256]{3,2,1,0:T(8,128)}, u32[]{:S(2)}) %copy-start.2) | copy-done | bytes 196632
  1.6 0.0 copy-start.4
  1.6 5.5 %collective-permute-start = (f32[1,8,4,256]{3,2,1,0:T(4,128)S(1)}, f32[1,8,4,256]{3,2,1,0:T(4,128)S(1)}, u32[]{:S(2)}, u32[]{:S(2)}) collective-permute-start(f32[1,8,4,256]{3,2,1,0:T(4,128)S(1)} %get-tuple-element.27), channel_id=1, source_target_pairs={{0,1},{1,2},{2,3},{3,4},{4,5},{5,6},{6,7},{8,9},{9,10},{10,11},{11... | collective-permute-start | bytes 98312 | tf_op jit(solution)/shard_map/ppermute | solution.py:265
  7.1 4.7 %collective-permute-start.1 = (f32[1,8,4,256]{3,2,1,0:T(4,128)S(1)}, f32[1,8,4,256]{3,2,1,0:T(4,128)S(1)}, u32[]{:S(2)}, u32[]{:S(2)}) collective-permute-start(f32[1,8,4,256]{3,2,1,0:T(4,128)S(1)} %get-tuple-element.28), channel_id=1, source_target_pairs={{1,0},{2,1},{3,2},{4,3},{5,4},{6,5},{7,6},{9,8},{10,9},{11,10},{12... | collective-permute-start | bytes 98312 | tf_op jit(solution)/shard_map/ppermute | solution.py:265
  11.8 0.0 copy-done.4
  11.8 0.0 copy-start
  11.8 1.1 %copy-done = f32[3,3,8,8,256]{4,3,2,1,0:T(8,128)S(1)} copy-done((f32[3,3,8,8,256]{4,3,2,1,0:T(8,128)S(1)}, f32[3,3,8,8,256]{4,3,2,1,0:T(8,128)}, u32[]{:S(2)}) %copy-start) | copy-done | bytes 589848
  12.9 0.0 copy-start.6
  12.9 0.0 collective-permute-done.low
  12.9 0.0 collective-permute-done.1.high
  12.9 9.1 %collective-permute-start.2 = (f32[45,8,256]{2,1,0:T(8,128)S(1)}, f32[45,8,256]{2,1,0:T(8,128)S(1)}, u32[]{:S(2)}, u32[]{:S(2)}) collective-permute-start(f32[45,8,256]{2,1,0:T(8,128)S(1)} %pack_forward.1), channel_id=1, source_target_pairs={{0,8},{8,16},{16,24},{24,32},{32,40},{40,48},{48,56},{56,64},{64,7... | collective-permute-start | bytes 1105928 | tf_op jit(solution)/shard_map/ppermute | solution.py:302
  22.1 0.8 divergence.1
  22.9 10.3 %all-to-all-start = ((f32[64,4,128]{2,1,0:T(4,128)}), f32[64,4,128]{2,1,0:T(4,128)S(1)}, u32[]{:S(2)}, u32[]{:S(2)}) async-start(f32[64,4,128]{2,1,0:T(4,128)} %bitcast), calls=%async_computation | async-start | bytes 262144 | tf_op jit(solution)/shard_map/all_to_all | solution.py:315
  33.2 2.4 %pack_rest.1 = (f32[45,8,256]{2,1,0:T(8,128)}, f32[14,8,4,256]{3,2,1,0:T(4,128)}, f32[14,8,4,256]{3,2,1,0:T(4,128)}) custom-call(f32[3,8,8,256]{3,2,1,0:T(8,128)} %vel.6, f32[3,8,8,256]{3,2,1,0:T(8,128)} %rhs.4, f32[3,3,8,8,256]{4,3,2,1,0:T(8,128)} %inv.4), custom_call_target="tpu_custom_call" | custom-call | tf_op jit(solution)/shard_map/pack_rest/pallas_call | solution.py:316
  35.6 0.0 copy-start.7
  35.6 11.5 %collective-permute-start.3 = (f32[45,8,256]{2,1,0:T(8,128)}, f32[45,8,256]{2,1,0:T(8,128)S(1)}, u32[]{:S(2)}, u32[]{:S(2)}) collective-permute-start(f32[45,8,256]{2,1,0:T(8,128)} %get-tuple-element.41), channel_id=1, source_target_pairs={{8,0},{16,8},{24,16},{32,24},{40,32},{48,40},{56,48},{64,56},{72,6... | collective-permute-start | bytes 1105928 | tf_op jit(solution)/shard_map/ppermute | solution.py:324
  47.1 0.0 collective-permute-done.2.halo.before
  47.1 0.0 all-to-all-done
  47.1 0.0 copy-done.6
  47.1 0.0 copy-done.7
  47.1 0.0 copy-start.8
  47.2 1.8 %modes.1 = f32[256,128]{1,0:T(8,128)} custom-call(f32[256,128]{1,0:T(8,128)S(1)} %bitcast.6, f32[8,8,512]{2,1,0:T(8,128)S(1)} %bitcast.7, bf16[1024,512]{1,0:T(8,128)(2,1)S(1)} %copy-done.6), custom_call_target="tpu_custom_call" | custom-call | tf_op jit(solution)/shard_map/modes/pallas_call | solution.py:329
  49.0 0.0 copy-start.1
  49.0 7.8 %all-to-all-start.1 = ((f32[64,4,128]{2,1,0:T(4,128)}), f32[64,4,128]{2,1,0:T(4,128)S(1)}, u32[]{:S(2)}, u32[]{:S(2)}) async-start(f32[64,4,128]{2,1,0:T(4,128)} %bitcast.3), calls=%async_computation.1 | async-start | bytes 262144 | tf_op jit(solution)/shard_map/all_to_all | solution.py:338
  56.8 7.3 %collective-permute-start.4 = (f32[14,8,4,256]{3,2,1,0:T(4,128)}, f32[14,8,4,256]{3,2,1,0:T(4,128)S(1)}, u32[]{:S(2)}, u32[]{:S(2)}) collective-permute-start(f32[14,8,4,256]{3,2,1,0:T(4,128)} %get-tuple-element.48), channel_id=1, source_target_pairs={{0,1},{1,2},{2,3},{3,4},{4,5},{5,6},{6,7},{8,9},{9,10},{10,11},{11... | collective-permute-start | bytes 1376264 | tf_op jit(solution)/shard_map/ppermute | solution.py:265
  64.1 0.0 copy-done.8
  64.1 1.9 %collective-permute-start.5 = (f32[14,8,4,256]{3,2,1,0:T(4,128)S(1)}, f32[14,8,4,256]{3,2,1,0:T(4,128)S(1)}, u32[]{:S(2)}, u32[]{:S(2)}) collective-permute-start(f32[14,8,4,256]{3,2,1,0:T(4,128)S(1)} %copy-done.8), channel_id=1, source_target_pairs={{1,0},{2,1},{3,2},{4,3},{5,4},{6,5},{7,6},{9,8},{10,9},{11,10},{12... | collective-permute-start | bytes 1376264 | tf_op jit(solution)/shard_map/ppermute | solution.py:265
  66.0 0.0 collective-permute-done.3.halo.after
  66.1 4.5 %all-to-all-done.1 = f32[64,4,128]{2,1,0:T(4,128)S(1)} async-done(((f32[64,4,128]{2,1,0:T(4,128)}), f32[64,4,128]{2,1,0:T(4,128)S(1)}, u32[]{:S(2)}, u32[]{:S(2)}) %all-to-all-start.1) | async-done | bytes 131104 | tf_op jit(solution)/shard_map/all_to_all | solution.py:338
  70.6 0.0 copy-start.3
  70.6 0.0 copy-start.5
  70.6 0.1 turn.1
  70.7 8.5 %collective-permute-start.6 = (f32[26,8,256]{2,1,0:T(8,128)S(1)}, f32[26,8,256]{2,1,0:T(8,128)S(1)}, u32[]{:S(2)}, u32[]{:S(2)}) collective-permute-start(f32[26,8,256]{2,1,0:T(8,128)S(1)} %get-tuple-element.50), channel_id=1, source_target_pairs={{0,1},{1,2},{2,3},{3,4},{4,5},{5,6},{6,7},{8,9},{9,10},{10,11},{11... | collective-permute-start | bytes 638984 | tf_op jit(solution)/shard_map/ppermute | solution.py:265
  79.2 1.9 %collective-permute-start.7 = (f32[26,8,256]{2,1,0:T(8,128)S(1)}, f32[26,8,256]{2,1,0:T(8,128)S(1)}, u32[]{:S(2)}, u32[]{:S(2)}) collective-permute-start(f32[26,8,256]{2,1,0:T(8,128)S(1)} %get-tuple-element.51), channel_id=1, source_target_pairs={{1,0},{2,1},{3,2},{4,3},{5,4},{6,5},{7,6},{9,8},{10,9},{11,10},{12... | collective-permute-start | bytes 638984 | tf_op jit(solution)/shard_map/ppermute | solution.py:265
  81.2 0.0 collective-permute-done.4.rad_low
  81.2 0.0 collective-permute-done.5.rad_high
  81.2 0.8 collective-permute-done.6.cor_low
  82.0 4.4 %collective-permute-done.7.cor_high = f32[26,8,256]{2,1,0:T(8,128)S(1)} collective-permute-done((f32[26,8,256]{2,1,0:T(8,128)S(1)}, f32[26,8,256]{2,1,0:T(8,128)S(1)}, u32[]{:S(2)}, u32[]{:S(2)}) %collective-permute-start.7) | collective-permute-done | bytes 213024 | tf_op jit(solution)/shard_map/ppermute | solution.py:265
  86.4 0.0 copy-done.1
  86.4 0.0 copy-done.3
  86.4 0.0 copy-done.5
  86.4 2.9 %sweeps.1 = (f32[3,8,8,256]{3,2,1,0:T(8,128)}, f32[8,8,256]{2,1,0:T(8,128)}) custom-call(f32[3,8,8,256]{3,2,1,0:T(8,128)S(1)} %copy-done.3, f32[3,8,8,256]{3,2,1,0:T(8,128)S(1)} %copy-done.5, f32[3,3,8,8,256]{4,3,2,1,0:T(8,128)S(1)} %copy-done.1, f32[128,256]{1,0:T(8,128)S(1)} %get-tuple-element.45.press, ...), custom_call_target="tpu_custom_call" | custom-call | tf_op jit(solution)/shard_map/sweeps/pallas_call | solution.py:353
  (4 shorter events, 0.1 us)
Async XLA Ops:
  0.6 0.9 %copy-start.2 = (f32[3,8,8,256]{3,2,1,0:T(8,128)S(1)}, f32[3,8,8,256]{3,2,1,0:T(8,128)}, u32[]{:S(2)}) copy-start(f32[3,8,8,256]{3,2,1,0:T(8,128)} %vel.6) | copy-start | bytes 589828
  1.6 10.2 %copy-start.4 = (f32[3,8,8,256]{3,2,1,0:T(8,128)S(1)}, f32[3,8,8,256]{3,2,1,0:T(8,128)}, u32[]{:S(2)}) copy-start(f32[3,8,8,256]{3,2,1,0:T(8,128)} %rhs.4) | copy-start | bytes 589828
  1.6 11.3 %collective-permute-start = (f32[1,8,4,256]{3,2,1,0:T(4,128)S(1)}, f32[1,8,4,256]{3,2,1,0:T(4,128)S(1)}, u32[]{:S(2)}, u32[]{:S(2)}) collective-permute-start(f32[1,8,4,256]{3,2,1,0:T(4,128)S(1)} %get-tuple-element.27), channel_id=1, source_target_pairs={{0,1},{1,2},{2,3},{3,4},{4,5},{5,6},{6,7},{8,9},{9,10},{10,11},{11... | collective-permute-start | bytes 98312 | tf_op jit(solution)/shard_map/ppermute | solution.py:265
  7.1 5.8 %collective-permute-start.1 = (f32[1,8,4,256]{3,2,1,0:T(4,128)S(1)}, f32[1,8,4,256]{3,2,1,0:T(4,128)S(1)}, u32[]{:S(2)}, u32[]{:S(2)}) collective-permute-start(f32[1,8,4,256]{3,2,1,0:T(4,128)S(1)} %get-tuple-element.28), channel_id=1, source_target_pairs={{1,0},{2,1},{3,2},{4,3},{5,4},{6,5},{7,6},{9,8},{10,9},{11,10},{12... | collective-permute-start | bytes 98312 | tf_op jit(solution)/shard_map/ppermute | solution.py:265
  11.8 1.1 %copy-start = (f32[3,3,8,8,256]{4,3,2,1,0:T(8,128)S(1)}, f32[3,3,8,8,256]{4,3,2,1,0:T(8,128)}, u32[]{:S(2)}) copy-start(f32[3,3,8,8,256]{4,3,2,1,0:T(8,128)} %inv.4) | copy-start | bytes 1769476
  12.9 34.2 %copy-start.6 = (bf16[1024,512]{1,0:T(8,128)(2,1)S(1)}, bf16[1024,512]{1,0:T(8,128)(2,1)}, u32[]{:S(2)}) copy-start(bf16[1024,512]{1,0:T(8,128)(2,1)} %constant.2.clone.table) | copy-start | bytes 3145732
  12.9 34.1 %collective-permute-start.2 = (f32[45,8,256]{2,1,0:T(8,128)S(1)}, f32[45,8,256]{2,1,0:T(8,128)S(1)}, u32[]{:S(2)}, u32[]{:S(2)}) collective-permute-start(f32[45,8,256]{2,1,0:T(8,128)S(1)} %pack_forward.1), channel_id=1, source_target_pairs={{0,8},{8,16},{16,24},{24,32},{32,40},{40,48},{48,56},{56,64},{64,7... | collective-permute-start | bytes 1105928 | tf_op jit(solution)/shard_map/ppermute | solution.py:302
  22.9 24.2 %all-to-all-start = ((f32[64,4,128]{2,1,0:T(4,128)}), f32[64,4,128]{2,1,0:T(4,128)S(1)}, u32[]{:S(2)}, u32[]{:S(2)}) async-start(f32[64,4,128]{2,1,0:T(4,128)} %bitcast), calls=%async_computation | async-start | bytes 262144 | tf_op jit(solution)/shard_map/all_to_all | solution.py:315
  35.6 11.6 %copy-start.7 = (f32[512,8,8]{0,2,1:T(8,128)S(1)}, f32[512,8,8]{0,2,1:T(8,128)}, u32[]{:S(2)}) copy-start(f32[512,8,8]{0,2,1:T(8,128)} %param.7) | copy-start | bytes 393220
  35.6 30.5 %collective-permute-start.3 = (f32[45,8,256]{2,1,0:T(8,128)}, f32[45,8,256]{2,1,0:T(8,128)S(1)}, u32[]{:S(2)}, u32[]{:S(2)}) collective-permute-start(f32[45,8,256]{2,1,0:T(8,128)} %get-tuple-element.41), channel_id=1, source_target_pairs={{8,0},{16,8},{24,16},{32,24},{40,32},{48,40},{56,48},{64,56},{72,6... | collective-permute-start | bytes 1105928 | tf_op jit(solution)/shard_map/ppermute | solution.py:324
  47.1 16.9 %copy-start.8 = (f32[14,8,4,256]{3,2,1,0:T(4,128)S(1)}, f32[14,8,4,256]{3,2,1,0:T(4,128)}, u32[]{:S(2)}) copy-start(f32[14,8,4,256]{3,2,1,0:T(4,128)} %get-tuple-element.49) | copy-start | bytes 1376260
  49.0 37.4 %copy-start.1 = (f32[3,3,8,8,256]{4,3,2,1,0:T(8,128)S(1)}, f32[3,3,8,8,256]{4,3,2,1,0:T(8,128)}, u32[]{:S(2)}) copy-start(f32[3,3,8,8,256]{4,3,2,1,0:T(8,128)} %inv.4) | copy-start | bytes 1769476
  49.0 21.6 %all-to-all-start.1 = ((f32[64,4,128]{2,1,0:T(4,128)}), f32[64,4,128]{2,1,0:T(4,128)S(1)}, u32[]{:S(2)}, u32[]{:S(2)}) async-start(f32[64,4,128]{2,1,0:T(4,128)} %bitcast.3), calls=%async_computation.1 | async-start | bytes 262144 | tf_op jit(solution)/shard_map/all_to_all | solution.py:338
  56.8 24.4 %collective-permute-start.4 = (f32[14,8,4,256]{3,2,1,0:T(4,128)}, f32[14,8,4,256]{3,2,1,0:T(4,128)S(1)}, u32[]{:S(2)}, u32[]{:S(2)}) collective-permute-start(f32[14,8,4,256]{3,2,1,0:T(4,128)} %get-tuple-element.48), channel_id=1, source_target_pairs={{0,1},{1,2},{2,3},{3,4},{4,5},{5,6},{6,7},{8,9},{9,10},{10,11},{11... | collective-permute-start | bytes 1376264 | tf_op jit(solution)/shard_map/ppermute | solution.py:265
  64.1 17.1 %collective-permute-start.5 = (f32[14,8,4,256]{3,2,1,0:T(4,128)S(1)}, f32[14,8,4,256]{3,2,1,0:T(4,128)S(1)}, u32[]{:S(2)}, u32[]{:S(2)}) collective-permute-start(f32[14,8,4,256]{3,2,1,0:T(4,128)S(1)} %copy-done.8), channel_id=1, source_target_pairs={{1,0},{2,1},{3,2},{4,3},{5,4},{6,5},{7,6},{9,8},{10,9},{11,10},{12... | collective-permute-start | bytes 1376264 | tf_op jit(solution)/shard_map/ppermute | solution.py:265
  70.6 15.8 %copy-start.3 = (f32[3,8,8,256]{3,2,1,0:T(8,128)S(1)}, f32[3,8,8,256]{3,2,1,0:T(8,128)}, u32[]{:S(2)}) copy-start(f32[3,8,8,256]{3,2,1,0:T(8,128)} %vel.6) | copy-start | bytes 589828
  70.6 15.8 %copy-start.5 = (f32[3,8,8,256]{3,2,1,0:T(8,128)S(1)}, f32[3,8,8,256]{3,2,1,0:T(8,128)}, u32[]{:S(2)}) copy-start(f32[3,8,8,256]{3,2,1,0:T(8,128)} %rhs.4) | copy-start | bytes 589828
  70.7 11.3 %collective-permute-start.6 = (f32[26,8,256]{2,1,0:T(8,128)S(1)}, f32[26,8,256]{2,1,0:T(8,128)S(1)}, u32[]{:S(2)}, u32[]{:S(2)}) collective-permute-start(f32[26,8,256]{2,1,0:T(8,128)S(1)} %get-tuple-element.50), channel_id=1, source_target_pairs={{0,1},{1,2},{2,3},{3,4},{4,5},{5,6},{6,7},{8,9},{9,10},{10,11},{11... | collective-permute-start | bytes 638984 | tf_op jit(solution)/shard_map/ppermute | solution.py:265
  79.2 7.2 %collective-permute-start.7 = (f32[26,8,256]{2,1,0:T(8,128)S(1)}, f32[26,8,256]{2,1,0:T(8,128)S(1)}, u32[]{:S(2)}, u32[]{:S(2)}) collective-permute-start(f32[26,8,256]{2,1,0:T(8,128)S(1)} %get-tuple-element.51), channel_id=1, source_target_pairs={{1,0},{2,1},{3,2},{4,3},{5,4},{6,5},{7,6},{9,8},{10,9},{11,10},{12... | collective-permute-start | bytes 638984 | tf_op jit(solution)/shard_map/ppermute | solution.py:265
